TPU v7x, 128 devices: a whole 4x4x4 slice. The times are simulated.
128 devices in a mesh: fsdp: 64 (over z_lo, x, y, core), ctx: 2 (over z_hi).
Axes of the slice: x: 4, y: 4, z: 4 (z_hi: 2, z_lo: 2; z = z_hi * 2 + z_lo), core: 2. Of those that a mesh axis runs over, the one named last changes fastest.
Arguments:
- tokens: bfloat16 [64, 256, 1024], P('fsdp', 'ctx'), may hold values from -16 to 16
- labels: int32 [64], P('fsdp'), may hold values from 0 to 999
- timesteps: int32 [64], P('fsdp'), may hold values from 0 to 999
- cotangent: bfloat16 [64, 256, 1024], P('fsdp', 'ctx'), may hold values from -6 to 6
- class_table: bfloat16 [1000, 1024], P(None, 'fsdp'), may hold values from -6 to 6
- time_weight: bfloat16 [256, 1024], P(None, 'fsdp'), may hold values from -0.375 to 0.375
- modulate_weight: bfloat16 [1, 1024, 6144], P(None, 'fsdp'), may hold values from -0.1875 to 0.1875
- modulate_offset: bfloat16 [1, 6144], P(None, 'fsdp'), may hold values from -3 to 3
- attend_weight: bfloat16 [1, 1024, 3072], P(None, 'fsdp'), may hold values from -0.1875 to 0.1875
- output_weight: bfloat16 [1, 1024, 1024], P(None, 'fsdp'), may hold values from -3 to 3
- expand_weight: bfloat16 [1, 1024, 4096], P(None, 'fsdp'), may hold values from -0.1875 to 0.1875
- hidden_offset: bfloat16 [1, 4096], P(None, 'fsdp'), may hold values from -3 to 3
- contract_weight: bfloat16 [1, 4096, 1024], P(None, 'fsdp'), may hold values from -0.09375 to 0.09375
Outputs:
- result: bfloat16 [64, 256, 1024], P('fsdp', 'ctx')
- tokens_grad: float32 [64, 256, 1024], P('fsdp', 'ctx')
- table_grad: float32 [1000, 1024], P(None, 'fsdp')
- time_grad: float32 [256, 1024], P(None, 'fsdp')
- modulate_grad: float32 [1, 1024, 6144], P(None, 'fsdp')
- offset_grad: float32 [1, 6144], P(None, 'fsdp')
- attend_grad: float32 [1, 1024, 3072], P(None, 'fsdp')
- output_grad: float32 [1, 1024, 1024], P(None, 'fsdp')
- expand_grad: float32 [1, 1024, 4096], P(None, 'fsdp')
- hidden_grad: float32 [1, 4096], P(None, 'fsdp')
- contract_grad: float32 [1, 4096, 1024], P(None, 'fsdp')
All inputs are finite; a program needn't handle non-finite values.
Results may differ from a plain program's by a relative error of at most 0.025.
Values may be sent and summed in bfloat16 or wider, within the bound.
A program may use at most 192 MiB of HBM per device.

v0:
```python
import math

import jax
import jax.numpy as jnp
from jax import lax
from jax.sharding import PartitionSpec as P

D = 1024
HEADS = 16
HEAD = 64
CLASSES = 1000
FREQ = 256
LAYERS = 1


HIGHEST = lax.Precision.HIGHEST
EPSILON = 1e-06


def normalize(values):
    centre = values - jnp.mean(values, -1, keepdims=True)
    spread = jnp.mean(centre * centre, -1, keepdims=True)
    return centre * lax.rsqrt(spread + EPSILON)


def modulated(values, shift_vec, scale_vec):
    return normalize(values) * (1.0 + scale_vec) + shift_vec


def gelu_tanh(values):
    return jax.nn.gelu(values, approximate=True)


def sinusoid(step_ids):
    half_width = FREQ // 2
    freq_rates = jnp.exp(
        -math.log(10000.0) * jnp.arange(half_width, dtype=jnp.float32) / half_width
    )
    angles = step_ids.astype(jnp.float32)[:, None] * freq_rates[None, :]
    return jnp.concatenate([jnp.cos(angles), jnp.sin(angles)], axis=-1)


def head_split(rows_in):
    return rows_in.reshape(rows_in.shape[0], HEADS, HEAD)


def attend_scores(query_rows, key_rows):
    return jnp.einsum(
        "qhd,khd->hqk",
        head_split(query_rows),
        head_split(key_rows),
        preferred_element_type=jnp.float32,
    ) * HEAD ** (-0.5)


def per_device(
    tokens,
    labels,
    timesteps,
    cotangent,
    class_table,
    time_weight,
    modulate_weight,
    modulate_offset,
    attend_weight,
    output_weight,
    expand_weight,
    hidden_offset,
    contract_weight,
):
    all_labels, all_steps = (
        lax.all_gather(labels, "fsdp", axis=0, tiled=True),
        lax.all_gather(timesteps, "fsdp", axis=0, tiled=True),
    )
    onehot = all_labels[:, None] == jnp.arange(CLASSES, dtype=jnp.int32)[None, :]
    sinus_rows = sinusoid(all_steps).astype(jnp.bfloat16)
    cond_cols = jnp.dot(
        onehot.astype(jnp.bfloat16), class_table, preferred_element_type=jnp.float32
    ) + jnp.dot(sinus_rows, time_weight, preferred_element_type=jnp.float32)
    shard_index = lax.axis_index("fsdp")
    offset_width = modulate_offset.shape[1]
    act_cols = jax.nn.silu(cond_cols).astype(jnp.bfloat16)
    partial_mod = jnp.einsum(
        "bd,ldk->blk", act_cols, modulate_weight, preferred_element_type=jnp.float32
    )
    placed = lax.dynamic_update_slice(
        jnp.zeros((LAYERS, 6 * D), jnp.float32),
        modulate_offset.astype(jnp.float32),
        (jnp.int32(0), shard_index * offset_width),
    )
    modulation = lax.psum_scatter(
        partial_mod + placed[None], "fsdp", scatter_dimension=0, tiled=True
    )
    hidden = tokens[0].astype(jnp.float32)
    which_layer = 0
    pieces = [modulation[0, which_layer, portion * D : (portion + 1) * D] for portion in range(6)]
    shift_one, scale_one, gate_one, shift_two, scale_two, gate_two = pieces
    layer_weights = (
        lax.all_gather(attend_weight[which_layer], "fsdp", axis=0, tiled=True),
        lax.all_gather(output_weight[which_layer], "fsdp", axis=0, tiled=True),
        lax.all_gather(expand_weight[which_layer], "fsdp", axis=0, tiled=True),
        lax.all_gather(hidden_offset[which_layer], "fsdp", axis=0, tiled=True),
        lax.all_gather(contract_weight[which_layer], "fsdp", axis=0, tiled=True),
    )
    w_attend, w_output, w_expand, b_hidden, w_contract = layer_weights
    first_in = modulated(hidden, shift_one, scale_one).astype(jnp.bfloat16)
    projected = jnp.dot(first_in, w_attend, preferred_element_type=jnp.float32).astype(jnp.bfloat16)
    query_rows = projected[:, :D]
    key_rows = lax.all_gather(projected[:, D : 2 * D], "ctx", axis=0, tiled=True)
    value_rows = lax.all_gather(projected[:, 2 * D :], "ctx", axis=0, tiled=True)
    scores = attend_scores(query_rows, key_rows)
    top_score = jnp.max(scores, -1, keepdims=True)
    exp_terms = jnp.exp(scores - top_score)
    totals = jnp.sum(exp_terms, -1, keepdims=True)
    softmaxed = exp_terms / totals
    logsum = (top_score + jnp.log(totals))[..., 0]
    attended = (
        jnp.einsum(
            "hqk,khd->qhd",
            softmaxed.astype(jnp.bfloat16),
            head_split(value_rows),
            preferred_element_type=jnp.float32,
        )
        .reshape(-1, D)
        .astype(jnp.bfloat16)
    )
    branch_one = jnp.dot(attended, w_output, preferred_element_type=jnp.float32)
    middle = hidden + gate_one * branch_one
    second_in = modulated(middle, shift_two, scale_two).astype(jnp.bfloat16)
    pre_act = jnp.dot(second_in, w_expand, preferred_element_type=jnp.float32) + b_hidden.astype(
        jnp.float32
    )
    activated = gelu_tanh(pre_act).astype(jnp.bfloat16)
    branch_two = jnp.dot(activated, w_contract, preferred_element_type=jnp.float32)
    kept_state = [
        (
            hidden,
            first_in,
            query_rows,
            key_rows,
            value_rows,
            logsum,
            attended,
            branch_one,
            middle,
            second_in,
            pre_act,
            activated,
            branch_two,
            layer_weights,
        )
    ]
    hidden = middle + gate_two * branch_two
    result = hidden.astype(jnp.bfloat16)[None]
    grad_hidden = cotangent[0].astype(jnp.float32)
    layer_terms = []
    mod_grads = []
    for which_layer in reversed(range(LAYERS)):
        (
            layer_in,
            first_in,
            query_rows,
            key_rows,
            value_rows,
            logsum,
            attended,
            branch_one,
            middle,
            second_in,
            pre_act,
            activated,
            branch_two,
            layer_weights,
        ) = kept_state[which_layer]
        w_attend, w_output, w_expand, b_hidden, w_contract = layer_weights
        pieces = [
            modulation[0, which_layer, portion * D : (portion + 1) * D] for portion in range(6)
        ]
        shift_one, scale_one, gate_one, shift_two, scale_two, gate_two = pieces
        grad_two = (grad_hidden * gate_two).astype(jnp.bfloat16)
        gate_two_grad = jnp.sum(grad_hidden * branch_two, 0)
        contract_term = jnp.einsum(
            "tf,td->fd", activated, grad_two, preferred_element_type=jnp.float32
        )
        grad_act = jnp.einsum("td,fd->tf", grad_two, w_contract, preferred_element_type=jnp.float32)
        gelu_value, gelu_pull = jax.vjp(gelu_tanh, pre_act)
        grad_pre = gelu_pull(grad_act)[0].astype(jnp.bfloat16)
        expand_term = jnp.einsum(
            "td,tf->df", second_in, grad_pre, preferred_element_type=jnp.float32
        )
        hidden_term = jnp.sum(grad_pre.astype(jnp.float32), 0)
        grad_second = jnp.einsum(
            "tf,df->td", grad_pre, w_expand, preferred_element_type=jnp.float32
        )
        norm_value, second_pull = jax.vjp(modulated, middle, shift_two, scale_two)
        grad_middle, shift_two_grad, scale_two_grad = second_pull(grad_second)
        grad_middle = grad_hidden + grad_middle
        grad_one = (grad_middle * gate_one).astype(jnp.bfloat16)
        gate_one_grad = jnp.sum(grad_middle * branch_one, 0)
        output_term = jnp.einsum(
            "td,te->de", attended, grad_one, preferred_element_type=jnp.float32
        )
        grad_att = jnp.einsum(
            "te,de->td", grad_one, w_output, preferred_element_type=jnp.float32
        ).astype(jnp.bfloat16)
        scores = attend_scores(query_rows, key_rows)
        softmaxed = jnp.exp(scores - logsum[..., None])
        grad_heads = head_split(grad_att)
        grad_probs = jnp.einsum(
            "qhd,khd->hqk", grad_heads, head_split(value_rows), preferred_element_type=jnp.float32
        )
        grad_scores = (
            softmaxed * (grad_probs - jnp.sum(softmaxed * grad_probs, -1, keepdims=True))
        ).astype(jnp.bfloat16)
        grad_query = jnp.einsum(
            "hqk,khd->qhd", grad_scores, head_split(key_rows), preferred_element_type=jnp.float32
        ) * HEAD ** (-0.5)
        grad_key = jnp.einsum(
            "hqk,qhd->khd", grad_scores, head_split(query_rows), preferred_element_type=jnp.float32
        ) * HEAD ** (-0.5)
        grad_value = jnp.einsum(
            "hqk,qhd->khd",
            softmaxed.astype(jnp.bfloat16),
            grad_heads,
            preferred_element_type=jnp.float32,
        )
        grad_key, grad_value = (
            lax.psum_scatter(
                grad_key.reshape(-1, D).astype(jnp.bfloat16), "ctx", scatter_dimension=0, tiled=True
            ).astype(jnp.float32),
            lax.psum_scatter(
                grad_value.reshape(-1, D).astype(jnp.bfloat16),
                "ctx",
                scatter_dimension=0,
                tiled=True,
            ).astype(jnp.float32),
        )
        grad_proj = jnp.concatenate(
            [
                grad_query.reshape(-1, D).astype(jnp.bfloat16),
                grad_key.astype(jnp.bfloat16),
                grad_value.astype(jnp.bfloat16),
            ],
            1,
        )
        attend_term = jnp.einsum(
            "td,te->de", first_in, grad_proj, preferred_element_type=jnp.float32
        )
        grad_first = jnp.einsum(
            "te,de->td", grad_proj, w_attend, preferred_element_type=jnp.float32
        )
        first_value, first_pull = jax.vjp(modulated, layer_in, shift_one, scale_one)
        grad_input, shift_one_grad, scale_one_grad = first_pull(grad_first)
        grad_hidden = grad_middle + grad_input
        grad_terms = (
            lax.psum_scatter(attend_term, "fsdp", scatter_dimension=0, tiled=True),
            lax.psum_scatter(output_term, "fsdp", scatter_dimension=0, tiled=True),
            lax.psum_scatter(expand_term, "fsdp", scatter_dimension=0, tiled=True),
            lax.psum_scatter(hidden_term, "fsdp", scatter_dimension=0, tiled=True),
            lax.psum_scatter(contract_term, "fsdp", scatter_dimension=0, tiled=True),
        )
        layer_terms.insert(0, grad_terms)
        mod_grads.insert(
            0,
            jnp.concatenate(
                [
                    shift_one_grad,
                    scale_one_grad,
                    gate_one_grad,
                    shift_two_grad,
                    scale_two_grad,
                    gate_two_grad,
                ]
            ),
        )
    tokens_grad = grad_hidden[None]
    stacked = [jnp.stack([grad_terms[member] for grad_terms in layer_terms]) for member in range(5)]
    mod_partial = jnp.stack(mod_grads)[None]
    attend_grad, output_grad, expand_grad, hidden_grad, contract_grad, mod_total = (
        lax.psum(stacked[0].astype(jnp.bfloat16), "ctx").astype(jnp.float32),
        lax.psum(stacked[1].astype(jnp.bfloat16), "ctx").astype(jnp.float32),
        lax.psum(stacked[2].astype(jnp.bfloat16), "ctx").astype(jnp.float32),
        lax.psum(stacked[3].astype(jnp.bfloat16), "ctx").astype(jnp.float32),
        lax.psum(stacked[4].astype(jnp.bfloat16), "ctx").astype(jnp.float32),
        lax.psum(mod_partial.astype(jnp.bfloat16), "ctx").astype(jnp.float32),
    )
    mod_rounded = mod_total.astype(jnp.bfloat16)
    all_mod = lax.all_gather(mod_rounded, "fsdp", axis=0, tiled=True)
    grad_act_cols = jnp.einsum(
        "blk,ldk->bd", all_mod, modulate_weight, preferred_element_type=jnp.float32
    )
    modulate_grad = jnp.einsum("bd,blk->ldk", act_cols, all_mod, preferred_element_type=jnp.float32)
    own_cols = lax.dynamic_slice_in_dim(all_mod, shard_index * offset_width, offset_width, 2)
    offset_grad = jnp.sum(own_cols.astype(jnp.float32), 0)
    silu_value, silu_pull = jax.vjp(jax.nn.silu, cond_cols)
    grad_cond = silu_pull(grad_act_cols)[0]
    table_grad = jnp.einsum("bc,bd->cd", onehot.astype(jnp.float32), grad_cond, precision=HIGHEST)
    time_grad = jnp.einsum(
        "bf,bd->fd", sinus_rows.astype(jnp.float32), grad_cond, precision=HIGHEST
    )
    return (
        result,
        tokens_grad,
        table_grad,
        time_grad,
        modulate_grad,
        offset_grad,
        attend_grad,
        output_grad,
        expand_grad,
        hidden_grad,
        contract_grad,
    )


def solution(mesh):
    in_specs = (
        P("fsdp", "ctx", None),
        P("fsdp"),
        P("fsdp"),
        P("fsdp", "ctx", None),
        P(None, "fsdp"),
        P(None, "fsdp"),
        P(None, "fsdp", None),
        P(None, "fsdp"),
        P(None, "fsdp", None),
        P(None, "fsdp", None),
        P(None, "fsdp", None),
        P(None, "fsdp"),
        P(None, "fsdp", None),
    )
    out_specs = (
        P("fsdp", "ctx", None),
        P("fsdp", "ctx", None),
        P(None, "fsdp"),
        P(None, "fsdp"),
        P(None, "fsdp", None),
        P(None, "fsdp"),
        P(None, "fsdp", None),
        P(None, "fsdp", None),
        P(None, "fsdp", None),
        P(None, "fsdp"),
        P(None, "fsdp", None),
    )
    return jax.shard_map(
        per_device, mesh=mesh, in_specs=in_specs, out_specs=out_specs, check_vma=False
    )
```

profile of v0, /device:TPU:1, one launch (start us, length us, event | category | flops | bytes accessed | tf_op | source)
XLA Modules:
  0.0 2347.0 jit_solution(4552782908197414354)
XLA Ops:
  8.7 1.3 fusion.100
  10.0 0.8 dynamic-update-slice
  10.8 0.8 dynamic-update-slice.1
  11.5 17.4 all-reduce.5
  28.9 1.0 fusion.65
  30.1 0.8 convert_dynamic-update-slice_fusion
  30.9 0.8 convolution_add_fusion.1
  31.7 1.6 fusion.8
  33.4 0.7 all-gather.10.cloned.1.call-update
  37.0 144.5 %all-reduce.2 = bf16[4096]{0:T(1024)(128)(2,1)S(1)} all-reduce(bf16[4096]{0:T(1024)(128)(2,1)S(1)} %dynamic-update-slice.2), channel_id=5, replica_groups=mesh['fsdp'=64,'ctx'=2] {'fsdp'}, use_global_device_ids=true, to_apply=%add.2 | all-reduce | flops 4096 | bytes 16384
  181.9 402.5 %all-reduce.11.cloned.1.call-done = f32[64,1,6144]{2,0,1:T(8,128)} async-done(((f32[64,1,6144]{2,0,1:T(8,128)}), f32[64,1,6144]{2,0,1:T(8,128)}) %all-reduce.11.cloned.1.call-update) | async-done | bytes 1572880
  584.4 1.6 constant_dynamic-slice_fusion
  586.0 110.1 %all-gather.10.cloned.1.call-done = bf16[1,1024,3072]{2,1,0:T(8,128)(2,1)} async-done(((bf16[1,16,3072]{2,1,0:T(8,128)(2,1)}), bf16[1,1024,3072]{2,1,0:T(8,128)(2,1)}) %all-gather.10.cloned.1.call-update) | async-done | bytes 6291472 | tf_op jit(solution)/shard_map/all_gather | solution.py:99
  696.2 3.9 fusion.16
  700.1 9.8 all_gather.34
  710.4 9.5 all_gather.33
  719.8 1.0 copy.36
  721.4 0.7 fusion.32
  722.2 1.1 convolution_convert_fusion.1
  723.3 77.1 %all-gather.12.cloned.1.call-done = bf16[1,1024,1024]{2,1,0:T(8,128)(2,1)} async-done(((bf16[1,16,1024]{2,1,0:T(8,128)(2,1)}), bf16[1,1024,1024]{2,1,0:T(8,128)(2,1)}) %all-gather.12.cloned.1.call-update) | async-done | bytes 2097168 | tf_op jit(solution)/shard_map/all_gather | solution.py:100
  800.4 2.9 fusion.97
  803.5 108.7 %all-gather.14.cloned.1.call-done = bf16[1,1024,4096]{2,1,0:T(8,128)(2,1)} async-done(((bf16[1,16,4096]{2,1,0:T(8,128)(2,1)}), bf16[1,1024,4096]{2,1,0:T(8,128)(2,1)}) %all-gather.14.cloned.1.call-update) | async-done | bytes 8388624 | tf_op jit(solution)/shard_map/all_gather | solution.py:101
  912.2 6.2 fusion.13
  918.3 105.9 %all-gather.16.cloned.1.call-done = bf16[1,4096,1024]{2,1,0:T(8,128)(2,1)} async-done(((bf16[1,64,1024]{2,1,0:T(8,128)(2,1)}), bf16[1,4096,1024]{2,1,0:T(8,128)(2,1)}) %all-gather.16.cloned.1.call-update) | async-done | bytes 8388624 | tf_op jit(solution)/shard_map/all_gather | solution.py:103
  1024.2 7.8 convert_reduce_fusion
  1032.0 3.0 multiply_reduce_fusion.2
  1035.3 0.8 copy-done.7
  1036.1 1.5 fusion.36
  1037.7 1.8 copy.39
  1039.5 2.4 convolution_convert_fusion
  1041.8 2.1 copy.44
  1044.2 2.0 multiply_reduce_fusion
  1046.3 0.8 multiply_convert_fusion
  1047.0 1.0 copy-done.4
  1048.3 1.0 copy.42
  1049.4 2.9 fusion.73
  1052.4 1.1 copy-done.5
  1054.2 7.6 reduce-scatter.22.cloned.1.call-done
  1061.8 1.1 copy.45
  1062.9 19.7 reduce-scatter.20.cloned.1.call-done
  1082.6 1.1 copy.43
  1083.8 6.4 fusion.60
  1090.3 1.5 copy-done.3
  1091.8 8.1 fusion.66
  1100.0 9.4 fusion.95
  1110.1 273.8 %all-reduce.4 = bf16[4096]{0:T(1024)(128)(2,1)S(1)} all-reduce(f32[4096]{0:T(1024)S(1)} %get-tuple-element.54), channel_id=13, replica_groups=mesh['fsdp'=64,'ctx'=2] {'fsdp'}, use_global_device_ids=true, to_apply=%region_29.30.clone | all-reduce | flops 4096 | bytes 24576
  1384.0 5.5 fusion.57
  1389.9 6.2 fusion.59
  1396.2 0.8 convert_bitcast_fusion.4
  1397.0 8.7 all-reduce.6
  1406.8 90.8 %all_gather.39 = bf16[64,1,6144]{2,1,0:T(2,128)(2,1)S(1)} all-gather(bf16[1,1,6144]{2,1,0:T(2,128)(2,1)S(1)} %get-tuple-element.21), channel_id=1, replica_groups=mesh['fsdp'=64,'ctx'=2] {'fsdp'}, dimensions={0}, use_global_device_ids=true | all-gather | bytes 798720 | tf_op jit(solution)/shard_map/all_gather | solution.py:288
  1498.8 0.8 fusion.76
  1499.6 176.2 %reduce-scatter.12.cloned.1.call-done = f32[16,3072]{1,0:T(8,128)} async-done(((f32[1024,3072]{1,0:T(8,128)}), f32[16,3072]{1,0:T(8,128)}) %reduce-scatter.12.cloned.1.call-update) | async-done | bytes 196624 | tf_op jit(solution)/shard_map/reduce_scatter | solution.py:256
  1675.8 1.6 convert_bitcast_fusion.3
  1677.4 307.8 %reduce-scatter.18.cloned.1.call-done = f32[64,1024]{1,0:T(8,128)} async-done(((f32[4096,1024]{1,0:T(8,128)}), f32[64,1024]{1,0:T(8,128)}) %reduce-scatter.18.cloned.1.call-update) | async-done | bytes 262160 | tf_op jit(solution)/shard_map/reduce_scatter | solution.py:260
  1985.2 1.6 convert_bitcast_fusion.1
  1986.8 308.1 %reduce-scatter.16.cloned.1.call-done = f32[16,4096]{1,0:T(8,128)} async-done(((f32[1024,4096]{1,0:T(8,128)}), f32[16,4096]{1,0:T(8,128)}) %reduce-scatter.16.cloned.1.call-update) | async-done | bytes 262160 | tf_op jit(solution)/shard_map/reduce_scatter | solution.py:258
  2294.9 1.6 convert_bitcast_fusion.2
  2296.6 1.3 convolution_bitcast_fusion
  2297.8 0.9 fusion.64
  2298.7 36.5 %all-reduce.13.cloned.1.call-done = (bf16[1,16,3072]{2,1,0:T(8,128)(2,1)}, bf16[1,16,4096]{2,1,0:T(8,128)(2,1)}, bf16[1,64,1024]{2,1,0:T(8,128)(2,1)}) async-done(((bf16[1,16,3072]{2,1,0:T(8,128)(2,1)}, bf16[1,16,4096]{2,1,0:T(8,128)(2,1)}, bf16[1,64,1024]{2,1,0:T(8,128)(2,1)}), (bf16[1,16,3072]{2,1,0:T(8,128)(2,1)}, bf16[1,16,4096]{2,1,0:T(8,128)(2,1)}, ...) | async-done | bytes 360464 | tf_op jit(solution)/shard_map/psum | solution.py:280
  2335.3 1.6 convert_element_type.198
  2336.9 1.6 convert_element_type.204
  2338.5 1.6 convert_element_type.211
  (108 shorter events, 8.8 us)
Async XLA Ops:
  7.2 24.6 %copy-start = (bf16[1,16,6144]{2,1,0:T(8,128)(2,1)S(1)}, bf16[1,16,6144]{2,1,0:T(8,128)(2,1)}, u32[]{:S(2)}) copy-start(bf16[1,16,6144]{2,1,0:T(8,128)(2,1)} %param.19) | copy-start | bytes 589828
  7.2 29.5 %copy-start.23 = (bf16[1,64]{1,0:T(2,128)(2,1)S(1)}, bf16[1,64]{1,0:T(2,128)(2,1)}, u32[]{:S(2)}) copy-start(bf16[1,64]{1,0:T(2,128)(2,1)} %param.24) | copy-start | bytes 388
  7.2 174.3 %copy-start.2 = (bf16[1,128,1024]{2,1,0:T(8,128)(2,1)S(1)}, bf16[1,128,1024]{2,1,0:T(8,128)(2,1)}, u32[]{:S(2)}) copy-start(bf16[1,128,1024]{2,1,0:T(8,128)(2,1)} %param.13) | copy-start | bytes 786436
  7.2 577.2 %all-reduce.11.cloned.1.call-start = ((), (), s32[]{:S(2)}) async-start(), calls=%async_computation.16 | async-start | bytes 3145728
  33.4 662.8 %all-gather.10.cloned.1.call-start = ((), (), s32[]{:S(2)}) async-start(), calls=%async_computation.10 | async-start | bytes 6389760 | tf_op jit(solution)/shard_map/all_gather | solution.py:99
  34.1 766.2 %all-gather.12.cloned.1.call-start = ((), (), s32[]{:S(2)}) async-start(), calls=%async_computation.11 | async-start | bytes 2129920 | tf_op jit(solution)/shard_map/all_gather | solution.py:100
  34.8 877.3 %all-gather.14.cloned.1.call-start = ((), (), s32[]{:S(2)}) async-start(), calls=%async_computation.12 | async-start | bytes 8519680 | tf_op jit(solution)/shard_map/all_gather | solution.py:101
  35.4 988.8 %all-gather.16.cloned.1.call-start = ((), (), s32[]{:S(2)}) async-start(), calls=%async_computation.13 | async-start | bytes 8519680 | tf_op jit(solution)/shard_map/all_gather | solution.py:103
  36.0 1025.7 %reduce-scatter.22.cloned.1.call-start = ((), (), s32[]{:S(2)}) async-start(), calls=%async_computation.15 | async-start | bytes 786432
  710.2 11.3 copy-start.10
  710.3 11.1 copy-start.14
  720.8 1.3 copy-start.16
  723.3 80.2 %copy-start.17 = (bf16[16,64,128]{2,1,0:T(8,128)(2,1)}, bf16[16,64,128]{2,1,0:T(8,128)(2,1)S(1)}, u32[]{:S(2)}) copy-start(bf16[16,64,128]{2,1,0:T(8,128)(2,1)S(1)} %convolution_convert_fusion.1) | copy-start | bytes 786436
  912.2 112.0 %copy-start.13 = (bf16[1,128,1024]{2,1,0:T(8,128)(2,1)S(1)}, bf16[1,128,1024]{2,1,0:T(8,128)(2,1)}, u32[]{:S(2)}) copy-start(bf16[1,128,1024]{2,1,0:T(8,128)(2,1)} %param.16) | copy-start | bytes 786436
  1024.2 7.8 copy-start.1
  1032.0 3.0 copy-start.12
  1032.0 4.1 copy-start.6
  1035.3 0.8 copy-start.7
  1043.9 38.7 %reduce-scatter.20.cloned.1.call-start = ((), (), s32[]{:S(2)}) async-start(), calls=%async_computation.14 | async-start | bytes 786432
  1046.3 1.8 copy-start.15
  1047.0 1.0 copy-start.4
  1048.0 1.4 copy-start.8
  1048.0 1.4 copy-start.18
  1049.4 346.8 %reduce-scatter.14.cloned.1.call-start = ((), (), s32[]{:S(2)}) async-start(), calls=%async_computation.7 | async-start | bytes 4259840 | tf_op jit(solution)/shard_map/reduce_scatter | solution.py:257
  1052.3 1.2 copy-start.5
  1052.3 1.4 copy-start.11
  1052.3 623.5 %reduce-scatter.12.cloned.1.call-start = ((), (), s32[]{:S(2)}) async-start(), calls=%async_computation.6 | async-start | bytes 12779520 | tf_op jit(solution)/shard_map/reduce_scatter | solution.py:256
  1054.2 36.1 %copy-start.19 = (bf16[16,64,128]{2,1,0:T(8,128)(2,1)}, bf16[16,64,128]{2,1,0:T(8,128)(2,1)S(1)}, u32[]{:S(2)}) copy-start(bf16[16,64,128]{2,1,0:T(8,128)(2,1)S(1)} %fusion.35) | copy-start | bytes 786436
  1062.9 27.3 %copy-start.20 = (bf16[128,1024]{0,1:T(8,128)(2,1)}, bf16[128,1024]{0,1:T(8,128)(2,1)S(1)}, u32[]{:S(2)}) copy-start(bf16[128,1024]{0,1:T(8,128)(2,1)S(1)} %copy.45) | copy-start | bytes 786436
  1083.8 6.5 copy-start.21
  1090.2 1.6 copy-start.3
  1090.3 895.0 %reduce-scatter.18.cloned.1.call-start = ((), (), s32[]{:S(2)}) async-start(), calls=%async_computation.9 | async-start | bytes 17039360 | tf_op jit(solution)/shard_map/reduce_scatter | solution.py:260
  1100.0 1195.0 %reduce-scatter.16.cloned.1.call-start = ((), (), s32[]{:S(2)}) async-start(), calls=%async_computation.8 | async-start | bytes 17039360 | tf_op jit(solution)/shard_map/reduce_scatter | solution.py:258
  1109.4 1225.8 %all-reduce.13.cloned.1.call-start = ((), (), s32[]{:S(2)}) async-start(), calls=%async_computation.17 | async-start | bytes 720896 | tf_op jit(solution)/shard_map/psum | solution.py:280
  1384.0 5.9 copy-start.9
  1384.0 5.9 copy-start.22
Sparse Core Ops, SparseCore 0:
  33.5 550.8 all-reduce.10
  586.2 109.8 all-gather.9
  698.0 102.3 all-gather.11
  802.0 110.0 all-gather.13
  913.9 110.3 all-gather.15
  1044.1 17.6 reduce-scatter.21
  1064.7 17.9 reduce-scatter.19
  1085.1 284.0 reduce-scatter.13
  1371.6 304.1 reduce-scatter.11
  1678.1 307.1 reduce-scatter.17
  1987.6 307.2 reduce-scatter.15
  2298.6 36.6 all-reduce.12
where the time goes:
time: 2350 us
  waiting for transfers between devices  1660 us (71%)
  blocking collectives  555 us (24%)
  matrix products  77.4 us (3%)
    unnamed x3, blocking collectives  436 us
    unnamed x15, waiting for transfers between devices  432 us
    reduce_scatter x1, waiting for transfers between devices, per_device(): lax.psum_scatter(expand_term, 'fsdp', scatter_dimension=0, tiled=True)  308 us
    reduce_scatter x1, waiting for transfers between devices, per_device(): lax.psum_scatter(contract_term, 'fsdp', scatter_dimension=0, tiled=True)  308 us
    reduce_scatter x1, waiting for transfers between devices, per_device(): lax.psum_scatter(attend_term, 'fsdp', scatter_dimension=0, tiled=True)  176 us
    all_gather x1, waiting for transfers between devices, per_device(): lax.all_gather(attend_weight[which_layer], 'fsdp', axis=0, tiled=True)  110 us
    all_gather x1, waiting for transfers between devices, per_device(): lax.all_gather(expand_weight[which_layer], 'fsdp', axis=0, tiled=True)  109 us
    all_gather x1, waiting for transfers between devices, per_device(): lax.all_gather(contract_weight[which_layer], 'fsdp', axis=0, tiled=True)  106 us
  transfers between devices with their start and end apart: 12, of which 11 were waited for; matrix products, arithmetic and copies ran while one was open for 3% of the time, Pallas kernels for 0%

commit v1 on v0

v1 whole, which is shorter than its diff:
```python
import functools
import math

import jax
import jax.numpy as jnp
from jax import lax
from jax.experimental import pallas as pl
from jax.experimental.pallas import tpu as pltpu
from jax.sharding import PartitionSpec as P

D = 1024
HEADS = 16
HEAD = 64
FF = 4096
CLASSES = 1000
FREQ = 256
SEQ = 256
HALF = SEQ // 2

ATTEND = (16, 3 * D, "zyx")
OUTPUT = (16, D, "zyx")
EXPAND = (16, FF, "xzy")
CONTRACT = (64, D, "yxz")
WEIGHTS = (ATTEND, OUTPUT, EXPAND, CONTRACT)

HIGHEST = lax.Precision.HIGHEST
EPSILON = 1e-06
MESH = pl.DeviceIdType.MESH
BF16 = jnp.bfloat16
F32 = jnp.float32


class Place:
    def __init__(self):
        shard = lax.axis_index("fsdp")
        self.z_hi = lax.axis_index("ctx")
        self.core = lax.rem(shard, 2)
        self.z_lo = lax.div(shard, 32)
        self.at = {
            "x": lax.rem(lax.div(shard, 8), 4),
            "y": lax.rem(lax.div(shard, 2), 4),
            "z": 2 * self.z_hi + self.z_lo,
        }

    def step(self, axis, distance):
        return lax.rem(self.at[axis] + distance + 4, 4)

    def device(self, core=None, **moved):
        at = {**self.at, **moved}
        core = self.core if core is None else core
        shard = ((lax.rem(at["z"], 2) * 4 + at["x"]) * 4 + at["y"]) * 2 + core
        return (shard, lax.div(at["z"], 2))

    def along(self, axis, distance):
        return self.device(**{axis: self.step(axis, distance)})

    def other_core(self):
        return self.device(core=1 - self.core)

    def other_z_lo(self):
        return self.device(z=2 * self.z_hi + 1 - self.z_lo)

    def everyone(self):
        ids = [self.other_core()]
        for axis in "xyz":
            ids += [self.along(axis, distance) for distance in (1, 2, 3)]
        return ids


def greet(ids):
    barrier = pltpu.get_barrier_semaphore()
    for device in ids:
        pl.semaphore_signal(barrier, inc=1, device_id=device, device_id_type=MESH)
    pl.semaphore_wait(barrier, len(ids))


class Copies:
    def __init__(self, send_sems, recv_sems, local_sems):
        self.send_sems, self.recv_sems, self.local_sems = send_sems, recv_sems, local_sems
        self.remote, self.local = [], []

    def send(self, source, target, device):
        slot = len(self.remote)
        copy = pltpu.make_async_remote_copy(
            src_ref=source,
            dst_ref=target,
            send_sem=self.send_sems.at[slot],
            recv_sem=self.recv_sems.at[slot],
            device_id=device,
            device_id_type=MESH,
        )
        copy.start()
        self.remote.append(copy)
        return copy

    def move(self, source, target):
        slot = len(self.local)
        copy = pltpu.make_async_copy(source, target, self.local_sems.at[slot])
        copy.start()
        self.local.append(copy)
        return copy

    def drain(self):
        for copy in self.remote:
            copy.wait_send()


def copy_scratch(remote, local):
    return [
        pltpu.SemaphoreType.DMA((remote,)),
        pltpu.SemaphoreType.DMA((remote,)),
        pltpu.SemaphoreType.DMA((max(local, 1),)),
    ]


class Gather:
    def __init__(self, place, copies, source, out, columns, order):
        self.place, self.copies, self.source, self.out = place, copies, source, out
        self.half, self.order = columns // 2, order
        self.done = []
        self.to_core = []

    def region(self, half_index, core, **sel):
        lead = [sel.get(axis) for axis in "xy"]
        lead = [slice(None) if index is None else index for index in lead]
        z = sel.get("z")
        start, width = half_index * self.half, self.half
        z_lo = slice(None)
        if z is not None:
            width = self.half // 2
            start = start + lax.div(z, 2) * width
            z_lo = lax.rem(z, 2)
        core = slice(None) if core is None else core
        return self.out.at[z_lo, lead[0], lead[1], core, :, pl.ds(pl.multiple_of(start, 128), width)]

    def begin(self):
        place = self.place
        quarter = self.half // 2
        mine = place.core * self.half + place.z_hi * quarter
        theirs = (1 - place.core) * self.half + place.z_hi * quarter
        mine, theirs = pl.multiple_of(mine, 128), pl.multiple_of(theirs, 128)
        self.first = self.copies.send(
            self.source.at[:, pl.ds(theirs, quarter)],
            self.region(1 - place.core, place.core, **place.at),
            place.other_core(),
        )
        self.own = self.copies.move(
            self.source.at[:, pl.ds(mine, quarter)], self.region(place.core, place.core, **place.at)
        )

    def ready(self):
        self.first.wait_recv()
        self.own.wait()

    def block(self, axis, index, core):
        sel = {a: self.place.at[a] for a in "xyz" if a not in self.done}
        return self.region(self.place.core, core, **{**sel, axis: index})

    def pass_on(self, phase, index, core):
        if phase == 2:
            piece = self.block(self.order[2], index, core)
            self.to_core.append(self.copies.send(piece, piece, self.place.other_core()))

    def start(self, phase):
        axis, place = self.order[phase], self.place
        self.arriving = {}
        for way, core in ((1, 0), (-1, 1), (1, 1), (-1, 0)):
            piece = self.block(axis, place.at[axis], core)
            self.arriving[way, core] = self.copies.send(piece, piece, place.along(axis, way))
        self.pass_on(phase, place.at[axis], None)

    def forward(self, phase):
        axis, place = self.order[phase], self.place
        self.last = {}
        for way, core in ((1, 0), (-1, 1)):
            self.arriving[way, core].wait_recv()
            piece = self.block(axis, place.step(axis, -way), core)
            self.last[way, core] = self.copies.send(piece, piece, place.along(axis, way))
            self.pass_on(phase, place.step(axis, -way), core)

    def finish(self, phase):
        axis, place = self.order[phase], self.place
        for way, core in ((1, 1), (-1, 0)):
            self.arriving[way, core].wait_recv()
            self.pass_on(phase, place.step(axis, -way), core)
        for way, core in ((1, 0), (-1, 1)):
            self.last[way, core].wait_recv()
            self.pass_on(phase, place.step(axis, 2), core)
        self.done.append(axis)


def add_rows(out, left, right, count):
    def body(i, _):
        out[i] = (left[i].astype(F32) + right[i].astype(F32)).astype(out.dtype)
        return 0

    lax.fori_loop(0, count, body, 0)


def enter_kernel(
    w0, w1, w2, w3, tokens, partial_mod,
    o0, o1, o2, o3, other_tokens, modulation,
    got_core, sum_core, got_z, sum_z, got_x, sum_x, got_y,
    send_sems, recv_sems, local_sems,
):
    place = Place()
    copies = Copies(send_sems, recv_sems, local_sems)
    greet(place.everyone())
    gathers = [
        Gather(place, copies, source, out, spec[1], spec[2])
        for source, out, spec in zip((w0, w1, w2, w3), (o0, o1, o2, o3), WEIGHTS)
    ]
    for gather in gathers:
        gather.begin()
    mod_core = copies.send(
        partial_mod.at[:, :, :, 1 - place.core], got_core, place.other_core()
    )
    for gather in gathers:
        gather.ready()
        gather.start(0)
    tokens_copy = copies.send(tokens, other_tokens, place.along("z", 2))

    mod_core.wait_recv()
    for z_lo in range(2):
        for x in range(4):
            for y in range(4):
                sum_core[z_lo, x, y] = (
                    partial_mod[z_lo, x, y, place.core].astype(F32) + got_core[z_lo, x, y].astype(F32)
                ).astype(BF16)
    mod_z = copies.send(sum_core.at[1 - place.z_lo], got_z, place.other_z_lo())
    for gather in gathers:
        gather.forward(0)
    mod_z.wait_recv()
    for x in range(4):
        for y in range(4):
            sum_z[x, y] = (
                sum_core[place.z_lo, x, y].astype(F32) + got_z[x, y].astype(F32)
            ).astype(BF16)
    mod_x = [
        copies.send(sum_z.at[place.step("x", distance)], got_x.at[distance - 1], place.along("x", distance))
        for distance in (1, 2, 3)
    ]
    for gather in gathers:
        gather.finish(0)
        gather.start(1)
    for copy in mod_x:
        copy.wait_recv()
    for y in range(4):
        total = sum_z[place.at["x"], y].astype(F32)
        for slot in range(3):
            total += got_x[slot, y].astype(F32)
        sum_x[y] = total.astype(BF16)
    mod_y = [
        copies.send(sum_x.at[place.step("y", distance)], got_y.at[distance - 1], place.along("y", distance))
        for distance in (1, 2, 3)
    ]
    for gather in gathers:
        gather.forward(1)
    for copy in mod_y:
        copy.wait_recv()
    total = sum_x[place.at["y"]].astype(F32)
    for slot in range(3):
        total += got_y[slot].astype(F32)
    modulation[...] = total
    for gather in gathers:
        gather.finish(1)
        gather.start(2)
    for gather in gathers:
        gather.forward(2)
    for gather in gathers:
        gather.finish(2)
    tokens_copy.wait_recv()
    for gather in gathers:
        for copy in gather.to_core:
            copy.wait_recv()
    copies.drain()


def enter(weights, tokens, partial_mod):
    anywhere = pl.BlockSpec(memory_space=pl.ANY)
    inside = pl.BlockSpec(memory_space=pltpu.VMEM)
    slab = (48, 128)
    shapes = [jax.ShapeDtypeStruct((2, 4, 4, 2, rows, columns), BF16) for rows, columns, _ in WEIGHTS]
    shapes += [jax.ShapeDtypeStruct((HALF, D), BF16), jax.ShapeDtypeStruct(slab, F32)]
    out = pl.pallas_call(
        enter_kernel,
        out_shape=shapes,
        in_specs=[anywhere] * 5 + [inside],
        out_specs=[anywhere] * 5 + [inside],
        scratch_shapes=[
            pltpu.VMEM((2, 4, 4) + slab, BF16),
            pltpu.VMEM((2, 4, 4) + slab, BF16),
            pltpu.VMEM((4, 4) + slab, BF16),
            pltpu.VMEM((4, 4) + slab, BF16),
            pltpu.VMEM((3, 4) + slab, BF16),
            pltpu.VMEM((4,) + slab, BF16),
            pltpu.VMEM((3,) + slab, BF16),
        ]
        + copy_scratch(4 * 26 + 9, 4),
        compiler_params=pltpu.CompilerParams(
            collective_id=0, has_side_effects=True, vmem_limit_bytes=32 * 2**20
        ),
        name="enter",
    )(*weights, tokens, partial_mod)
    full = [
        whole.reshape(64 * rows, columns) for whole, (rows, columns, _) in zip(out[:4], WEIGHTS)
    ]
    return full, out[4], out[5].reshape(6, D)


class SmallGather:
    def __init__(self, place, copies, whole):
        self.place, self.copies, self.whole = place, copies, whole
        self.waiting = []

    def arrive(self):
        for copy in self.waiting:
            copy.wait_recv()
        self.waiting = []

    def stage(self, which):
        self.arrive()
        place, whole, send = self.place, self.whole, self.copies.send
        at, core = place.at, place.core
        if which == 0:
            piece = whole.at[place.z_lo, at["x"], at["y"], core]
            self.waiting = [send(piece, piece, place.along("y", d)) for d in (1, 2, 3)]
        elif which == 1:
            piece = whole.at[place.z_lo, at["x"], :, core]
            self.waiting = [send(piece, piece, place.along("x", d)) for d in (1, 2, 3)]
        elif which == 2:
            piece = whole.at[place.z_lo, :, :, core]
            self.waiting = [send(piece, piece, place.other_z_lo())]
        else:
            piece = whole.at[:, :, :, core]
            self.waiting = [send(piece, piece, place.other_core())]


def ids_kernel(own, whole, send_sems, recv_sems, local_sems):
    place = Place()
    copies = Copies(send_sems, recv_sems, local_sems)
    whole[place.z_lo, place.at["x"], place.at["y"], place.core] = own[...]
    greet(place.everyone())
    gather = SmallGather(place, copies, whole)
    for which in range(4):
        gather.stage(which)
    gather.arrive()
    copies.drain()


def gather_ids(labels, timesteps):
    inside = pl.BlockSpec(memory_space=pltpu.VMEM)
    lane = lax.broadcasted_iota(jnp.int32, (8, 128), 1)
    own = jnp.where(lane == 0, labels[0], timesteps[0])
    whole = pl.pallas_call(
        ids_kernel,
        out_shape=jax.ShapeDtypeStruct((2, 4, 4, 2, 8, 128), jnp.int32),
        in_specs=[inside],
        out_specs=inside,
        scratch_shapes=copy_scratch(8, 0),
        compiler_params=pltpu.CompilerParams(collective_id=1, has_side_effects=True),
        name="gather_ids",
    )(own).reshape(64, 8, 128)
    return whole[:, 0, 0], whole[:, 0, 1]


def swap_kernel(own, other, send_sems, recv_sems, local_sems):
    place = Place()
    copies = Copies(send_sems, recv_sems, local_sems)
    partner = place.along("z", 2)
    greet([partner])
    copies.send(own, other, partner).wait_recv()
    copies.drain()


def swap(own):
    inside = pl.BlockSpec(memory_space=pltpu.VMEM)
    return pl.pallas_call(
        swap_kernel,
        out_shape=jax.ShapeDtypeStruct(own.shape, own.dtype),
        in_specs=[inside],
        out_specs=inside,
        scratch_shapes=copy_scratch(1, 0),
        compiler_params=pltpu.CompilerParams(collective_id=2, has_side_effects=True),
        name="swap",
    )(own)


class Scatter:
    def __init__(self, place, copies, spec, left, right, lefts, rights, parts, bufs, final, out):
        self.place, self.copies = place, copies
        self.rows, self.columns, self.order = spec[0], spec[1], spec[2][::-1]
        self.left, self.right, self.lefts, self.rights = left, right, lefts, rights
        self.parts, self.bufs, self.final, self.out = parts, bufs, final, out
        self.done = []

    def begin(self):
        place, copies, quarter = self.place, self.copies, self.columns // 4
        self.inputs = [copies.send(self.left, self.lefts.at[pl.ds(HALF, HALF)], place.other_core())]
        for q in range(2):
            start = pl.multiple_of((1 - place.core) * 2 * quarter + q * quarter, 128)
            self.inputs.append(
                copies.send(
                    self.right.at[:, pl.ds(start, quarter)],
                    self.rights.at[q, pl.ds(HALF, HALF)],
                    place.other_core(),
                )
            )
        self.own = [copies.move(self.left, self.lefts.at[pl.ds(0, HALF)])]
        for q in range(2):
            start = pl.multiple_of(place.core * 2 * quarter + q * quarter, 128)
            self.own.append(
                copies.move(self.right.at[:, pl.ds(start, quarter)], self.rights.at[q, pl.ds(0, HALF)])
            )

    def make(self):
        for copy in self.inputs:
            copy.wait_recv()
        for copy in self.own:
            copy.wait()
        rows, quarter = self.rows, self.columns // 4
        chunk = 8 * rows

        def body(i, _):
            q, z_lo, x = lax.div(i, 8), lax.rem(lax.div(i, 4), 2), lax.rem(i, 4)
            start = pl.multiple_of(lax.rem(i, 8) * chunk, 128)
            made = lax.dot_general(
                self.lefts[:, pl.ds(start, chunk)],
                self.rights[q],
                (((0,), (0,)), ((), ())),
                preferred_element_type=F32,
            )
            self.parts[2 * q + z_lo, x] = made.astype(BF16).reshape(4, 2, rows, quarter)
            return 0

        lax.fori_loop(0, 16, body, 0)

    def sel(self, axis, index):
        at = {a: self.place.at[a] if a in self.done else None for a in "xyz"}
        at[axis] = index
        return [at[a] for a in "zxy"]

    def block(self, axis, index, core):
        lead = [slice(None) if i is None else i for i in self.sel(axis, index)]
        return self.parts.at[(*lead, core)]

    def add(self, axis, index, core, bufs):
        sel = self.sel(axis, index)
        free = [i for i, s in enumerate(sel) if s is None]

        def body(step, _):
            where, inner = list(sel), []
            for i in reversed(free):
                where[i] = lax.rem(step, 4)
                inner.insert(0, where[i])
                step = lax.div(step, 4)
            total = self.parts[(*where, core)].astype(F32)
            for buf in bufs:
                total += buf[tuple(inner)].astype(F32)
            self.parts[(*where, core)] = total.astype(BF16)
            return 0

        if free:
            lax.fori_loop(0, 4 ** len(free), body, 0)
        else:
            body(jnp.int32(0), 0)

    def start(self, phase):
        axis, place = self.order[phase], self.place
        buf = self.bufs[phase]
        send = self.copies.send
        up, down = place.along(axis, 1), place.along(axis, -1)
        far = place.step(axis, 2)
        self.far = {
            1: send(self.block(axis, far, 0), buf.at[0], up),
            -1: send(self.block(axis, far, 1), buf.at[1], down),
        }
        self.raw = {
            1: send(self.block(axis, place.step(axis, 1), 1), buf.at[3], up),
            -1: send(self.block(axis, place.step(axis, -1), 0), buf.at[2], down),
        }

    def forward(self, phase):
        axis, place = self.order[phase], self.place
        buf = self.bufs[phase]
        self.near = {}
        for way, core in ((1, 0), (-1, 1)):
            self.far[way].wait_recv()
            index = place.step(axis, way)
            self.add(axis, index, core, [buf.at[core]])
            self.near[way] = self.copies.send(
                self.block(axis, index, core), buf.at[4 + core], place.along(axis, way)
            )

    def finish(self, phase):
        axis, place = self.order[phase], self.place
        buf = self.bufs[phase]
        for way, core in ((1, 0), (-1, 1)):
            self.raw[-way].wait_recv()
            self.near[way].wait_recv()
            self.add(axis, place.at[axis], core, [buf.at[2 + core], buf.at[4 + core]])
        self.done.append(axis)

    def share(self):
        place, at = self.place, self.place.at
        slot = place.core * 2 + place.z_hi
        mine = self.parts.at[at["z"], at["x"], at["y"], place.core]
        theirs = self.parts.at[at["z"], at["x"], at["y"], 1 - place.core]
        far = place.step("z", 2)
        target = self.final.at[slot]
        self.shared = [
            self.copies.send(theirs, target, place.other_core()),
            self.copies.send(mine, target, place.device(z=far)),
            self.copies.send(theirs, target, place.device(z=far, core=1 - place.core)),
        ]
        self.kept = self.copies.move(mine, target)

    def store(self):
        for copy in self.shared:
            copy.wait_recv()
        self.kept.wait()
        quarter = self.columns // 4
        for slot in range(4):
            self.out[:, slot * quarter : (slot + 1) * quarter] = self.final[slot].astype(F32)


LEFTS = (D, D, D, FF)


def leave_kernel(*refs):
    refs = list(refs)

    def take(count):
        taken, refs[:count] = refs[:count], []
        return taken

    lefts_in, rights_in = take(4), take(4)
    (vector,) = take(1)
    outs = take(4)
    (whole,) = take(1)
    lefts, rights, parts = take(4), take(4), take(4)
    bufs = [take(3) for _ in range(4)]
    finals = take(4)
    (vector_got,) = take(1)
    send_sems, recv_sems, local_sems = refs
    place = Place()
    copies = Copies(send_sems, recv_sems, local_sems)
    far = place.step("z", 2)
    greet(place.everyone() + [place.device(z=far, core=1 - place.core)])
    scatters = [
        Scatter(place, copies, WEIGHTS[i], lefts_in[i], rights_in[i], lefts[i], rights[i], parts[i], bufs[i], finals[i], outs[i])
        for i in (3, 2, 0, 1)
    ]
    for scatter in scatters:
        scatter.begin()
    vector_copy = copies.send(vector, vector_got, place.along("z", 2))
    for scatter in scatters:
        scatter.make()
        scatter.start(0)
    vector_copy.wait_recv()
    whole[place.z_lo, place.at["x"], place.at["y"], place.core] = (
        vector[...].astype(F32) + vector_got[...].astype(F32)
    ).astype(BF16)
    gather = SmallGather(place, copies, whole)
    gather.stage(0)
    for scatter in scatters:
        scatter.forward(0)
    gather.stage(1)
    for scatter in scatters:
        scatter.finish(0)
        scatter.start(1)
    gather.stage(2)
    for scatter in scatters:
        scatter.forward(1)
    gather.stage(3)
    for scatter in scatters:
        scatter.finish(1)
        scatter.start(2)
    for scatter in scatters:
        scatter.forward(2)
    for scatter in scatters:
        scatter.finish(2)
        scatter.share()
    gather.arrive()
    for scatter in scatters:
        scatter.store()
    copies.drain()


def buffer_shapes(rows, columns, order):
    shapes = []
    for left in (2, 1, 0):
        shapes.append(pltpu.VMEM((6,) + (4,) * left + (rows, columns // 4), BF16))
    return shapes


def leave(lefts, rights, vector):
    anywhere = pl.BlockSpec(memory_space=pl.ANY)
    inside = pl.BlockSpec(memory_space=pltpu.VMEM)
    scratch = [pltpu.VMEM((SEQ, width), BF16) for width in LEFTS]
    scratch += [pltpu.VMEM((2, SEQ, columns // 4), BF16) for _, columns, _ in WEIGHTS]
    scratch += [pltpu.VMEM((4, 4, 4, 2, rows, columns // 4), BF16) for rows, columns, _ in WEIGHTS]
    for spec in WEIGHTS:
        scratch += buffer_shapes(*spec)
    scratch += [pltpu.VMEM((4, rows, columns // 4), BF16) for rows, columns, _ in WEIGHTS]
    scratch += [pltpu.VMEM(vector.shape, BF16)]
    scratch += copy_scratch(4 * 24 + 9, 16)
    return pl.pallas_call(
        leave_kernel,
        out_shape=[jax.ShapeDtypeStruct((rows, columns), F32) for rows, columns, _ in WEIGHTS]
        + [jax.ShapeDtypeStruct((2, 4, 4, 2) + vector.shape, BF16)],
        in_specs=[anywhere] * 8 + [inside],
        out_specs=[inside] * 5,
        scratch_shapes=scratch,
        compiler_params=pltpu.CompilerParams(
            collective_id=3, has_side_effects=True, vmem_limit_bytes=56 * 2**20
        ),
        name="leave",
    )(*lefts, *rights, vector)


def normalize(values):
    centre = values - jnp.mean(values, -1, keepdims=True)
    spread = jnp.mean(centre * centre, -1, keepdims=True)
    return centre * lax.rsqrt(spread + EPSILON)


def modulated(values, shift_vec, scale_vec):
    return normalize(values) * (1.0 + scale_vec) + shift_vec


def gelu_tanh(values):
    return jax.nn.gelu(values, approximate=True)


def sinusoid(step_ids):
    half_width = FREQ // 2
    freq_rates = jnp.exp(
        -math.log(10000.0) * jnp.arange(half_width, dtype=jnp.float32) / half_width
    )
    angles = step_ids.astype(jnp.float32)[:, None] * freq_rates[None, :]
    return jnp.concatenate([jnp.cos(angles), jnp.sin(angles)], axis=-1)


def head_split(rows_in):
    return rows_in.reshape(rows_in.shape[0], HEADS, HEAD)


def attend_scores(query_rows, key_rows):
    return jnp.einsum(
        "qhd,khd->hqk",
        head_split(query_rows),
        head_split(key_rows),
        preferred_element_type=F32,
    ) * HEAD ** (-0.5)


def per_device(
    tokens,
    labels,
    timesteps,
    cotangent,
    class_table,
    time_weight,
    modulate_weight,
    modulate_offset,
    attend_weight,
    output_weight,
    expand_weight,
    hidden_offset,
    contract_weight,
):
    shard_index = lax.axis_index("fsdp")
    token_half = lax.axis_index("ctx")
    all_labels, all_steps = gather_ids(labels, timesteps)
    onehot = all_labels[:, None] == jnp.arange(CLASSES, dtype=jnp.int32)[None, :]
    sinus_rows = sinusoid(all_steps).astype(BF16)
    cond_cols = jnp.dot(
        onehot.astype(BF16), class_table, preferred_element_type=F32
    ) + jnp.dot(sinus_rows, time_weight, preferred_element_type=F32)
    offset_width = modulate_offset.shape[1]
    act_cols = jax.nn.silu(cond_cols).astype(BF16)
    partial_mod = jnp.dot(act_cols, modulate_weight[0], preferred_element_type=F32)
    placed = lax.dynamic_update_slice(
        jnp.zeros((1, 6 * D), F32),
        modulate_offset.astype(F32),
        (jnp.int32(0), shard_index * offset_width),
    )
    partial_mod = (partial_mod + placed).astype(BF16).reshape(2, 4, 4, 2, 48, 128)
    (w_attend, w_output, w_expand, w_contract), other_tokens, modulation = enter(
        (attend_weight[0], output_weight[0], expand_weight[0], contract_weight[0]),
        tokens[0],
        partial_mod,
    )
    b_hidden = lax.all_gather(hidden_offset[0], "fsdp", axis=0, tiled=True)
    shift_one, scale_one, gate_one, shift_two, scale_two, gate_two = [modulation[i] for i in range(6)]

    hidden = tokens[0].astype(F32)
    both_hidden = jnp.concatenate([tokens[0], other_tokens], 0).astype(F32)
    both_first = modulated(both_hidden, shift_one, scale_one).astype(BF16)
    first_in = both_first[:HALF]
    projected = jnp.dot(both_first, w_attend, preferred_element_type=F32).astype(BF16)
    query_rows, key_rows, value_rows = projected[:, :D], projected[:, D : 2 * D], projected[:, 2 * D :]
    scores = attend_scores(query_rows, key_rows)
    top_score = jnp.max(scores, -1, keepdims=True)
    exp_terms = jnp.exp(scores - top_score)
    totals = jnp.sum(exp_terms, -1, keepdims=True)
    softmaxed = exp_terms / totals
    rounded_probs = softmaxed.astype(BF16)
    attended = (
        jnp.einsum(
            "hqk,khd->qhd", rounded_probs[:, :HALF], head_split(value_rows), preferred_element_type=F32
        )
        .reshape(-1, D)
        .astype(BF16)
    )
    branch_one = jnp.dot(attended, w_output, preferred_element_type=F32)
    middle = hidden + gate_one * branch_one
    second_in = modulated(middle, shift_two, scale_two).astype(BF16)
    pre_act = jnp.dot(second_in, w_expand, preferred_element_type=F32) + b_hidden.astype(F32)
    activated = gelu_tanh(pre_act).astype(BF16)
    branch_two = jnp.dot(activated, w_contract, preferred_element_type=F32)
    result = (middle + gate_two * branch_two).astype(BF16)[None]

    grad_hidden = cotangent[0].astype(F32)
    grad_two = (grad_hidden * gate_two).astype(BF16)
    gate_two_grad = jnp.sum(grad_hidden * branch_two, 0)
    grad_act = jnp.einsum("td,fd->tf", grad_two, w_contract, preferred_element_type=F32)
    _, gelu_pull = jax.vjp(gelu_tanh, pre_act)
    grad_pre = gelu_pull(grad_act)[0].astype(BF16)
    hidden_term = jnp.sum(grad_pre.astype(F32), 0)
    grad_second = jnp.einsum("tf,df->td", grad_pre, w_expand, preferred_element_type=F32)
    _, second_pull = jax.vjp(modulated, middle, shift_two, scale_two)
    grad_middle, shift_two_grad, scale_two_grad = second_pull(grad_second)
    grad_middle = grad_hidden + grad_middle
    grad_one = (grad_middle * gate_one).astype(BF16)
    gate_one_grad = jnp.sum(grad_middle * branch_one, 0)
    grad_att = jnp.einsum("te,de->td", grad_one, w_output, preferred_element_type=F32).astype(BF16)
    both_att = jnp.concatenate([grad_att, swap(grad_att)], 0)
    grad_heads = head_split(both_att)
    grad_probs = jnp.einsum(
        "qhd,khd->hqk", grad_heads, head_split(value_rows), preferred_element_type=F32
    )
    grad_scores = (
        softmaxed * (grad_probs - jnp.sum(softmaxed * grad_probs, -1, keepdims=True))
    ).astype(BF16)
    grad_query = jnp.einsum(
        "hqk,khd->qhd", grad_scores[:, :HALF], head_split(key_rows), preferred_element_type=F32
    ) * HEAD ** (-0.5)
    grad_key = jnp.einsum(
        "hqk,qhd->khd", grad_scores[:, :, :HALF], head_split(query_rows), preferred_element_type=F32
    ) * HEAD ** (-0.5)
    grad_value = jnp.einsum(
        "hqk,qhd->khd", rounded_probs[:, :, :HALF], grad_heads, preferred_element_type=F32
    )
    grad_proj = jnp.concatenate(
        [part.reshape(-1, D).astype(BF16) for part in (grad_query, grad_key, grad_value)], 1
    )
    grad_first = jnp.einsum("te,de->td", grad_proj, w_attend, preferred_element_type=F32)
    _, first_pull = jax.vjp(modulated, hidden, shift_one, scale_one)
    grad_input, shift_one_grad, scale_one_grad = first_pull(grad_first)
    tokens_grad = (grad_middle + grad_input)[None]

    vector = jnp.concatenate(
        [
            shift_one_grad,
            scale_one_grad,
            gate_one_grad,
            shift_two_grad,
            scale_two_grad,
            gate_two_grad,
            hidden_term,
        ]
    )
    vector = vector.astype(BF16).reshape(80, 128)
    attend_grad, output_grad, expand_grad, contract_grad, all_vectors = leave(
        (first_in, attended, second_in, activated), (grad_proj, grad_one, grad_pre, grad_two), vector
    )
    all_vectors = all_vectors.reshape(64, 80 * 128)
    all_mod = all_vectors[:, : 6 * D]
    own_hidden = lax.dynamic_slice_in_dim(all_vectors, 6 * D + shard_index * (FF // 64), FF // 64, 1)
    hidden_grad = jnp.sum(own_hidden.astype(F32), 0)
    grad_act_cols = jnp.einsum("bk,dk->bd", all_mod, modulate_weight[0], preferred_element_type=F32)
    modulate_grad = jnp.einsum("bd,bk->dk", act_cols, all_mod, preferred_element_type=F32)
    own_cols = lax.dynamic_slice_in_dim(all_mod, shard_index * offset_width, offset_width, 1)
    offset_grad = jnp.sum(own_cols.astype(F32), 0)
    _, silu_pull = jax.vjp(jax.nn.silu, cond_cols)
    grad_cond = silu_pull(grad_act_cols)[0]
    table_grad = jnp.einsum("bc,bd->cd", onehot.astype(F32), grad_cond, precision=HIGHEST)
    time_grad = jnp.einsum("bf,bd->fd", sinus_rows.astype(F32), grad_cond, precision=HIGHEST)
    return (
        result,
        tokens_grad,
        table_grad,
        time_grad,
        modulate_grad[None],
        offset_grad[None],
        attend_grad[None],
        output_grad[None],
        expand_grad[None],
        hidden_grad[None],
        contract_grad[None],
    )


def solution(mesh):
    rows = P(None, "fsdp", None)
    columns = P(None, "fsdp")
    halves = P("fsdp", "ctx", None)
    each = P("fsdp")
    in_specs = (
        halves, each, each, halves, columns, columns, rows, columns, rows, rows, rows, columns, rows,
    )
    out_specs = (
        halves, halves, columns, columns, rows, columns, rows, rows, rows, columns, rows,
    )
    return jax.shard_map(
        per_device, mesh=mesh, in_specs=in_specs, out_specs=out_specs, check_vma=False
    )
```

time: 2350 us -> 418 us (0.18)
  waiting for transfers between devices: 1660 us -> 0 us
  blocking collectives: 555 us -> 142 us
  Pallas kernels: 0 us -> 191 us
  matrix products: 77.4 us -> 50.4 us
    reduce_scatter x4 -> x0, waiting for transfers between devices: 792 us -> none  [the longest x1 308 us: per_device(): lax.psum_scatter(expand_term, 'fsdp', scatter_dimension=0, tiled=True)]
    unnamed x15 -> x0, waiting for transfers between devices: 432 us -> none
    all_gather x4 -> x0, waiting for transfers between devices: 402 us -> none  [the longest x1 110 us: per_device(): lax.all_gather(attend_weight[which_layer], 'fsdp', axis=0, tiled=True)]
    unnamed x3 -> x1, blocking collectives: 436 us -> 142 us
    pallas_call x0 -> x4, Pallas kernels: none -> 191 us  [the longest x1 84.9 us: leave(): pl.pallas_call(leave_kernel, out_shape=[jax.ShapeDtypeStruct((rows, colum...]
    all_gather x3 -> x0, blocking collectives: 110 us -> none  [the longest x1 90.8 us: per_device(): all_mod = lax.all_gather(mod_rounded, 'fsdp', axis=0, tiled=True)]
    dot_general x25 -> x19, matrix products: 77.4 us -> 38.5 us  [the longest x1 6.5 us: per_device(): jnp.dot(second_in, w_expand, preferred_element_type=F32)]
    psum x1 -> x0, waiting for transfers between devices: 36.5 us -> none  [per_device(): lax.psum(stacked[0].astype(jnp.bfloat16), 'ctx').astype(jnp.float32)]
  transfers between devices with their start and end apart: 12 -> 0, of which waited for: 11 -> 0; matrix products, arithmetic and copies ran while one was open for 3% -> 0% of each run, Pallas kernels for 0% -> 0%
where the time goes in v1:
time: 418 us
  Pallas kernels  191 us (46%)
  blocking collectives  142 us (34%)
  matrix products  50.4 us (12%)
  local copies, waits for them, and re-layouts  22.2 us (5%)
  other arithmetic  8.82 us (2%)
    unnamed x1, blocking collectives  142 us
    pallas_call x1, Pallas kernels, leave(): pl.pallas_call(leave_kernel, out_shape=[jax.ShapeDtypeStruct((rows, colum...  84.9 us
    pallas_call x1, Pallas kernels, enter(): pl.pallas_call(enter_kernel, out_shape=shapes, in_specs=[anywhere] * 5 +...  78.5 us
    pallas_call x1, Pallas kernels, gather_ids(): pl.pallas_call(ids_kernel, out_shape=jax.ShapeDtypeStruct((2, 4, 4, 2, 8,...  16.2 us
    unnamed x79, local copies, waits for them, and re-layouts  11.4 us
    pallas_call x1, Pallas kernels, swap(): pl.pallas_call(swap_kernel, out_shape=jax.ShapeDtypeStruct(own.shape, own...  11.2 us

profile of v1, /device:TPU:1, one launch (start us, length us, event | category | flops | bytes accessed | tf_op | source)
XLA Modules:
  0.0 417.6 jit_solution(3917186194063923697)
XLA Ops:
  2.1 1.2 dynamic-slice
  4.0 0.6 iota.16.own
  4.6 0.8 dynamic-update-slice
  5.4 142.1 %all-reduce = bf16[4096]{0:T(1024)(128)(2,1)S(1)} all-reduce(bf16[4096]{0:T(1024)(128)(2,1)S(1)} %dynamic-update-slice), channel_id=2, replica_groups=mesh['fsdp'=64,'ctx'=2] {'fsdp'}, use_global_device_ids=true, to_apply=%add | all-reduce | flops 4096 | bytes 16384
  147.6 0.8 convert_dynamic-update-slice_fusion
  148.3 16.2 %gather_ids.1 = s32[2,4,4,2,8,128]{5,4,3,2,1,0:T(8,128)} custom-call(s32[8,128]{1,0:T(8,128)} %iota.16.own), custom_call_target="tpu_custom_call" | custom-call | tf_op jit(solution)/shard_map/gather_ids/pallas_call | solution.py:355
  164.5 1.2 fusion.82
  165.8 1.0 fusion.56
  166.8 0.2 fusion.62
  167.1 0.8 convolution_add_fusion.2
  167.9 0.4 fusion.17
  168.5 78.5 %enter.1 = (bf16[2,4,4,2,16,3072]{5,4,3,2,1,0:T(8,128)(2,1)S(1)}, bf16[2,4,4,2,16,1024]{5,4,3,2,1,0:T(8,128)(2,1)S(1)}, bf16[2,4,4,2,16,4096]{5,4,3,2,1,0:T(8,12...) custom-call(bf16[16,3072]{1,0:T(8,128)(2,1)S(1)} %bitcast.158, ...), custom_call_target="tpu_custom_call" | custom-call | tf_op jit(solution)/shard_map/enter/pallas_call | solution.py:285
  247.0 0.1 convert_reduce_fusion
  247.1 0.3 fusion.22
  247.4 0.3 fusion.25
  247.7 1.2 slice.83.refs_0_
  249.0 1.8 convolution_convert_fusion
  250.8 1.4 copy-done.7
  252.2 1.1 fusion.81
  253.3 2.1 copy.46
  255.4 1.0 copy.45
  256.4 1.2 copy.44
  257.6 4.9 %fusion.83 = (f32[16,256]{1,0:T(8,128)S(1)}, f32[16,256,256]{1,2,0:T(8,128)}) fusion(bf16[256,16,64]{0,2,1:T(8,128)(2,1)} %bitcast.180, bf16[256,16,64]{0,2,1:T(8,128)(2,1)} %bitcast.178), kind=kOutput, calls=%fused_computation.147 | convolution fusion | flops 137363712 | bytes 5259264 | tf_op jit(solution)/shard_map/sub | solution.py:706
  262.6 2.6 fusion.78
  265.2 1.3 copy-done.8
  266.5 0.3 convolution_convert_fusion.3
  266.8 0.9 copy.55.refs_1_
  267.7 1.3 fusion.80
  268.9 0.2 multiply_reduce_fusion.5
  269.2 0.2 add_convert_fusion.1.refs_2_
  269.4 6.5 %multiply_convert_fusion.1 = (bf16[128,4096]{1,0:T(8,128)(2,1)}, f32[128,4096]{1,0:T(8,128)S(1)}) fusion(f32[4096]{0:T(1024)S(1)} %convert_element_type.165, bf16[128,1024]{1,0:T(8,128)(2,1)S(1)} %add_convert_fusion.1.refs_2_, bf16[1024,4096]{1,0:T(8,128)(2,1)} %bitcast.151), kind=kOutput, calls=%fused_computation.22 | convolution fusion | flops 1078984704 | bytes 11812864 | tf_op jit(solution)/shard_map/dot_general | solution.py:720
  275.9 4.1 fusion.84
  280.1 3.0 multiply_reduce_fusion.2
  283.1 0.3 fusion.79
  283.4 0.8 copy-done.11
  284.2 0.2 multiply_convert_fusion.2.refs_5_
  284.4 1.5 convolution_convert_fusion.2.own
  285.9 11.2 %swap.1 = bf16[128,1024]{1,0:T(8,128)(2,1)} custom-call(bf16[128,1024]{1,0:T(8,128)(2,1)} %convolution_convert_fusion.2.own), custom_call_target="tpu_custom_call" | custom-call | tf_op jit(solution)/shard_map/swap/pallas_call | solution.py:378
  297.1 1.1 pad_maximum_fusion.2
  298.2 1.0 copy.48
  299.2 7.0 %multiply_convert_fusion = bf16[16,256,256]{1,2,0:T(8,128)(2,1)} fusion(bf16[256,16,64]{0,2,1:T(8,128)(2,1)} %bitcast.174, bf16[256,16,64]{0,2,1:T(8,128)(2,1)} %bitcast.173, f32[16,256,256]{1,2,0:T(8,128)} %get-tuple-element.67, f32[16,256]{1,0:T(8,128)S(1)} %get-tuple-element.66), kind=kOutput, calls=%fused_computation.6 | convolution fusion | flops 274731264 | bytes 7356416 | tf_op jit(solution)/shard_map/sub | solution.py:745
  306.2 1.7 convolution_convert_fusion.1
  307.9 1.9 fusion.21
  309.8 0.3 fusion.20
  310.1 0.1 copy.52
  310.2 0.1 copy.53
  310.5 5.1 %fusion.40 = (f32[128]{0:T(128)S(1)}, f32[128]{0:T(128)S(1)}, f32[128,1024]{1,0:T(8,128)S(1)}) fusion(f32[128]{0:T(128)S(1)} %get-tuple-element.76, bf16[1,128,1024]{2,1,0:T(8,128)(2,1)S(1)} %copy-done.1, f32[1024]{0:T(1024)S(1)} %get-tuple-element.60, bf16[1024,3072]{1,0:T(8,128)(2,1)} %bitcast.161, bf16[128,1024]{1,0:T(8,128)(2,1)S(1)} %copy.54, ...), kind=kOutput, calls=%fused_computation.65 | convolution fusion | flops 808582912 | bytes 7869952 | tf_op jit(solution)/shard_map/te,de->td/dot_general | solution.py:759
  315.6 1.0 pad_maximum_fusion.refs_4_
  316.6 0.4 fusion.43
  317.2 0.2 copy-done.15
  317.4 5.9 %fusion.38 = (bf16[1024]{0:T(1024)(128)(2,1)S(1)}, bf16[1024]{0:T(1024)(128)(2,1)S(1)}, f32[1,128,1024]{2,1,0:T(8,128)}, bf16[1,128,1024]{2,1,0:T(8,128)(2,1)}, bf16[128,1024]{1,0:T(8,128)(2,1)}) fusion(bf16[1,128,1024]{2,1,0:T(8,128)(2,1)S(1)} %copy-done.18, f32[128,1024]{1,0:T(8,128)S(1)} %copy-done.15, f32[128,1024]{1,0:T(8,128)S(1)} %copy-done.12, ...), kind=kOutput, calls=%fused_computation.63 | convolution fusion | flops 1076492288 | bytes 13122048 | tf_op jit(solution)/shard_map/dot_general | solution.py:722
  323.4 0.6 copy-done.25
  324.0 84.9 %leave.1 = (f32[16,3072]{1,0:T(8,128)}, f32[16,1024]{1,0:T(8,128)}, f32[16,4096]{1,0:T(8,128)}, f32[64,1024]{1,0:T(8,128)}, bf16[2,4,4,2,80,128]{5,4,3,2,1,0:T(8,128)(2,1)}) custom-call(bf16[128,1024]{1,0:T(8,128)(2,1)} %slice.83.refs_0_, bf16[128,1024]{1,0:T(8,128)(2,1)} %copy.55.refs_1_, bf16[128,1024]{1,0:T(8,128)(2,1)} %copy-done.19, ...), custom_call_target="tpu_custom_call" | custom-call | tf_op jit(solution)/shard_map/leave/pallas_call | solution.py:608
  408.9 1.7 copy.65
  410.6 0.6 convert_reduce_fusion.2
  411.2 0.3 fusion.66
  411.5 0.8 fusion.64
  412.3 0.9 fusion.55
  413.2 1.0 convolution_bitcast_fusion
  414.2 0.6 convert_reduce_fusion.3
  414.8 0.7 copy.80
  415.5 0.6 copy.81
  416.1 0.7 copy.82
  416.9 0.7 copy.83
  (86 shorter events, 1.0 us)
Async XLA Ops:
  0.6 167.2 %copy-start = (bf16[1,16,6144]{2,1,0:T(8,128)(2,1)S(1)}, bf16[1,16,6144]{2,1,0:T(8,128)(2,1)}, u32[]{:S(2)}) copy-start(bf16[1,16,6144]{2,1,0:T(8,128)(2,1)} %param.19) | copy-start | bytes 589828
  0.7 167.8 %copy-start.1 = (bf16[1,128,1024]{2,1,0:T(8,128)(2,1)S(1)}, bf16[1,128,1024]{2,1,0:T(8,128)(2,1)}, u32[]{:S(2)}) copy-start(bf16[1,128,1024]{2,1,0:T(8,128)(2,1)} %param.13) | copy-start | bytes 786436
  0.7 167.8 %copy-start.4 = (bf16[1,64,1024]{2,1,0:T(8,128)(2,1)S(1)}, bf16[1,64,1024]{2,1,0:T(8,128)(2,1)}, u32[]{:S(2)}) copy-start(bf16[1,64,1024]{2,1,0:T(8,128)(2,1)} %param.25) | copy-start | bytes 393220
  0.7 167.8 %copy-start.3 = (bf16[1,16,4096]{2,1,0:T(8,128)(2,1)S(1)}, bf16[1,16,4096]{2,1,0:T(8,128)(2,1)}, u32[]{:S(2)}) copy-start(bf16[1,16,4096]{2,1,0:T(8,128)(2,1)} %param.23) | copy-start | bytes 393220
  0.7 167.8 %copy-start.6 = (bf16[1,16,1024]{2,1,0:T(8,128)(2,1)S(1)}, bf16[1,16,1024]{2,1,0:T(8,128)(2,1)}, u32[]{:S(2)}) copy-start(bf16[1,16,1024]{2,1,0:T(8,128)(2,1)} %param.22) | copy-start | bytes 98308
  0.7 167.8 %copy-start.5 = (bf16[1,16,3072]{2,1,0:T(8,128)(2,1)S(1)}, bf16[1,16,3072]{2,1,0:T(8,128)(2,1)}, u32[]{:S(2)}) copy-start(bf16[1,16,3072]{2,1,0:T(8,128)(2,1)} %param.21) | copy-start | bytes 294916
  247.0 3.8 copy-start.2
  247.0 5.2 %copy-start.7 = (bf16[2,4,4,2,16,3072]{5,4,3,2,1,0:T(8,128)(2,1)}, bf16[2,4,4,2,16,3072]{5,4,3,2,1,0:T(8,128)(2,1)S(1)}, u32[]{:S(2)}) copy-start(bf16[2,4,4,2,16,3072]{5,4,3,2,1,0:T(8,128)(2,1)S(1)} %get-tuple-element.24) | copy-start | bytes 18874372
  257.6 7.6 %copy-start.16 = (bf16[256,1024]{0,1:T(8,128)(2,1)}, bf16[256,1024]{0,1:T(8,128)(2,1)S(1)}, u32[]{:S(2)}) copy-start(bf16[256,1024]{0,1:T(8,128)(2,1)S(1)} %copy.44) | copy-start | bytes 1572868
  265.2 1.3 copy-start.8
  267.7 8.2 %slice-start.2 = ((s8[8388608]{0:T(1024)(128)(4,1)}), s8[4194304]{0:T(1024)(128)(4,1)S(1)}, s32[]{:S(2)}) async-start(s8[8388608]{0:T(1024)(128)(4,1)} %bitcast.163), calls=%async_computation.2 | async-start | bytes 8388608
  269.3 6.5 %copy-start.19 = (bf16[128,1024]{1,0:T(8,128)(2,1)}, bf16[128,1024]{1,0:T(8,128)(2,1)S(1)}, u32[]{:S(2)}) copy-start(bf16[128,1024]{1,0:T(8,128)(2,1)S(1)} %add_convert_fusion.1.refs_2_) | copy-start | bytes 786436
  269.3 6.5 %slice-start.3 = ((s8[8388608]{0:T(1024)(128)(4,1)}), s8[4194304]{0:T(1024)(128)(4,1)S(1)}, s32[]{:S(2)}) async-start(s8[8388608]{0:T(1024)(128)(4,1)} %bitcast.163), calls=%async_computation.3 | async-start | bytes 8388608
  269.4 6.5 %copy-start.17 = (bf16[1,128,1024]{2,1,0:T(8,128)(2,1)S(1)}, bf16[1,128,1024]{2,1,0:T(8,128)(2,1)}, u32[]{:S(2)}) copy-start(bf16[1,128,1024]{2,1,0:T(8,128)(2,1)} %param.16) | copy-start | bytes 786436
  269.4 10.7 %slice-start = ((s8[8388608]{0:T(1024)(128)(4,1)}), s8[4194304]{0:T(1024)(128)(4,1)S(1)}, s32[]{:S(2)}) async-start(s8[8388608]{0:T(1024)(128)(4,1)} %bitcast.152), calls=%async_computation | async-start | bytes 8388608
  275.9 4.2 slice-start.1
  280.1 3.1 copy-start.13
  283.4 0.8 copy-start.11
  284.4 13.8 %copy-start.14 = (bf16[128,1024]{1,0:T(8,128)(2,1)}, bf16[128,1024]{1,0:T(8,128)(2,1)S(1)}, u32[]{:S(2)}) copy-start(bf16[128,1024]{1,0:T(8,128)(2,1)S(1)} %multiply_convert_fusion.2.refs_5_) | copy-start | bytes 786436
  299.2 7.0 %copy-start.9 = (bf16[16,256,256]{1,2,0:T(8,128)(2,1)S(1)}, bf16[16,256,256]{1,2,0:T(8,128)(2,1)}, u32[]{:S(2)}) copy-start(bf16[16,256,256]{1,2,0:T(8,128)(2,1)} %copy-done.8) | copy-start | bytes 6291460
  306.2 3.6 copy-start.20
  306.2 3.6 copy-start.26
  315.6 1.5 copy-start.10
  315.6 1.6 copy-start.12
  315.6 1.8 copy-start.15
  315.6 1.8 copy-start.18
  323.4 0.6 copy-start.25
  410.6 4.3 %copy-start.23 = (f32[16,3072]{1,0:T(8,128)S(1)}, f32[16,3072]{1,0:T(8,128)}, u32[]{:S(2)}) copy-start(f32[16,3072]{1,0:T(8,128)} %get-tuple-element.29) | copy-start | bytes 589828
  411.2 4.3 %copy-start.24 = (f32[16,1024]{1,0:T(8,128)S(1)}, f32[16,1024]{1,0:T(8,128)}, u32[]{:S(2)}) copy-start(f32[16,1024]{1,0:T(8,128)} %get-tuple-element.30) | copy-start | bytes 196612
  411.2 4.9 %copy-start.22 = (f32[16,4096]{1,0:T(8,128)S(1)}, f32[16,4096]{1,0:T(8,128)}, u32[]{:S(2)}) copy-start(f32[16,4096]{1,0:T(8,128)} %get-tuple-element.31) | copy-start | bytes 786436
  411.5 5.3 %copy-start.21 = (f32[64,1024]{1,0:T(8,128)S(1)}, f32[64,1024]{1,0:T(8,128)}, u32[]{:S(2)}) copy-start(f32[64,1024]{1,0:T(8,128)} %get-tuple-element.32) | copy-start | bytes 786436

commit v2 on v1

--- a/solution.py
+++ b/solution.py
@@ -17,17 +17,27 @@
 SEQ = 256
 HALF = SEQ // 2
 
-ATTEND = (16, 3 * D, "zyx")
-OUTPUT = (16, D, "zyx")
-EXPAND = (16, FF, "xzy")
-CONTRACT = (64, D, "yxz")
-WEIGHTS = (ATTEND, OUTPUT, EXPAND, CONTRACT)
+WEIGHTS = ((16, 3 * D), (16, D), (16, FF), (64, D))
+ORDERS = ("zyx", "xzy", "yxz")
+WAVES = tuple(
+    tuple((weight, row, column, order) for (weight, row, column), order in zip(wave, ORDERS))
+    for wave in (
+        ((0, 0, 0), (0, 0, D), (0, 0, 2 * D)),
+        ((1, 0, 0), (2, 0, 0), (2, 0, D)),
+        ((2, 0, 2 * D), (2, 0, 3 * D), (3, 0, 0)),
+        ((3, 16, 0), (3, 32, 0), (3, 48, 0)),
+    )
+)
+UNITS = tuple(unit for wave in WAVES for unit in wave)
+QUARTER = D // 4
 
 HIGHEST = lax.Precision.HIGHEST
 EPSILON = 1e-06
 MESH = pl.DeviceIdType.MESH
 BF16 = jnp.bfloat16
 F32 = jnp.float32
+NT = (((1,), (1,)), ((), ()))
+TN = (((0,), (0,)), ((), ()))
 
 
 class Place:
@@ -114,9 +124,10 @@
 
 
 class Gather:
-    def __init__(self, place, copies, source, out, columns, order):
+    def __init__(self, place, copies, source, out, unit, direct):
         self.place, self.copies, self.source, self.out = place, copies, source, out
-        self.half, self.order = columns // 2, order
+        self.direct = direct
+        _, self.row, self.column, self.order = unit
         self.done = []
         self.to_core = []
 
@@ -124,28 +135,29 @@
         lead = [sel.get(axis) for axis in "xy"]
         lead = [slice(None) if index is None else index for index in lead]
         z = sel.get("z")
-        start, width = half_index * self.half, self.half
+        start, width = self.column + half_index * 2 * QUARTER, 2 * QUARTER
         z_lo = slice(None)
         if z is not None:
-            width = self.half // 2
-            start = start + lax.div(z, 2) * width
+            width = QUARTER
+            start = start + lax.div(z, 2) * QUARTER
             z_lo = lax.rem(z, 2)
         core = slice(None) if core is None else core
-        return self.out.at[z_lo, lead[0], lead[1], core, :, pl.ds(pl.multiple_of(start, 128), width)]
+        rows = pl.ds(self.row, 16)
+        return self.out.at[z_lo, lead[0], lead[1], core, rows, pl.ds(pl.multiple_of(start, 128), width)]
 
     def begin(self):
         place = self.place
-        quarter = self.half // 2
-        mine = place.core * self.half + place.z_hi * quarter
-        theirs = (1 - place.core) * self.half + place.z_hi * quarter
+        mine = self.column + (place.core * 2 + place.z_hi) * QUARTER
+        theirs = self.column + ((1 - place.core) * 2 + place.z_hi) * QUARTER
         mine, theirs = pl.multiple_of(mine, 128), pl.multiple_of(theirs, 128)
+        rows = pl.ds(self.row, 16)
         self.first = self.copies.send(
-            self.source.at[:, pl.ds(theirs, quarter)],
+            self.source.at[rows, pl.ds(theirs, QUARTER)],
             self.region(1 - place.core, place.core, **place.at),
             place.other_core(),
         )
         self.own = self.copies.move(
-            self.source.at[:, pl.ds(mine, quarter)], self.region(place.core, place.core, **place.at)
+            self.source.at[rows, pl.ds(mine, QUARTER)], self.region(place.core, place.core, **place.at)
         )
 
     def ready(self):
@@ -164,6 +176,11 @@
     def start(self, phase):
         axis, place = self.order[phase], self.place
         self.arriving = {}
+        if phase in self.direct:
+            piece = self.block(axis, place.at[axis], None)
+            for distance in (1, 3, 2):
+                self.arriving[distance] = self.copies.send(piece, piece, place.along(axis, distance))
+            return
         for way, core in ((1, 0), (-1, 1), (1, 1), (-1, 0)):
             piece = self.block(axis, place.at[axis], core)
             self.arriving[way, core] = self.copies.send(piece, piece, place.along(axis, way))
@@ -180,6 +197,12 @@
 
     def finish(self, phase):
         axis, place = self.order[phase], self.place
+        self.done.append(axis)
+        if phase in self.direct:
+            for copy in self.arriving.values():
+                copy.wait_recv()
+            return
+        self.done.pop()
         for way, core in ((1, 1), (-1, 0)):
             self.arriving[way, core].wait_recv()
             self.pass_on(phase, place.step(axis, -way), core)
@@ -187,14 +210,6 @@
             self.last[way, core].wait_recv()
             self.pass_on(phase, place.step(axis, 2), core)
         self.done.append(axis)
-
-
-def add_rows(out, left, right, count):
-    def body(i, _):
-        out[i] = (left[i].astype(F32) + right[i].astype(F32)).astype(out.dtype)
-        return 0
-
-    lax.fori_loop(0, count, body, 0)
 
 
 def enter_kernel(
@@ -206,10 +221,29 @@
     place = Place()
     copies = Copies(send_sems, recv_sems, local_sems)
     greet(place.everyone())
-    gathers = [
-        Gather(place, copies, source, out, spec[1], spec[2])
-        for source, out, spec in zip((w0, w1, w2, w3), (o0, o1, o2, o3), WEIGHTS)
+    sources, wholes = (w0, w1, w2, w3), (o0, o1, o2, o3)
+    waves = [
+        [
+            Gather(place, copies, sources[unit[0]], wholes[unit[0]], unit, (0, 1) if index == 0 else (0,))
+            for unit in wave
+        ]
+        for index, wave in enumerate(WAVES)
     ]
+    gathers = [gather for wave in waves for gather in wave]
+
+    def start(wave, phase):
+        for gather in waves[wave]:
+            gather.start(phase)
+
+    def forward(wave, phase):
+        for gather in waves[wave]:
+            gather.forward(phase)
+
+    def finish(wave, phase):
+        for gather in waves[wave]:
+            gather.finish(phase)
+
+    tokens_copy = copies.send(tokens, other_tokens, place.along("z", 2))
     for gather in gathers:
         gather.begin()
     mod_core = copies.send(
@@ -218,8 +252,6 @@
     for gather in gathers:
         gather.ready()
         gather.start(0)
-    tokens_copy = copies.send(tokens, other_tokens, place.along("z", 2))
-
     mod_core.wait_recv()
     for z_lo in range(2):
         for x in range(4):
@@ -228,8 +260,9 @@
                     partial_mod[z_lo, x, y, place.core].astype(F32) + got_core[z_lo, x, y].astype(F32)
                 ).astype(BF16)
     mod_z = copies.send(sum_core.at[1 - place.z_lo], got_z, place.other_z_lo())
-    for gather in gathers:
-        gather.forward(0)
+    for wave in range(4):
+        finish(wave, 0)
+        start(wave, 1)
     mod_z.wait_recv()
     for x in range(4):
         for y in range(4):
@@ -240,9 +273,10 @@
         copies.send(sum_z.at[place.step("x", distance)], got_x.at[distance - 1], place.along("x", distance))
         for distance in (1, 2, 3)
     ]
-    for gather in gathers:
-        gather.finish(0)
-        gather.start(1)
+    finish(0, 1)
+    start(0, 2)
+    for wave in (1, 2, 3):
+        forward(wave, 1)
     for copy in mod_x:
         copy.wait_recv()
     for y in range(4):
@@ -254,21 +288,26 @@
         copies.send(sum_x.at[place.step("y", distance)], got_y.at[distance - 1], place.along("y", distance))
         for distance in (1, 2, 3)
     ]
-    for gather in gathers:
-        gather.forward(1)
+    finish(1, 1)
+    start(1, 2)
+    finish(2, 1)
+    forward(0, 2)
+    start(2, 2)
     for copy in mod_y:
         copy.wait_recv()
     total = sum_x[place.at["y"]].astype(F32)
     for slot in range(3):
         total += got_y[slot].astype(F32)
     modulation[...] = total
-    for gather in gathers:
-        gather.finish(1)
-        gather.start(2)
-    for gather in gathers:
-        gather.forward(2)
-    for gather in gathers:
-        gather.finish(2)
+    finish(3, 1)
+    forward(1, 2)
+    start(3, 2)
+    finish(0, 2)
+    forward(2, 2)
+    finish(1, 2)
+    forward(3, 2)
+    finish(2, 2)
+    finish(3, 2)
     tokens_copy.wait_recv()
     for gather in gathers:
         for copy in gather.to_core:
@@ -280,7 +319,7 @@
     anywhere = pl.BlockSpec(memory_space=pl.ANY)
     inside = pl.BlockSpec(memory_space=pltpu.VMEM)
     slab = (48, 128)
-    shapes = [jax.ShapeDtypeStruct((2, 4, 4, 2, rows, columns), BF16) for rows, columns, _ in WEIGHTS]
+    shapes = [jax.ShapeDtypeStruct((2, 4, 4, 2, rows, columns), BF16) for rows, columns in WEIGHTS]
     shapes += [jax.ShapeDtypeStruct((HALF, D), BF16), jax.ShapeDtypeStruct(slab, F32)]
     out = pl.pallas_call(
         enter_kernel,
@@ -296,14 +335,14 @@
             pltpu.VMEM((4,) + slab, BF16),
             pltpu.VMEM((3,) + slab, BF16),
         ]
-        + copy_scratch(4 * 26 + 9, 4),
+        + copy_scratch(12 * 23 + 9, 12),
         compiler_params=pltpu.CompilerParams(
             collective_id=0, has_side_effects=True, vmem_limit_bytes=32 * 2**20
         ),
         name="enter",
     )(*weights, tokens, partial_mod)
     full = [
-        whole.reshape(64 * rows, columns) for whole, (rows, columns, _) in zip(out[:4], WEIGHTS)
+        whole.reshape(64 * rows, columns) for whole, (rows, columns) in zip(out[:4], WEIGHTS)
     ]
     return full, out[4], out[5].reshape(6, D)
 
@@ -348,92 +387,90 @@
     copies.drain()
 
 
-def gather_ids(labels, timesteps):
+def gather_ids(labels, timesteps, offsets):
     inside = pl.BlockSpec(memory_space=pltpu.VMEM)
-    lane = lax.broadcasted_iota(jnp.int32, (8, 128), 1)
-    own = jnp.where(lane == 0, labels[0], timesteps[0])
+    lane = lax.broadcasted_iota(jnp.int32, (7, 128), 1)
+    ids = jnp.where(lane == 0, labels[0], timesteps[0]).astype(F32)
+    own = jnp.concatenate([jnp.pad(offsets.astype(F32)[None], ((0, 0), (0, 64))), ids], 0)
     whole = pl.pallas_call(
         ids_kernel,
-        out_shape=jax.ShapeDtypeStruct((2, 4, 4, 2, 8, 128), jnp.int32),
+        out_shape=jax.ShapeDtypeStruct((2, 4, 4, 2, 8, 128), F32),
         in_specs=[inside],
         out_specs=inside,
         scratch_shapes=copy_scratch(8, 0),
         compiler_params=pltpu.CompilerParams(collective_id=1, has_side_effects=True),
         name="gather_ids",
     )(own).reshape(64, 8, 128)
-    return whole[:, 0, 0], whole[:, 0, 1]
-
-
-def swap_kernel(own, other, send_sems, recv_sems, local_sems):
-    place = Place()
-    copies = Copies(send_sems, recv_sems, local_sems)
-    partner = place.along("z", 2)
-    greet([partner])
-    copies.send(own, other, partner).wait_recv()
-    copies.drain()
-
-
-def swap(own):
-    inside = pl.BlockSpec(memory_space=pltpu.VMEM)
-    return pl.pallas_call(
-        swap_kernel,
-        out_shape=jax.ShapeDtypeStruct(own.shape, own.dtype),
-        in_specs=[inside],
-        out_specs=inside,
-        scratch_shapes=copy_scratch(1, 0),
-        compiler_params=pltpu.CompilerParams(collective_id=2, has_side_effects=True),
-        name="swap",
-    )(own)
+    ids = whole[:, 1, :2].astype(jnp.int32)
+    return ids[:, 0], ids[:, 1], whole[:, 0, :64].reshape(FF)
+
+
+class Pair:
+    def __init__(self, place, copies, source, both, blocks=None):
+        self.copies = []
+        other = place.other_core()
+        if blocks is None:
+            self.copies.append(copies.send(source, both.at[pl.ds(HALF, HALF)], other))
+            self.copies.append(copies.move(source, both.at[pl.ds(0, HALF)]))
+            return
+        for block in range(blocks):
+            mine = pl.multiple_of(block * D + place.core * 2 * QUARTER, 128)
+            theirs = pl.multiple_of(block * D + (1 - place.core) * 2 * QUARTER, 128)
+            width = 2 * QUARTER
+            self.copies.append(
+                copies.send(source.at[:, pl.ds(theirs, width)], both.at[block, pl.ds(HALF, HALF)], other)
+            )
+            self.copies.append(
+                copies.move(source.at[:, pl.ds(mine, width)], both.at[block, pl.ds(0, HALF)])
+            )
+
+    def wait(self):
+        for index, copy in enumerate(self.copies):
+            if index % 2:
+                copy.wait()
+            else:
+                copy.wait_recv()
+
+
+def make_parts(left, right, scatters):
+    def body(i, _):
+        z_lo, x = lax.div(i, 4), lax.rem(i, 4)
+        chosen = left[:, pl.ds(pl.multiple_of(i * 128, 128), 128)]
+        for scatter in scatters:
+            made = lax.dot_general(
+                chosen, right[scatter.column // D], TN, preferred_element_type=F32
+            ).astype(BF16)
+            for q in range(2):
+                scatter.parts[2 * q + z_lo, x] = made[:, q * QUARTER : (q + 1) * QUARTER].reshape(
+                    4, 2, 16, QUARTER
+                )
+        return 0
+
+    lax.fori_loop(0, 8, body, 0)
+
+
+def make_tall_parts(left, right, scatters):
+    def body(i, _):
+        z_lo, x = lax.div(i, 4), lax.rem(i, 4)
+        chosen = left[:, pl.ds(pl.multiple_of(i * 512, 128), 512)]
+        made = lax.dot_general(chosen, right[0], TN, preferred_element_type=F32).astype(BF16)
+        made = made.reshape(4, 2, 64, 2 * QUARTER)
+        for scatter in scatters:
+            rows = made[:, :, scatter.row : scatter.row + 16]
+            for q in range(2):
+                scatter.parts[2 * q + z_lo, x] = rows[..., q * QUARTER : (q + 1) * QUARTER]
+        return 0
+
+    lax.fori_loop(0, 8, body, 0)
 
 
 class Scatter:
-    def __init__(self, place, copies, spec, left, right, lefts, rights, parts, bufs, final, out):
+    def __init__(self, place, copies, unit, parts, bufs, final, out):
         self.place, self.copies = place, copies
-        self.rows, self.columns, self.order = spec[0], spec[1], spec[2][::-1]
-        self.left, self.right, self.lefts, self.rights = left, right, lefts, rights
+        _, self.row, self.column, order = unit
+        self.order = order[::-1]
         self.parts, self.bufs, self.final, self.out = parts, bufs, final, out
         self.done = []
-
-    def begin(self):
-        place, copies, quarter = self.place, self.copies, self.columns // 4
-        self.inputs = [copies.send(self.left, self.lefts.at[pl.ds(HALF, HALF)], place.other_core())]
-        for q in range(2):
-            start = pl.multiple_of((1 - place.core) * 2 * quarter + q * quarter, 128)
-            self.inputs.append(
-                copies.send(
-                    self.right.at[:, pl.ds(start, quarter)],
-                    self.rights.at[q, pl.ds(HALF, HALF)],
-                    place.other_core(),
-                )
-            )
-        self.own = [copies.move(self.left, self.lefts.at[pl.ds(0, HALF)])]
-        for q in range(2):
-            start = pl.multiple_of(place.core * 2 * quarter + q * quarter, 128)
-            self.own.append(
-                copies.move(self.right.at[:, pl.ds(start, quarter)], self.rights.at[q, pl.ds(0, HALF)])
-            )
-
-    def make(self):
-        for copy in self.inputs:
-            copy.wait_recv()
-        for copy in self.own:
-            copy.wait()
-        rows, quarter = self.rows, self.columns // 4
-        chunk = 8 * rows
-
-        def body(i, _):
-            q, z_lo, x = lax.div(i, 8), lax.rem(lax.div(i, 4), 2), lax.rem(i, 4)
-            start = pl.multiple_of(lax.rem(i, 8) * chunk, 128)
-            made = lax.dot_general(
-                self.lefts[:, pl.ds(start, chunk)],
-                self.rights[q],
-                (((0,), (0,)), ((), ())),
-                preferred_element_type=F32,
-            )
-            self.parts[2 * q + z_lo, x] = made.astype(BF16).reshape(4, 2, rows, quarter)
-            return 0
-
-        lax.fori_loop(0, 16, body, 0)
 
     def sel(self, axis, index):
         at = {a: self.place.at[a] if a in self.done else None for a in "xyz"}
@@ -449,26 +486,37 @@
         free = [i for i, s in enumerate(sel) if s is None]
 
         def body(step, _):
-            where, inner = list(sel), []
-            for i in reversed(free):
-                where[i] = lax.rem(step, 4)
-                inner.insert(0, where[i])
-                step = lax.div(step, 4)
-            total = self.parts[(*where, core)].astype(F32)
+            where = [slice(None) if s is None else s for s in sel]
+            inner = (slice(None),) * len(free)
+            if len(free) == 2:
+                where[free[0]], inner = step, (step, slice(None))
+            if core is not None:
+                where.append(core)
+            total = self.parts[tuple(where)].astype(F32)
             for buf in bufs:
-                total += buf[tuple(inner)].astype(F32)
-            self.parts[(*where, core)] = total.astype(BF16)
+                total += buf[inner].astype(F32)
+            self.parts[tuple(where)] = total.astype(BF16)
             return 0
 
-        if free:
-            lax.fori_loop(0, 4 ** len(free), body, 0)
+        if len(free) == 2:
+            lax.fori_loop(0, 4, body, 0)
         else:
-            body(jnp.int32(0), 0)
+            body(0, 0)
 
     def start(self, phase):
         axis, place = self.order[phase], self.place
         buf = self.bufs[phase]
         send = self.copies.send
+        if phase > 0:
+            self.direct = [
+                send(
+                    self.block(axis, place.step(axis, distance), slice(None)),
+                    buf.at[distance - 1],
+                    place.along(axis, distance),
+                )
+                for distance in (1, 3, 2)
+            ]
+            return
         up, down = place.along(axis, 1), place.along(axis, -1)
         far = place.step(axis, 2)
         self.far = {
@@ -480,9 +528,9 @@
             -1: send(self.block(axis, place.step(axis, -1), 0), buf.at[2], down),
         }
 
-    def forward(self, phase):
-        axis, place = self.order[phase], self.place
-        buf = self.bufs[phase]
+    def forward(self):
+        axis, place = self.order[0], self.place
+        buf = self.bufs[0]
         self.near = {}
         for way, core in ((1, 0), (-1, 1)):
             self.far[way].wait_recv()
@@ -495,10 +543,15 @@
     def finish(self, phase):
         axis, place = self.order[phase], self.place
         buf = self.bufs[phase]
-        for way, core in ((1, 0), (-1, 1)):
-            self.raw[-way].wait_recv()
-            self.near[way].wait_recv()
-            self.add(axis, place.at[axis], core, [buf.at[2 + core], buf.at[4 + core]])
+        if phase > 0:
+            for copy in self.direct:
+                copy.wait_recv()
+            self.add(axis, place.at[axis], None, [buf.at[slot] for slot in range(3)])
+        else:
+            for way, core in ((1, 0), (-1, 1)):
+                self.raw[-way].wait_recv()
+                self.near[way].wait_recv()
+                self.add(axis, place.at[axis], core, [buf.at[2 + core], buf.at[4 + core]])
         self.done.append(axis)
 
     def share(self):
@@ -519,12 +572,59 @@
         for copy in self.shared:
             copy.wait_recv()
         self.kept.wait()
-        quarter = self.columns // 4
         for slot in range(4):
-            self.out[:, slot * quarter : (slot + 1) * quarter] = self.final[slot].astype(F32)
+            start = self.column + slot * QUARTER
+            self.out[self.row : self.row + 16, start : start + QUARTER] = self.final[slot].astype(F32)
 
 
 LEFTS = (D, D, D, FF)
+BLOCKS = (3, 1, 4, 1)
+
+
+def attention_back(projected, grad_att, grad_proj, pairs):
+    low = lax.broadcasted_iota(jnp.int32, (1, 128), 1) < HEAD
+
+    def body(pair, _):
+        def columns(part):
+            return pl.ds(pl.multiple_of(part * D + pair * 128, 128), 128)
+
+        query = projected[:, columns(0)] * jnp.asarray(HEAD ** (-0.5), BF16)
+        key = projected[:, columns(1)]
+        value = projected[:, columns(2)]
+        grad = grad_att[:, columns(0)]
+        zero = jnp.zeros((), BF16)
+        pieces = []
+        for mine in (low, jnp.logical_not(low)):
+            scores = lax.dot_general(
+                jnp.where(mine, query, zero), key, NT, preferred_element_type=F32
+            )
+            terms = jnp.exp(scores - jnp.max(scores, -1, keepdims=True))
+            probs = terms * (1.0 / jnp.sum(terms, -1, keepdims=True))
+            grad_probs = lax.dot_general(
+                jnp.where(mine, grad, zero), value, NT, preferred_element_type=F32
+            )
+            inner = jnp.sum(probs * grad_probs, -1, keepdims=True)
+            grad_scores = (probs * (grad_probs - inner)).astype(BF16)
+            rounded = probs.astype(BF16)
+            pieces.append(
+                (
+                    jnp.dot(grad_scores[:HALF], key, preferred_element_type=F32) * HEAD ** (-0.5),
+                    lax.dot_general(grad_scores[:, :HALF], query, TN, preferred_element_type=F32),
+                    lax.dot_general(rounded[:, :HALF], grad, TN, preferred_element_type=F32),
+                )
+            )
+        for part in range(3):
+            both = jnp.where(low, pieces[0][part], pieces[1][part])
+            grad_proj[:, columns(part)] = both.astype(BF16)
+        return 0
+
+    lax.fori_loop(*pairs, body, 0)
+
+
+def normal_parts(values):
+    centre = values - jnp.mean(values, -1, keepdims=True)
+    scale = lax.rsqrt(jnp.mean(centre * centre, -1, keepdims=True) + EPSILON)
+    return centre * scale, scale
 
 
 def leave_kernel(*refs):
@@ -534,89 +634,189 @@
         taken, refs[:count] = refs[:count], []
         return taken
 
-    lefts_in, rights_in = take(4), take(4)
-    (vector,) = take(1)
+    lefts_in, rights_in = take(4), take(3)
+    w_attend, projected, own_att, tokens, grad_middle, scale_one, sums = take(7)
     outs = take(4)
-    (whole,) = take(1)
-    lefts, rights, parts = take(4), take(4), take(4)
-    bufs = [take(3) for _ in range(4)]
-    finals = take(4)
-    (vector_got,) = take(1)
+    whole, tokens_grad = take(2)
+    lefts, rights, parts = take(4), take(4), take(12)
+    bufs = [take(3) for _ in range(12)]
+    finals = take(12)
+    weight, both_att, grad_proj, vector, vector_sent, vector_got = take(6)
     send_sems, recv_sems, local_sems = refs
     place = Place()
     copies = Copies(send_sems, recv_sems, local_sems)
     far = place.step("z", 2)
+    rights_in = [grad_proj] + rights_in
     greet(place.everyone() + [place.device(z=far, core=1 - place.core)])
     scatters = [
-        Scatter(place, copies, WEIGHTS[i], lefts_in[i], rights_in[i], lefts[i], rights[i], parts[i], bufs[i], finals[i], outs[i])
-        for i in (3, 2, 0, 1)
+        Scatter(place, copies, UNITS[i], parts[i], bufs[i], finals[i], outs[UNITS[i][0]]) for i in range(12)
     ]
-    for scatter in scatters:
-        scatter.begin()
-    vector_copy = copies.send(vector, vector_got, place.along("z", 2))
-    for scatter in scatters:
-        scatter.make()
-        scatter.start(0)
+
+    def of(weight_index, wave=None):
+        return [
+            scatters[i]
+            for i in range(12)
+            if UNITS[i][0] == weight_index and wave in (None, i // 3)
+        ]
+
+    def start(wave, phase):
+        for scatter in scatters[3 * wave : 3 * wave + 3]:
+            scatter.start(phase)
+
+    def forward(wave):
+        for scatter in scatters[3 * wave : 3 * wave + 3]:
+            scatter.forward()
+
+    def finish(wave, phase):
+        for scatter in scatters[3 * wave : 3 * wave + 3]:
+            scatter.finish(phase)
+
+    def share(wave):
+        for scatter in scatters[3 * wave : 3 * wave + 3]:
+            scatter.share()
+
+    def store(wave):
+        for scatter in scatters[3 * wave : 3 * wave + 3]:
+            scatter.store()
+
+    pairs = {}
+    for i in (3, 2, 1):
+        pairs[i] = [
+            Pair(place, copies, lefts_in[i], lefts[i]),
+            Pair(place, copies, rights_in[i], rights[i], BLOCKS[i]),
+        ]
+    att_copy = copies.send(own_att, both_att.at[pl.ds(HALF, HALF)], place.along("z", 2))
+    late = [Pair(place, copies, lefts_in[0], lefts[0])]
+    weight_copy = copies.move(w_attend, weight)
+    both_att[:HALF] = own_att[...]
+
+    def meet(pair):
+        for half in pair:
+            half.wait()
+
+    meet(pairs[3])
+    make_tall_parts(lefts[3], rights[3], of(3))
+    start(3, 0)
+    meet(pairs[2])
+    make_parts(lefts[2], rights[2], of(2, 2))
+    start(2, 0)
+    meet(pairs[1])
+    make_parts(lefts[2], rights[2], of(2, 1))
+    make_parts(lefts[1], rights[1], of(1))
+    start(1, 0)
+
+    att_copy.wait_recv()
+    attention_back(projected, both_att, grad_proj, (0, HEADS // 4))
+    forward(3)
+    attention_back(projected, both_att, grad_proj, (HEADS // 4, HEADS // 2))
+    late.append(Pair(place, copies, grad_proj, rights[0], BLOCKS[0]))
+    forward(2)
+    forward(1)
+    finish(3, 0)
+    start(3, 1)
+    meet(late)
+    make_parts(lefts[0], rights[0], of(0))
+    start(0, 0)
+
+    weight_copy.wait()
+    normal, scale = normal_parts(tokens[...].astype(F32))
+    grad_first = jnp.concatenate(
+        [
+            lax.dot_general(
+                grad_proj[...], weight[start : start + 256], NT, preferred_element_type=F32
+            )
+            for start in range(0, D, 256)
+        ],
+        1,
+    )
+    back = grad_first * (1.0 + scale_one[...])
+    tokens_grad[...] = grad_middle[...] + scale * (
+        back
+        - jnp.mean(back, -1, keepdims=True)
+        - normal * jnp.mean(back * normal, -1, keepdims=True)
+    )
+    vector[...] = sums[...]
+    for place_of, total in ((0, grad_first), (8, grad_first * normal)):
+        total = jnp.sum(total, 0, keepdims=True)
+        for row in range(8):
+            vector[place_of + row : place_of + row + 1, :] = total[:, row * 128 : (row + 1) * 128]
+    vector_sent[...] = vector[...].astype(BF16)
+    vector_copy = copies.send(vector_sent, vector_got, place.along("z", 2))
+
+    finish(2, 0)
+    start(2, 1)
+    finish(3, 1)
+    start(3, 2)
+    forward(0)
+    finish(1, 0)
+    start(1, 1)
     vector_copy.wait_recv()
     whole[place.z_lo, place.at["x"], place.at["y"], place.core] = (
-        vector[...].astype(F32) + vector_got[...].astype(F32)
+        vector_sent[...].astype(F32) + vector_got[...].astype(F32)
     ).astype(BF16)
     gather = SmallGather(place, copies, whole)
     gather.stage(0)
-    for scatter in scatters:
-        scatter.forward(0)
+    finish(2, 1)
+    start(2, 2)
+    finish(3, 2)
+    share(3)
     gather.stage(1)
-    for scatter in scatters:
-        scatter.finish(0)
-        scatter.start(1)
+    finish(1, 1)
+    start(1, 2)
+    finish(0, 0)
+    start(0, 1)
     gather.stage(2)
-    for scatter in scatters:
-        scatter.forward(1)
+    finish(2, 2)
+    share(2)
+    finish(1, 2)
+    share(1)
+    store(3)
+    finish(0, 1)
+    start(0, 2)
     gather.stage(3)
-    for scatter in scatters:
-        scatter.finish(1)
-        scatter.start(2)
-    for scatter in scatters:
-        scatter.forward(2)
-    for scatter in scatters:
-        scatter.finish(2)
-        scatter.share()
+    store(2)
+    finish(0, 2)
+    share(0)
+    store(1)
     gather.arrive()
-    for scatter in scatters:
-        scatter.store()
+    store(0)
     copies.drain()
 
 
-def buffer_shapes(rows, columns, order):
-    shapes = []
-    for left in (2, 1, 0):
-        shapes.append(pltpu.VMEM((6,) + (4,) * left + (rows, columns // 4), BF16))
-    return shapes
-
-
-def leave(lefts, rights, vector):
+def buffer_shapes():
+    shapes = [(6, 4, 4, 16, QUARTER), (3, 4, 2, 16, QUARTER), (3, 2, 16, QUARTER)]
+    return [pltpu.VMEM(shape, BF16) for shape in shapes]
+
+
+def leave(lefts, rights, w_attend, projected, grad_att, tokens, grad_middle, scale_one, sums):
     anywhere = pl.BlockSpec(memory_space=pl.ANY)
     inside = pl.BlockSpec(memory_space=pltpu.VMEM)
     scratch = [pltpu.VMEM((SEQ, width), BF16) for width in LEFTS]
-    scratch += [pltpu.VMEM((2, SEQ, columns // 4), BF16) for _, columns, _ in WEIGHTS]
-    scratch += [pltpu.VMEM((4, 4, 4, 2, rows, columns // 4), BF16) for rows, columns, _ in WEIGHTS]
-    for spec in WEIGHTS:
-        scratch += buffer_shapes(*spec)
-    scratch += [pltpu.VMEM((4, rows, columns // 4), BF16) for rows, columns, _ in WEIGHTS]
-    scratch += [pltpu.VMEM(vector.shape, BF16)]
-    scratch += copy_scratch(4 * 24 + 9, 16)
+    scratch += [pltpu.VMEM((blocks, SEQ, 2 * QUARTER), BF16) for blocks in BLOCKS]
+    scratch += [pltpu.VMEM((4, 4, 4, 2, 16, QUARTER), BF16)] * 12
+    scratch += buffer_shapes() * 12
+    scratch += [pltpu.VMEM((4, 16, QUARTER), BF16)] * 12
+    scratch += [
+        pltpu.VMEM((D, 3 * D), BF16),
+        pltpu.VMEM((SEQ, D), BF16),
+        pltpu.VMEM((HALF, 3 * D), BF16),
+        pltpu.VMEM(sums.shape, F32),
+        pltpu.VMEM(sums.shape, BF16),
+        pltpu.VMEM(sums.shape, BF16),
+    ]
+    scratch += copy_scratch(12 * 15 + 4 + 9 + 10, 4 + 9 + 1 + 12)
     return pl.pallas_call(
         leave_kernel,
-        out_shape=[jax.ShapeDtypeStruct((rows, columns), F32) for rows, columns, _ in WEIGHTS]
-        + [jax.ShapeDtypeStruct((2, 4, 4, 2) + vector.shape, BF16)],
-        in_specs=[anywhere] * 8 + [inside],
-        out_specs=[inside] * 5,
+        out_shape=[jax.ShapeDtypeStruct((rows, columns), F32) for rows, columns in WEIGHTS]
+        + [jax.ShapeDtypeStruct((2, 4, 4, 2) + sums.shape, BF16), jax.ShapeDtypeStruct((HALF, D), F32)],
+        in_specs=[anywhere] * 8 + [inside] * 6,
+        out_specs=[inside] * 6,
         scratch_shapes=scratch,
         compiler_params=pltpu.CompilerParams(
-            collective_id=3, has_side_effects=True, vmem_limit_bytes=56 * 2**20
+            collective_id=3, has_side_effects=True, vmem_limit_bytes=58 * 2**20
         ),
         name="leave",
-    )(*lefts, *rights, vector)
+    )(*lefts, *rights, w_attend, projected, grad_att, tokens, grad_middle, scale_one, sums)
 
 
 def normalize(values):
@@ -672,7 +872,7 @@
 ):
     shard_index = lax.axis_index("fsdp")
     token_half = lax.axis_index("ctx")
-    all_labels, all_steps = gather_ids(labels, timesteps)
+    all_labels, all_steps, b_hidden = gather_ids(labels, timesteps, hidden_offset[0])
     onehot = all_labels[:, None] == jnp.arange(CLASSES, dtype=jnp.int32)[None, :]
     sinus_rows = sinusoid(all_steps).astype(BF16)
     cond_cols = jnp.dot(
@@ -692,7 +892,6 @@
         tokens[0],
         partial_mod,
     )
-    b_hidden = lax.all_gather(hidden_offset[0], "fsdp", axis=0, tiled=True)
     shift_one, scale_one, gate_one, shift_two, scale_two, gate_two = [modulation[i] for i in range(6)]
 
     hidden = tokens[0].astype(F32)
@@ -701,15 +900,14 @@
     first_in = both_first[:HALF]
     projected = jnp.dot(both_first, w_attend, preferred_element_type=F32).astype(BF16)
     query_rows, key_rows, value_rows = projected[:, :D], projected[:, D : 2 * D], projected[:, 2 * D :]
-    scores = attend_scores(query_rows, key_rows)
+    scores = attend_scores(query_rows[:HALF], key_rows)
     top_score = jnp.max(scores, -1, keepdims=True)
     exp_terms = jnp.exp(scores - top_score)
     totals = jnp.sum(exp_terms, -1, keepdims=True)
-    softmaxed = exp_terms / totals
-    rounded_probs = softmaxed.astype(BF16)
+    rounded_probs = (exp_terms / totals).astype(BF16)
     attended = (
         jnp.einsum(
-            "hqk,khd->qhd", rounded_probs[:, :HALF], head_split(value_rows), preferred_element_type=F32
+            "hqk,khd->qhd", rounded_probs, head_split(value_rows), preferred_element_type=F32
         )
         .reshape(-1, D)
         .astype(BF16)
@@ -717,7 +915,7 @@
     branch_one = jnp.dot(attended, w_output, preferred_element_type=F32)
     middle = hidden + gate_one * branch_one
     second_in = modulated(middle, shift_two, scale_two).astype(BF16)
-    pre_act = jnp.dot(second_in, w_expand, preferred_element_type=F32) + b_hidden.astype(F32)
+    pre_act = jnp.dot(second_in, w_expand, preferred_element_type=F32) + b_hidden
     activated = gelu_tanh(pre_act).astype(BF16)
     branch_two = jnp.dot(activated, w_contract, preferred_element_type=F32)
     result = (middle + gate_two * branch_two).astype(BF16)[None]
@@ -736,45 +934,26 @@
     grad_one = (grad_middle * gate_one).astype(BF16)
     gate_one_grad = jnp.sum(grad_middle * branch_one, 0)
     grad_att = jnp.einsum("te,de->td", grad_one, w_output, preferred_element_type=F32).astype(BF16)
-    both_att = jnp.concatenate([grad_att, swap(grad_att)], 0)
-    grad_heads = head_split(both_att)
-    grad_probs = jnp.einsum(
-        "qhd,khd->hqk", grad_heads, head_split(value_rows), preferred_element_type=F32
-    )
-    grad_scores = (
-        softmaxed * (grad_probs - jnp.sum(softmaxed * grad_probs, -1, keepdims=True))
-    ).astype(BF16)
-    grad_query = jnp.einsum(
-        "hqk,khd->qhd", grad_scores[:, :HALF], head_split(key_rows), preferred_element_type=F32
-    ) * HEAD ** (-0.5)
-    grad_key = jnp.einsum(
-        "hqk,qhd->khd", grad_scores[:, :, :HALF], head_split(query_rows), preferred_element_type=F32
-    ) * HEAD ** (-0.5)
-    grad_value = jnp.einsum(
-        "hqk,qhd->khd", rounded_probs[:, :, :HALF], grad_heads, preferred_element_type=F32
-    )
-    grad_proj = jnp.concatenate(
-        [part.reshape(-1, D).astype(BF16) for part in (grad_query, grad_key, grad_value)], 1
-    )
-    grad_first = jnp.einsum("te,de->td", grad_proj, w_attend, preferred_element_type=F32)
-    _, first_pull = jax.vjp(modulated, hidden, shift_one, scale_one)
-    grad_input, shift_one_grad, scale_one_grad = first_pull(grad_first)
-    tokens_grad = (grad_middle + grad_input)[None]
-
-    vector = jnp.concatenate(
+    sums = jnp.concatenate(
         [
-            shift_one_grad,
-            scale_one_grad,
+            jnp.zeros((2 * D,), F32),
             gate_one_grad,
             shift_two_grad,
             scale_two_grad,
             gate_two_grad,
             hidden_term,
         ]
-    )
-    vector = vector.astype(BF16).reshape(80, 128)
-    attend_grad, output_grad, expand_grad, contract_grad, all_vectors = leave(
-        (first_in, attended, second_in, activated), (grad_proj, grad_one, grad_pre, grad_two), vector
+    ).reshape(80, 128)
+    attend_grad, output_grad, expand_grad, contract_grad, all_vectors, tokens_grad = leave(
+        (first_in, attended, second_in, activated),
+        (grad_one, grad_pre, grad_two),
+        w_attend,
+        projected,
+        grad_att,
+        tokens[0],
+        grad_middle,
+        scale_one[None],
+        sums,
     )
     all_vectors = all_vectors.reshape(64, 80 * 128)
     all_mod = all_vectors[:, : 6 * D]
@@ -790,7 +969,7 @@
     time_grad = jnp.einsum("bf,bd->fd", sinus_rows.astype(F32), grad_cond, precision=HIGHEST)
     return (
         result,
-        tokens_grad,
+        tokens_grad[None],
         table_grad,
         time_grad,
         modulate_grad[None],

time: 418 us -> 230 us (0.55)
  blocking collectives: 142 us -> 0 us
  matrix products: 50.4 us -> 31.4 us
  Pallas kernels: 191 us -> 173 us
  local copies, waits for them, and re-layouts: 22.2 us -> 17.1 us
    unnamed x1 -> x0, blocking collectives: 142 us -> none
    pallas_call x1 -> x0, Pallas kernels: 11.2 us -> none  [swap(): pl.pallas_call(swap_kernel, out_shape=jax.ShapeDtypeStruct(own.shape, own...]
    pallas_call x1, Pallas kernels: 78.5 us -> 69.6 us  [enter(): pl.pallas_call(enter_kernel, out_shape=shapes, in_specs=[anywhere] * 5 +...]
    sub x1 -> x0, matrix products: 6.95 us -> none  [per_device(): grad_probs - jnp.sum(softmaxed * grad_probs, -1, keepdims=True)]
    dot_general x6 -> x2, matrix products: 15.7 us -> 9.34 us  [the longest x1 7.01 us: per_device(): jnp.dot(second_in, w_expand, preferred_element_type=F32) + b_hidden]
    pallas_call x1, Pallas kernels: 16.2 us -> 20.8 us  [gather_ids(): pl.pallas_call(ids_kernel, out_shape=jax.ShapeDtypeStruct((2, 4, 4, 2, 8,...]
    unnamed x79 -> x63, local copies, waits for them, and re-layouts: 11.4 us -> 7.11 us
where the time goes in v2:
time: 230 us; the launch traced here: 229 us
  Pallas kernels  173 us (75%)
  matrix products  31.4 us (14%)
  local copies, waits for them, and re-layouts  17.1 us (7%)
  other arithmetic  5.73 us (2%)
  between operations  2.49 us (1%)
    pallas_call x1, Pallas kernels, leave(): pl.pallas_call(leave_kernel, out_shape=[jax.ShapeDtypeStruct((rows, colum...  82.4 us
    pallas_call x1, Pallas kernels, enter(): pl.pallas_call(enter_kernel, out_shape=shapes, in_specs=[anywhere] * 5 +...  69.6 us
    pallas_call x1, Pallas kernels, gather_ids(): pl.pallas_call(ids_kernel, out_shape=jax.ShapeDtypeStruct((2, 4, 4, 2, 8,...  20.8 us
    unnamed x63, local copies, waits for them, and re-layouts  7.11 us
    dot_general x1, matrix products, per_device(): jnp.dot(second_in, w_expand, preferred_element_type=F32) + b_hidden  7.01 us
    dot_general x1, matrix products, per_device(): jnp.einsum('td,fd->tf', grad_two, w_contract, preferred_element_type=F32)  5.71 us

profile of v2, /device:TPU:1, one launch (start us, length us, event | category | flops | bytes accessed | tf_op | source)
XLA Modules:
  0.0 229.5 jit_solution(7778080776568666202)
XLA Ops:
  0.6 0.0 copy-start
  0.7 0.0 copy-start.1
  2.1 0.7 pad_convert_fusion
  2.8 0.6 pad_maximum_fusion.4.own
  3.4 0.7 convert_dynamic-update-slice_fusion
  4.1 20.8 %gather_ids.1 = f32[2,4,4,2,8,128]{5,4,3,2,1,0:T(8,128)} custom-call(f32[8,128]{1,0:T(8,128)} %pad_maximum_fusion.4.own), custom_call_target="tpu_custom_call" | custom-call | tf_op jit(solution)/shard_map/gather_ids/pallas_call | solution.py:395
  24.9 1.0 slice_reduce_fusion
  26.0 1.0 slice.68
  26.9 0.1 copy.34
  27.0 0.1 add.150
  27.1 1.0 fusion.32
  28.1 0.2 fusion.40
  28.3 0.8 convolution_add_fusion.2
  29.1 0.0 copy-done
  29.1 0.4 fusion.10
  29.5 0.1 copy.35
  29.7 69.6 %enter.1 = (bf16[2,4,4,2,16,3072]{5,4,3,2,1,0:T(8,128)(2,1)S(1)}, bf16[2,4,4,2,16,1024]{5,4,3,2,1,0:T(8,128)(2,1)S(1)}, bf16[2,4,4,2,16,4096]{5,4,3,2,1,0:T(8,12...) custom-call(bf16[16,3072]{1,0:T(8,128)(2,1)S(1)} %bitcast.128, ...), custom_call_target="tpu_custom_call" | custom-call | tf_op jit(solution)/shard_map/enter/pallas_call | solution.py:324
  99.3 0.0 copy-start.2
  99.3 0.0 copy-start.3
  99.3 0.1 convert_reduce_fusion.1
  99.5 0.3 fusion.13
  99.8 0.9 fusion.58
  100.7 0.3 fusion.16
  101.0 1.3 slice.73.refs_0_
  102.3 1.8 convolution_convert_fusion.refs_8_
  104.1 0.0 copy-done.2
  104.1 0.4 copy-done.3
  104.5 1.2 copy-done.9
  105.8 0.2 copy.31
  106.0 2.3 fusion.57
  108.2 1.2 copy.32
  109.5 2.0 copy.30
  111.5 2.0 fusion.59
  113.5 2.3 %convolution_convert_fusion.2 = bf16[16,64,128]{2,1,0:T(8,128)(2,1)S(1)} fusion(bf16[256,16,64]{0,2,1:T(8,128)(2,1)} %bitcast.144, f32[16,128,256]{2,1,0:T(8,128)} %get-tuple-element.63, f32[16,128]{1,0:T(8,128)S(1)} %get-tuple-element.62), kind=kOutput, calls=%fused_computation.28 | convolution fusion | flops 68288512 | bytes 2891776 | tf_op jit(solution)/shard_map/hqk,khd->qhd/dot_general | solution.py:909
  115.9 0.9 copy.33.refs_1_
  116.7 0.5 fusion.56
  117.3 0.2 multiply_reduce_fusion.4
  117.5 0.2 add_convert_fusion.1.refs_2_
  117.7 0.0 slice-start.3
  117.7 0.0 copy-start.13
  117.7 0.0 slice-start
  117.7 7.0 %multiply_convert_fusion = (bf16[128,4096]{1,0:T(8,128)(2,1)S(1)}, f32[128,4096]{1,0:T(8,128)}) fusion(f32[4096]{0:T(1024)S(1)} %add.150, bf16[128,1024]{1,0:T(8,128)(2,1)S(1)} %add_convert_fusion.1.refs_2_, bf16[1024,4096]{1,0:T(8,128)(2,1)} %bitcast.119), kind=kOutput, calls=%fused_computation.16 | convolution fusion | flops 1078984704 | bytes 11812864 | tf_op jit(solution)/shard_map/dot_general | solution.py:918
  124.8 0.0 slice-start.1
  124.8 5.7 %convert_reduce_fusion = (f32[4096]{0:T(1024)S(1)}, bf16[128,4096]{1,0:T(8,128)(2,1)S(1)}) fusion(f32[128,4096]{1,0:T(8,128)} %get-tuple-element.66, bf16[4096,1024]{1,0:T(8,128)(2,1)S(1)} %bitcast.132, bf16[1,128,1024]{2,1,0:T(8,128)(2,1)S(1)} %copy-done.13, f32[1024]{0:T(1024)S(1)} %get-tuple-element.55), kind=kOutput, calls=%fused_computation.15 | convolution fusion | flops 1085665280 | bytes 11816960 | tf_op jit(solution)/shard_map/td,fd->tf/dot_general | solution.py:926
  130.5 3.0 %multiply_reduce_fusion.1 = (f32[1024]{0:T(1024)S(1)}, f32[128]{0:T(128)S(1)}, f32[1024]{0:T(1024)S(1)}, f32[128,1024]{1,0:T(8,128)S(1)}) fusion(f32[128,1024]{1,0:T(8,128)S(1)} %get-tuple-element.43, f32[128]{0:T(128)S(1)} %fusion.48, f32[128]{0:T(128)S(1)} %broadcast_multiply_fusion.1, f32[1024]{0:T(1024)S(1)} %get-tuple-element.54, ...), kind=kOutput, calls=%fused_computation.45 | convolution fusion | flops 1074788224 | bytes 10499584 | tf_op jit(solution)/shard_map/tf,df->td/dot_general | solution.py:930
  133.6 2.2 fusion.22
  135.8 0.2 multiply_reduce_fusion.2
  136.0 0.0 copy-start.10
  136.0 0.0 copy-start.20
  136.1 1.5 convolution_convert_fusion.1.refs_9_
  137.7 82.4 %leave.1 = (f32[16,3072]{1,0:T(8,128)}, f32[16,1024]{1,0:T(8,128)}, f32[16,4096]{1,0:T(8,128)}, f32[64,1024]{1,0:T(8,128)}, bf16[2,4,4,2,80,128]{5,4,3,2,1,0:T(8,128)(2,1)}, /*index=5*/f32[128,1024]{1,0:T(8,128)}) custom-call(bf16[128,1024]{1,0:T(8,128)(2,1)} %slice.73.refs_0_, bf16[128,1024]{1,0:T(8,128)(2,1)} %copy.33.refs_1_, ...), custom_call_target="tpu_custom_call" | custom-call | tf_op jit(solution)/shard_map/leave/pallas_call | solution.py:808
  220.0 1.7 copy.38
  221.7 0.6 convert_reduce_fusion.2
  222.3 0.3 fusion.44
  222.6 0.8 fusion.42
  223.4 0.9 fusion.31
  224.3 1.0 convolution_bitcast_fusion
  225.3 0.1 slice.74
  225.3 0.6 convert_reduce_fusion.3
  225.9 0.8 copy.52
  226.7 0.7 copy.53
  227.4 0.6 copy.54
  228.0 0.7 copy.55
  228.7 0.7 copy.56
  (58 shorter events, 0.2 us)
Async XLA Ops:
  0.6 28.5 %copy-start = (bf16[1,16,6144]{2,1,0:T(8,128)(2,1)S(1)}, bf16[1,16,6144]{2,1,0:T(8,128)(2,1)}, u32[]{:S(2)}) copy-start(bf16[1,16,6144]{2,1,0:T(8,128)(2,1)} %param.19) | copy-start | bytes 589828
  0.7 29.0 %copy-start.1 = (bf16[1,128,1024]{2,1,0:T(8,128)(2,1)S(1)}, bf16[1,128,1024]{2,1,0:T(8,128)(2,1)}, u32[]{:S(2)}) copy-start(bf16[1,128,1024]{2,1,0:T(8,128)(2,1)} %param.13) | copy-start | bytes 786436
  0.7 29.0 %copy-start.5 = (bf16[1,64,1024]{2,1,0:T(8,128)(2,1)S(1)}, bf16[1,64,1024]{2,1,0:T(8,128)(2,1)}, u32[]{:S(2)}) copy-start(bf16[1,64,1024]{2,1,0:T(8,128)(2,1)} %param.25) | copy-start | bytes 393220
  0.7 29.0 %copy-start.4 = (bf16[1,16,4096]{2,1,0:T(8,128)(2,1)S(1)}, bf16[1,16,4096]{2,1,0:T(8,128)(2,1)}, u32[]{:S(2)}) copy-start(bf16[1,16,4096]{2,1,0:T(8,128)(2,1)} %param.23) | copy-start | bytes 393220
  0.7 29.0 %copy-start.7 = (bf16[1,16,1024]{2,1,0:T(8,128)(2,1)S(1)}, bf16[1,16,1024]{2,1,0:T(8,128)(2,1)}, u32[]{:S(2)}) copy-start(bf16[1,16,1024]{2,1,0:T(8,128)(2,1)} %param.22) | copy-start | bytes 98308
  0.7 29.0 %copy-start.6 = (bf16[1,16,3072]{2,1,0:T(8,128)(2,1)S(1)}, bf16[1,16,3072]{2,1,0:T(8,128)(2,1)}, u32[]{:S(2)}) copy-start(bf16[1,16,3072]{2,1,0:T(8,128)(2,1)} %param.21) | copy-start | bytes 294916
  99.3 4.8 %copy-start.2 = (bf16[2,4,4,2,16,4096]{5,4,3,2,1,0:T(8,128)(2,1)}, bf16[2,4,4,2,16,4096]{5,4,3,2,1,0:T(8,128)(2,1)S(1)}, u32[]{:S(2)}) copy-start(bf16[2,4,4,2,16,4096]{5,4,3,2,1,0:T(8,128)(2,1)S(1)} %get-tuple-element.27) | copy-start | bytes 25165828
  99.3 5.2 %copy-start.3 = (bf16[2,4,4,2,16,3072]{5,4,3,2,1,0:T(8,128)(2,1)}, bf16[2,4,4,2,16,3072]{5,4,3,2,1,0:T(8,128)(2,1)S(1)}, u32[]{:S(2)}) copy-start(bf16[2,4,4,2,16,3072]{5,4,3,2,1,0:T(8,128)(2,1)S(1)} %get-tuple-element.25) | copy-start | bytes 18874372
  104.5 1.2 copy-start.9
  116.7 8.0 %slice-start.2 = ((s8[8388608]{0:T(1024)(128)(4,1)}), s8[4194304]{0:T(1024)(128)(4,1)S(1)}, s32[]{:S(2)}) async-start(s8[8388608]{0:T(1024)(128)(4,1)} %bitcast.130), calls=%async_computation.2 | async-start | bytes 8388608
  117.7 7.1 %copy-start.14 = (bf16[128,1024]{1,0:T(8,128)(2,1)}, bf16[128,1024]{1,0:T(8,128)(2,1)S(1)}, u32[]{:S(2)}) copy-start(bf16[128,1024]{1,0:T(8,128)(2,1)S(1)} %add_convert_fusion.1.refs_2_) | copy-start | bytes 786436
  117.7 7.1 %slice-start.3 = ((s8[8388608]{0:T(1024)(128)(4,1)}), s8[4194304]{0:T(1024)(128)(4,1)S(1)}, s32[]{:S(2)}) async-start(s8[8388608]{0:T(1024)(128)(4,1)} %bitcast.130), calls=%async_computation.3 | async-start | bytes 8388608
  117.7 7.0 %copy-start.13 = (bf16[1,128,1024]{2,1,0:T(8,128)(2,1)S(1)}, bf16[1,128,1024]{2,1,0:T(8,128)(2,1)}, u32[]{:S(2)}) copy-start(bf16[1,128,1024]{2,1,0:T(8,128)(2,1)} %param.16) | copy-start | bytes 786436
  117.7 12.8 %slice-start = ((s8[8388608]{0:T(1024)(128)(4,1)}), s8[4194304]{0:T(1024)(128)(4,1)S(1)}, s32[]{:S(2)}) async-start(s8[8388608]{0:T(1024)(128)(4,1)} %bitcast.120), calls=%async_computation | async-start | bytes 8388608
  124.7 8.9 %copy-start.8 = (bf16[128,4096]{1,0:T(8,128)(2,1)}, bf16[128,4096]{1,0:T(8,128)(2,1)S(1)}, u32[]{:S(2)}) copy-start(bf16[128,4096]{1,0:T(8,128)(2,1)S(1)} %get-tuple-element.65.refs_3_) | copy-start | bytes 3145732
  124.8 5.7 %slice-start.1 = ((s8[8388608]{0:T(1024)(128)(4,1)}), s8[4194304]{0:T(1024)(128)(4,1)S(1)}, s32[]{:S(2)}) async-start(s8[8388608]{0:T(1024)(128)(4,1)} %bitcast.120), calls=%async_computation.1 | async-start | bytes 8388608
  130.5 3.1 %copy-start.11 = (bf16[128,4096]{1,0:T(8,128)(2,1)}, bf16[128,4096]{1,0:T(8,128)(2,1)S(1)}, u32[]{:S(2)}) copy-start(bf16[128,4096]{1,0:T(8,128)(2,1)S(1)} %get-tuple-element.69.refs_5_) | copy-start | bytes 3145732
  136.0 1.7 copy-start.10
  136.0 1.6 copy-start.20
  136.1 1.6 copy-start.12
  221.7 4.3 %copy-start.15 = (f32[128,1024]{1,0:T(8,128)S(1)}, f32[128,1024]{1,0:T(8,128)}, u32[]{:S(2)}) copy-start(f32[128,1024]{1,0:T(8,128)} %get-tuple-element.29) | copy-start | bytes 1572868
  222.6 4.1 %copy-start.18 = (f32[16,3072]{1,0:T(8,128)S(1)}, f32[16,3072]{1,0:T(8,128)}, u32[]{:S(2)}) copy-start(f32[16,3072]{1,0:T(8,128)} %get-tuple-element.31) | copy-start | bytes 589828
  224.3 3.1 %copy-start.19 = (f32[16,1024]{1,0:T(8,128)S(1)}, f32[16,1024]{1,0:T(8,128)}, u32[]{:S(2)}) copy-start(f32[16,1024]{1,0:T(8,128)} %get-tuple-element.32) | copy-start | bytes 196612
  224.3 3.8 %copy-start.17 = (f32[16,4096]{1,0:T(8,128)S(1)}, f32[16,4096]{1,0:T(8,128)}, u32[]{:S(2)}) copy-start(f32[16,4096]{1,0:T(8,128)} %get-tuple-element.33) | copy-start | bytes 786436
  225.3 3.5 %copy-start.16 = (f32[64,1024]{1,0:T(8,128)S(1)}, f32[64,1024]{1,0:T(8,128)}, u32[]{:S(2)}) copy-start(f32[64,1024]{1,0:T(8,128)} %get-tuple-element.34) | copy-start | bytes 786436

commit v3 on v2

--- a/solution.py
+++ b/solution.py
@@ -212,15 +212,109 @@
         self.done.append(axis)
 
 
+class SmallGather:
+    def __init__(self, place, copies, whole):
+        self.place, self.copies, self.whole = place, copies, whole
+        self.waiting = []
+
+    def arrive(self):
+        for copy in self.waiting:
+            copy.wait_recv()
+        self.waiting = []
+
+    def stage(self, which):
+        self.arrive()
+        place, whole, send = self.place, self.whole, self.copies.send
+        at, core = place.at, place.core
+        if which == 0:
+            piece = whole.at[core, place.z_lo, at["x"], at["y"]]
+            self.waiting = [send(piece, piece, place.along("y", d)) for d in (1, 2, 3)]
+        elif which == 1:
+            piece = whole.at[core, place.z_lo, at["x"]]
+            self.waiting = [send(piece, piece, place.along("x", d)) for d in (1, 2, 3)]
+        elif which == 2:
+            piece = whole.at[core, place.z_lo]
+            self.waiting = [send(piece, piece, place.other_z_lo())]
+        else:
+            piece = whole.at[core]
+            self.waiting = [send(piece, piece, place.other_core())]
+
+
+def conditioned(ids, class_table, time_weight, labels, sinus, bias):
+    def body(row, _):
+        core, z_lo = lax.div(row, 32), lax.rem(lax.div(row, 16), 2)
+        x, y = lax.rem(lax.div(row, 4), 4), lax.rem(row, 4)
+        labels[pl.ds(row, 1), :] = ids[core, z_lo, x, y, 1:2, :]
+        for half in range(2):
+            sinus[half, pl.ds(row, 1), :] = ids[core, z_lo, x, y, 2 + half : 3 + half, :]
+        return 0
+
+    def join(row, _):
+        z_lo, x, y = lax.div(row, 16), lax.rem(lax.div(row, 4), 4), lax.rem(row, 4)
+        bias[pl.ds(row, 1), :] = ids[0, z_lo, x, y, 0:1, :] + ids[1, z_lo, x, y, 0:1, :]
+        return 0
+
+    lax.fori_loop(0, 32, join, 0)
+
+    lax.fori_loop(0, 64, body, 0)
+    cond = jnp.zeros((64, 16), F32)
+    lane = lax.broadcasted_iota(jnp.int32, (64, 128), 1).astype(F32)
+    for start in range(0, CLASSES, 128):
+        width = min(128, CLASSES - start)
+        chosen = jnp.where(labels[...] == lane + float(start), 1.0, 0.0).astype(BF16)
+        cond += lax.dot_general(
+            chosen[:, :width], class_table[:, start : start + width], NT, preferred_element_type=F32
+        )
+    for half in range(2):
+        cond += lax.dot_general(
+            sinus[half].astype(BF16),
+            time_weight[:, half * 128 : half * 128 + 128],
+            NT,
+            preferred_element_type=F32,
+        )
+    return cond
+
+
+def attention_forward(projected, attended, pairs):
+    low = lax.broadcasted_iota(jnp.int32, (1, 128), 1) < HEAD
+
+    def body(pair, _):
+        def columns(part):
+            return pl.ds(pl.multiple_of(part * D + pair * 128, 128), 128)
+
+        query = projected[:HALF, columns(0)] * jnp.asarray(HEAD ** (-0.5), BF16)
+        key = projected[:, columns(1)]
+        value = projected[:, columns(2)]
+        pieces = []
+        for mine in (low, jnp.logical_not(low)):
+            scores = lax.dot_general(
+                jnp.where(mine, query, jnp.zeros((), BF16)), key, NT, preferred_element_type=F32
+            )
+            terms = jnp.exp(scores - jnp.max(scores, -1, keepdims=True))
+            probs = terms * (1.0 / jnp.sum(terms, -1, keepdims=True))
+            pieces.append(jnp.dot(probs.astype(BF16), value, preferred_element_type=F32))
+        attended[:, columns(0)] = jnp.where(low, *pieces).astype(BF16)
+        return 0
+
+    lax.fori_loop(*pairs, body, 0)
+
+
+def normal_parts(values):
+    centre = values - jnp.mean(values, -1, keepdims=True)
+    scale = lax.rsqrt(jnp.mean(centre * centre, -1, keepdims=True) + EPSILON)
+    return centre * scale, scale
+
+
 def enter_kernel(
-    w0, w1, w2, w3, tokens, partial_mod,
-    o0, o1, o2, o3, other_tokens, modulation,
-    got_core, sum_core, got_z, sum_z, got_x, sum_x, got_y,
+    w0, w1, w2, w3, tokens_in, class_in, time_in, modulate_in, own_ids, placed,
+    o0, o1, o2, o3, modulation, labels, sinus, bias, cond, first_in, projected, attended,
+    ids, other_tokens, w_attend,
+    partial_mod, got_core, sum_core, got_z, slabs, sum_z, got_x, sum_x, got_y, both_first,
+    tokens, class_table, time_weight, modulate_weight,
     send_sems, recv_sems, local_sems,
 ):
     place = Place()
     copies = Copies(send_sems, recv_sems, local_sems)
-    greet(place.everyone())
     sources, wholes = (w0, w1, w2, w3), (o0, o1, o2, o3)
     waves = [
         [
@@ -243,40 +337,75 @@
         for gather in waves[wave]:
             gather.finish(phase)
 
-    tokens_copy = copies.send(tokens, other_tokens, place.along("z", 2))
+    operands = [
+        copies.move(source, target)
+        for source, target in (
+            (class_in, class_table),
+            (time_in, time_weight),
+            (modulate_in, modulate_weight),
+            (tokens_in, tokens),
+        )
+    ]
+    ids[place.core, place.z_lo, place.at["x"], place.at["y"]] = own_ids[...]
+    greet(place.everyone())
+    id_gather = SmallGather(place, copies, ids)
+    id_gather.stage(0)
     for gather in gathers:
         gather.begin()
-    mod_core = copies.send(
-        partial_mod.at[:, :, :, 1 - place.core], got_core, place.other_core()
-    )
+    tokens_copy = copies.send(tokens_in, other_tokens, place.along("z", 2))
+    id_gather.stage(1)
     for gather in gathers:
         gather.ready()
         gather.start(0)
-    mod_core.wait_recv()
-    for z_lo in range(2):
-        for x in range(4):
-            for y in range(4):
-                sum_core[z_lo, x, y] = (
-                    partial_mod[z_lo, x, y, place.core].astype(F32) + got_core[z_lo, x, y].astype(F32)
-                ).astype(BF16)
-    mod_z = copies.send(sum_core.at[1 - place.z_lo], got_z, place.other_z_lo())
-    for wave in range(4):
+    id_gather.stage(2)
+    for wave in range(2):
         finish(wave, 0)
         start(wave, 1)
+    id_gather.stage(3)
+    for wave in range(2, 4):
+        finish(wave, 0)
+        start(wave, 1)
+    id_gather.arrive()
+    finish(0, 1)
+    start(0, 2)
+
+    for copy in operands:
+        copy.wait()
+    cond[...] = conditioned(ids, class_table, time_weight, labels, sinus, bias)
+    act = (cond[...] / (1.0 + jnp.exp(-cond[...]))).astype(BF16)
+    for column in range(0, 6 * D, D):
+        columns = slice(column, column + D)
+        partial_mod[:, columns] = (
+            jnp.dot(act, modulate_weight[:, columns], preferred_element_type=F32) + placed[:, columns]
+        ).astype(BF16)
+
+    def share(index, count):
+        return pl.ds(pl.multiple_of(index * count, count), count)
+
+    mod_core = copies.send(partial_mod.at[share(1 - place.core, 32)], got_core, place.other_core())
+    for wave in (1, 2, 3):
+        forward(wave, 1)
+    mod_core.wait_recv()
+    sum_core[...] = (
+        partial_mod[share(place.core, 32)].astype(F32) + got_core[...].astype(F32)
+    ).astype(BF16)
+    mod_z = copies.send(sum_core.at[share(1 - place.z_lo, 16)], got_z, place.other_z_lo())
+    finish(1, 1)
+    start(1, 2)
     mod_z.wait_recv()
-    for x in range(4):
-        for y in range(4):
-            sum_z[x, y] = (
-                sum_core[place.z_lo, x, y].astype(F32) + got_z[x, y].astype(F32)
-            ).astype(BF16)
+    for row in range(48):
+        columns = slice(row * 128, row * 128 + 128)
+        slabs[:, row, :] = sum_core[share(place.z_lo, 16), columns].astype(F32) + got_z[
+            :, columns
+        ].astype(F32)
+    sum_z[...] = slabs[...].astype(BF16).reshape(4, 4, 48, 128)
     mod_x = [
         copies.send(sum_z.at[place.step("x", distance)], got_x.at[distance - 1], place.along("x", distance))
         for distance in (1, 2, 3)
     ]
-    finish(0, 1)
-    start(0, 2)
-    for wave in (1, 2, 3):
-        forward(wave, 1)
+    finish(2, 1)
+    forward(0, 2)
+    start(2, 2)
     for copy in mod_x:
         copy.wait_recv()
     for y in range(4):
@@ -288,121 +417,98 @@
         copies.send(sum_x.at[place.step("y", distance)], got_y.at[distance - 1], place.along("y", distance))
         for distance in (1, 2, 3)
     ]
-    finish(1, 1)
-    start(1, 2)
-    finish(2, 1)
-    forward(0, 2)
-    start(2, 2)
+    finish(3, 1)
+    finish(0, 2)
+    for gather in waves[0]:
+        for copy in gather.to_core:
+            copy.wait_recv()
+    weight_copy = copies.move(o0, w_attend)
+    forward(1, 2)
+    start(3, 2)
     for copy in mod_y:
         copy.wait_recv()
     total = sum_x[place.at["y"]].astype(F32)
     for slot in range(3):
         total += got_y[slot].astype(F32)
-    modulation[...] = total
-    finish(3, 1)
-    forward(1, 2)
-    start(3, 2)
-    finish(0, 2)
+    for row in range(48):
+        vector, lane = divmod(row, 8)
+        modulation[vector : vector + 1, lane * 128 : lane * 128 + 128] = total[row : row + 1]
+    tokens_copy.wait_recv()
+    for row, source in enumerate((tokens, other_tokens)):
+        normal, _ = normal_parts(source[...].astype(F32))
+        both_first[row * HALF : row * HALF + HALF] = (
+            normal * (1.0 + modulation[1:2]) + modulation[0:1]
+        ).astype(BF16)
+    first_in[...] = both_first[:HALF]
     forward(2, 2)
+    weight_copy.wait()
+    for column in range(0, 3 * D, 512):
+        columns = slice(column, column + 512)
+        projected[:, columns] = jnp.dot(
+            both_first[...],
+            w_attend[:, :, :, :, :, columns].reshape(D, 512),
+            preferred_element_type=F32,
+        ).astype(BF16)
     finish(1, 2)
     forward(3, 2)
+    attention_forward(projected, attended, (0, HEADS // 4))
     finish(2, 2)
+    attention_forward(projected, attended, (HEADS // 4, HEADS // 2))
     finish(3, 2)
-    tokens_copy.wait_recv()
-    for gather in gathers:
-        for copy in gather.to_core:
-            copy.wait_recv()
+    for wave in waves[1:]:
+        for gather in wave:
+            for copy in gather.to_core:
+                copy.wait_recv()
     copies.drain()
 
 
-def enter(weights, tokens, partial_mod):
-    anywhere = pl.BlockSpec(memory_space=pl.ANY)
+def enter(weights, tokens, class_table, time_weight, modulate_weight, own_ids, placed):
+    outside = pl.BlockSpec(memory_space=pl.ANY)
     inside = pl.BlockSpec(memory_space=pltpu.VMEM)
     slab = (48, 128)
     shapes = [jax.ShapeDtypeStruct((2, 4, 4, 2, rows, columns), BF16) for rows, columns in WEIGHTS]
-    shapes += [jax.ShapeDtypeStruct((HALF, D), BF16), jax.ShapeDtypeStruct(slab, F32)]
+    shapes += [
+        jax.ShapeDtypeStruct((6, D), F32),
+        jax.ShapeDtypeStruct((64, 128), F32),
+        jax.ShapeDtypeStruct((2, 64, 128), F32),
+        jax.ShapeDtypeStruct((32, 128), F32),
+        jax.ShapeDtypeStruct((64, 16), F32),
+        jax.ShapeDtypeStruct((HALF, D), BF16),
+        jax.ShapeDtypeStruct((SEQ, 3 * D), BF16),
+        jax.ShapeDtypeStruct((HALF, D), BF16),
+    ]
     out = pl.pallas_call(
         enter_kernel,
         out_shape=shapes,
-        in_specs=[anywhere] * 5 + [inside],
-        out_specs=[anywhere] * 5 + [inside],
+        in_specs=[outside] * 8 + [inside] * 2,
+        out_specs=[outside] * 4 + [inside] * 8,
         scratch_shapes=[
-            pltpu.VMEM((2, 4, 4) + slab, BF16),
-            pltpu.VMEM((2, 4, 4) + slab, BF16),
-            pltpu.VMEM((4, 4) + slab, BF16),
+            pltpu.VMEM((2, 2, 4, 4, 8, 128), F32),
+            pltpu.VMEM((HALF, D), BF16),
+            pltpu.VMEM((2, 4, 4, 2, 16, 3 * D), BF16),
+            pltpu.VMEM((64, 6 * D), BF16),
+            pltpu.VMEM((32, 6 * D), BF16),
+            pltpu.VMEM((32, 6 * D), BF16),
+            pltpu.VMEM((16, 6 * D), BF16),
+            pltpu.VMEM((16,) + slab, F32),
             pltpu.VMEM((4, 4) + slab, BF16),
             pltpu.VMEM((3, 4) + slab, BF16),
             pltpu.VMEM((4,) + slab, BF16),
             pltpu.VMEM((3,) + slab, BF16),
+            pltpu.VMEM((SEQ, D), BF16),
+            pltpu.VMEM((HALF, D), BF16),
+            pltpu.VMEM((16, CLASSES), BF16),
+            pltpu.VMEM((16, FREQ), BF16),
+            pltpu.VMEM((16, 6 * D), BF16),
         ]
-        + copy_scratch(12 * 23 + 9, 12),
+        + copy_scratch(12 * 23 + 9 + 8, 17),
         compiler_params=pltpu.CompilerParams(
-            collective_id=0, has_side_effects=True, vmem_limit_bytes=32 * 2**20
+            collective_id=0, has_side_effects=True, vmem_limit_bytes=60 * 2**20
         ),
         name="enter",
-    )(*weights, tokens, partial_mod)
-    full = [
-        whole.reshape(64 * rows, columns) for whole, (rows, columns) in zip(out[:4], WEIGHTS)
-    ]
-    return full, out[4], out[5].reshape(6, D)
-
-
-class SmallGather:
-    def __init__(self, place, copies, whole):
-        self.place, self.copies, self.whole = place, copies, whole
-        self.waiting = []
-
-    def arrive(self):
-        for copy in self.waiting:
-            copy.wait_recv()
-        self.waiting = []
-
-    def stage(self, which):
-        self.arrive()
-        place, whole, send = self.place, self.whole, self.copies.send
-        at, core = place.at, place.core
-        if which == 0:
-            piece = whole.at[place.z_lo, at["x"], at["y"], core]
-            self.waiting = [send(piece, piece, place.along("y", d)) for d in (1, 2, 3)]
-        elif which == 1:
-            piece = whole.at[place.z_lo, at["x"], :, core]
-            self.waiting = [send(piece, piece, place.along("x", d)) for d in (1, 2, 3)]
-        elif which == 2:
-            piece = whole.at[place.z_lo, :, :, core]
-            self.waiting = [send(piece, piece, place.other_z_lo())]
-        else:
-            piece = whole.at[:, :, :, core]
-            self.waiting = [send(piece, piece, place.other_core())]
-
-
-def ids_kernel(own, whole, send_sems, recv_sems, local_sems):
-    place = Place()
-    copies = Copies(send_sems, recv_sems, local_sems)
-    whole[place.z_lo, place.at["x"], place.at["y"], place.core] = own[...]
-    greet(place.everyone())
-    gather = SmallGather(place, copies, whole)
-    for which in range(4):
-        gather.stage(which)
-    gather.arrive()
-    copies.drain()
-
-
-def gather_ids(labels, timesteps, offsets):
-    inside = pl.BlockSpec(memory_space=pltpu.VMEM)
-    lane = lax.broadcasted_iota(jnp.int32, (7, 128), 1)
-    ids = jnp.where(lane == 0, labels[0], timesteps[0]).astype(F32)
-    own = jnp.concatenate([jnp.pad(offsets.astype(F32)[None], ((0, 0), (0, 64))), ids], 0)
-    whole = pl.pallas_call(
-        ids_kernel,
-        out_shape=jax.ShapeDtypeStruct((2, 4, 4, 2, 8, 128), F32),
-        in_specs=[inside],
-        out_specs=inside,
-        scratch_shapes=copy_scratch(8, 0),
-        compiler_params=pltpu.CompilerParams(collective_id=1, has_side_effects=True),
-        name="gather_ids",
-    )(own).reshape(64, 8, 128)
-    ids = whole[:, 1, :2].astype(jnp.int32)
-    return ids[:, 0], ids[:, 1], whole[:, 0, :64].reshape(FF)
+    )(*weights, tokens, class_table, time_weight, modulate_weight, own_ids, placed)
+    full = [whole.reshape(64 * rows, columns) for whole, (rows, columns) in zip(out[:4], WEIGHTS)]
+    return full, out[4:]
 
 
 class Pair:
@@ -621,10 +727,13 @@
     lax.fori_loop(*pairs, body, 0)
 
 
-def normal_parts(values):
-    centre = values - jnp.mean(values, -1, keepdims=True)
-    scale = lax.rsqrt(jnp.mean(centre * centre, -1, keepdims=True) + EPSILON)
-    return centre * scale, scale
+LEAVE_STEPS = (
+    "M3", "S30", "M2", "S20", "M1", "S10", "A0", "F3", "A1", "F2",
+    "F1", "M0", "S00", "L", "N30", "S31", "N20", "S21", "F0", "G0",
+    "N10", "S11", "N31", "S32", "N21", "S22", "G1", "N00", "S01", "N11",
+    "S12", "G2", "N32", "H3", "N22", "H2", "N01", "S02", "G3", "N12",
+    "H1", "T3", "T2", "N02", "H0", "T1", "G4", "T0",
+)
 
 
 def leave_kernel(*refs):
@@ -694,92 +803,83 @@
         for half in pair:
             half.wait()
 
-    meet(pairs[3])
-    make_tall_parts(lefts[3], rights[3], of(3))
-    start(3, 0)
-    meet(pairs[2])
-    make_parts(lefts[2], rights[2], of(2, 2))
-    start(2, 0)
-    meet(pairs[1])
-    make_parts(lefts[2], rights[2], of(2, 1))
-    make_parts(lefts[1], rights[1], of(1))
-    start(1, 0)
-
-    att_copy.wait_recv()
-    attention_back(projected, both_att, grad_proj, (0, HEADS // 4))
-    forward(3)
-    attention_back(projected, both_att, grad_proj, (HEADS // 4, HEADS // 2))
-    late.append(Pair(place, copies, grad_proj, rights[0], BLOCKS[0]))
-    forward(2)
-    forward(1)
-    finish(3, 0)
-    start(3, 1)
-    meet(late)
-    make_parts(lefts[0], rights[0], of(0))
-    start(0, 0)
-
-    weight_copy.wait()
-    normal, scale = normal_parts(tokens[...].astype(F32))
-    grad_first = jnp.concatenate(
-        [
-            lax.dot_general(
-                grad_proj[...], weight[start : start + 256], NT, preferred_element_type=F32
-            )
-            for start in range(0, D, 256)
-        ],
-        1,
-    )
-    back = grad_first * (1.0 + scale_one[...])
-    tokens_grad[...] = grad_middle[...] + scale * (
-        back
-        - jnp.mean(back, -1, keepdims=True)
-        - normal * jnp.mean(back * normal, -1, keepdims=True)
-    )
-    vector[...] = sums[...]
-    for place_of, total in ((0, grad_first), (8, grad_first * normal)):
-        total = jnp.sum(total, 0, keepdims=True)
-        for row in range(8):
-            vector[place_of + row : place_of + row + 1, :] = total[:, row * 128 : (row + 1) * 128]
-    vector_sent[...] = vector[...].astype(BF16)
-    vector_copy = copies.send(vector_sent, vector_got, place.along("z", 2))
-
-    finish(2, 0)
-    start(2, 1)
-    finish(3, 1)
-    start(3, 2)
-    forward(0)
-    finish(1, 0)
-    start(1, 1)
-    vector_copy.wait_recv()
-    whole[place.z_lo, place.at["x"], place.at["y"], place.core] = (
-        vector_sent[...].astype(F32) + vector_got[...].astype(F32)
-    ).astype(BF16)
+    later = []
+
+    def make(which):
+        if which == 0:
+            meet(late)
+            make_parts(lefts[0], rights[0], of(0))
+        elif which == 3:
+            meet(pairs[3])
+            make_tall_parts(lefts[3], rights[3], of(3))
+        elif which == 2:
+            meet(pairs[2])
+            make_parts(lefts[2], rights[2], of(2, 2))
+        else:
+            meet(pairs[1])
+            make_parts(lefts[2], rights[2], of(2, 1))
+            make_parts(lefts[1], rights[1], of(1))
+
+    def attention(which):
+        if which == 0:
+            att_copy.wait_recv()
+            attention_back(projected, both_att, grad_proj, (0, HEADS // 4))
+        else:
+            attention_back(projected, both_att, grad_proj, (HEADS // 4, HEADS // 2))
+            late.append(Pair(place, copies, grad_proj, rights[0], BLOCKS[0]))
+
+    def input_gradient():
+        weight_copy.wait()
+        normal, scale = normal_parts(tokens[...].astype(F32))
+        grad_first = jnp.concatenate(
+            [
+                lax.dot_general(
+                    grad_proj[...], weight[start : start + 256], NT, preferred_element_type=F32
+                )
+                for start in range(0, D, 256)
+            ],
+            1,
+        )
+        back = grad_first * (1.0 + scale_one[...])
+        tokens_grad[...] = grad_middle[...] + scale * (
+            back
+            - jnp.mean(back, -1, keepdims=True)
+            - normal * jnp.mean(back * normal, -1, keepdims=True)
+        )
+        vector[...] = sums[...]
+        for place_of, total in ((0, grad_first), (8, grad_first * normal)):
+            total = jnp.sum(total, 0, keepdims=True)
+            for row in range(8):
+                vector[place_of + row : place_of + row + 1, :] = total[:, row * 128 : (row + 1) * 128]
+        vector_sent[...] = vector[...].astype(BF16)
+        later.append(copies.send(vector_sent, vector_got, place.along("z", 2)))
+
     gather = SmallGather(place, copies, whole)
-    gather.stage(0)
-    finish(2, 1)
-    start(2, 2)
-    finish(3, 2)
-    share(3)
-    gather.stage(1)
-    finish(1, 1)
-    start(1, 2)
-    finish(0, 0)
-    start(0, 1)
-    gather.stage(2)
-    finish(2, 2)
-    share(2)
-    finish(1, 2)
-    share(1)
-    store(3)
-    finish(0, 1)
-    start(0, 2)
-    gather.stage(3)
-    store(2)
-    finish(0, 2)
-    share(0)
-    store(1)
-    gather.arrive()
-    store(0)
+
+    def vectors(which):
+        if which == 0:
+            later[0].wait_recv()
+            whole[place.core, place.z_lo, place.at["x"], place.at["y"]] = (
+                vector_sent[...].astype(F32) + vector_got[...].astype(F32)
+            ).astype(BF16)
+        if which < 4:
+            gather.stage(which)
+        else:
+            gather.arrive()
+
+    steps = {
+        "M": make,
+        "A": attention,
+        "L": input_gradient,
+        "G": vectors,
+        "S": start,
+        "F": forward,
+        "N": finish,
+        "H": share,
+        "T": store,
+    }
+    for step in LEAVE_STEPS:
+        steps[step[0]](*(int(number) for number in step[1:]))
     copies.drain()
 
 
@@ -789,7 +889,7 @@
 
 
 def leave(lefts, rights, w_attend, projected, grad_att, tokens, grad_middle, scale_one, sums):
-    anywhere = pl.BlockSpec(memory_space=pl.ANY)
+    outside = pl.BlockSpec(memory_space=pl.ANY)
     inside = pl.BlockSpec(memory_space=pltpu.VMEM)
     scratch = [pltpu.VMEM((SEQ, width), BF16) for width in LEFTS]
     scratch += [pltpu.VMEM((blocks, SEQ, 2 * QUARTER), BF16) for blocks in BLOCKS]
@@ -808,12 +908,12 @@
     return pl.pallas_call(
         leave_kernel,
         out_shape=[jax.ShapeDtypeStruct((rows, columns), F32) for rows, columns in WEIGHTS]
-        + [jax.ShapeDtypeStruct((2, 4, 4, 2) + sums.shape, BF16), jax.ShapeDtypeStruct((HALF, D), F32)],
-        in_specs=[anywhere] * 8 + [inside] * 6,
+        + [jax.ShapeDtypeStruct((2, 2, 4, 4) + sums.shape, BF16), jax.ShapeDtypeStruct((HALF, D), F32)],
+        in_specs=[outside] * 8 + [inside] * 6,
         out_specs=[inside] * 6,
         scratch_shapes=scratch,
         compiler_params=pltpu.CompilerParams(
-            collective_id=3, has_side_effects=True, vmem_limit_bytes=58 * 2**20
+            collective_id=3, has_side_effects=True, vmem_limit_bytes=60 * 2**20
         ),
         name="leave",
     )(*lefts, *rights, w_attend, projected, grad_att, tokens, grad_middle, scale_one, sums)
@@ -840,19 +940,6 @@
     )
     angles = step_ids.astype(jnp.float32)[:, None] * freq_rates[None, :]
     return jnp.concatenate([jnp.cos(angles), jnp.sin(angles)], axis=-1)
-
-
-def head_split(rows_in):
-    return rows_in.reshape(rows_in.shape[0], HEADS, HEAD)
-
-
-def attend_scores(query_rows, key_rows):
-    return jnp.einsum(
-        "qhd,khd->hqk",
-        head_split(query_rows),
-        head_split(key_rows),
-        preferred_element_type=F32,
-    ) * HEAD ** (-0.5)
 
 
 def per_device(
@@ -871,47 +958,42 @@
     contract_weight,
 ):
     shard_index = lax.axis_index("fsdp")
-    token_half = lax.axis_index("ctx")
-    all_labels, all_steps, b_hidden = gather_ids(labels, timesteps, hidden_offset[0])
-    onehot = all_labels[:, None] == jnp.arange(CLASSES, dtype=jnp.int32)[None, :]
-    sinus_rows = sinusoid(all_steps).astype(BF16)
-    cond_cols = jnp.dot(
-        onehot.astype(BF16), class_table, preferred_element_type=F32
-    ) + jnp.dot(sinus_rows, time_weight, preferred_element_type=F32)
     offset_width = modulate_offset.shape[1]
-    act_cols = jax.nn.silu(cond_cols).astype(BF16)
-    partial_mod = jnp.dot(act_cols, modulate_weight[0], preferred_element_type=F32)
     placed = lax.dynamic_update_slice(
         jnp.zeros((1, 6 * D), F32),
         modulate_offset.astype(F32),
         (jnp.int32(0), shard_index * offset_width),
     )
-    partial_mod = (partial_mod + placed).astype(BF16).reshape(2, 4, 4, 2, 48, 128)
-    (w_attend, w_output, w_expand, w_contract), other_tokens, modulation = enter(
+    lane = lax.broadcasted_iota(jnp.int32, (1, 128), 1)
+    own_bias = jnp.where(
+        lax.div(lane, 64) == lax.rem(shard_index, 2), jnp.tile(hidden_offset.astype(F32), (1, 2)), 0.0
+    )
+    own_ids = jnp.concatenate(
+        [
+            own_bias,
+            jnp.broadcast_to(labels[0].astype(F32), (1, 128)),
+            sinusoid(timesteps).astype(BF16).astype(F32).reshape(2, 128),
+            jnp.zeros((4, 128), F32),
+        ],
+        0,
+    )
+    full, (modulation, labels, sinus, bias, cond_cols, first_in, projected, attended) = enter(
         (attend_weight[0], output_weight[0], expand_weight[0], contract_weight[0]),
         tokens[0],
-        partial_mod,
+        class_table.T,
+        time_weight.T,
+        modulate_weight[0],
+        own_ids,
+        placed,
     )
-    shift_one, scale_one, gate_one, shift_two, scale_two, gate_two = [modulation[i] for i in range(6)]
+    w_attend, w_output, w_expand, w_contract = full
+    b_hidden = bias.reshape(FF)
+    onehot = labels[:, :1].astype(jnp.int32) == jnp.arange(CLASSES, dtype=jnp.int32)[None, :]
+    sinus_rows = jnp.concatenate([sinus[0], sinus[1]], 1)
+    act_cols = jax.nn.silu(cond_cols).astype(BF16)
+    _, scale_one, gate_one, shift_two, scale_two, gate_two = [modulation[i] for i in range(6)]
 
     hidden = tokens[0].astype(F32)
-    both_hidden = jnp.concatenate([tokens[0], other_tokens], 0).astype(F32)
-    both_first = modulated(both_hidden, shift_one, scale_one).astype(BF16)
-    first_in = both_first[:HALF]
-    projected = jnp.dot(both_first, w_attend, preferred_element_type=F32).astype(BF16)
-    query_rows, key_rows, value_rows = projected[:, :D], projected[:, D : 2 * D], projected[:, 2 * D :]
-    scores = attend_scores(query_rows[:HALF], key_rows)
-    top_score = jnp.max(scores, -1, keepdims=True)
-    exp_terms = jnp.exp(scores - top_score)
-    totals = jnp.sum(exp_terms, -1, keepdims=True)
-    rounded_probs = (exp_terms / totals).astype(BF16)
-    attended = (
-        jnp.einsum(
-            "hqk,khd->qhd", rounded_probs, head_split(value_rows), preferred_element_type=F32
-        )
-        .reshape(-1, D)
-        .astype(BF16)
-    )
     branch_one = jnp.dot(attended, w_output, preferred_element_type=F32)
     middle = hidden + gate_one * branch_one
     second_in = modulated(middle, shift_two, scale_two).astype(BF16)
@@ -966,7 +1048,7 @@
     _, silu_pull = jax.vjp(jax.nn.silu, cond_cols)
     grad_cond = silu_pull(grad_act_cols)[0]
     table_grad = jnp.einsum("bc,bd->cd", onehot.astype(F32), grad_cond, precision=HIGHEST)
-    time_grad = jnp.einsum("bf,bd->fd", sinus_rows.astype(F32), grad_cond, precision=HIGHEST)
+    time_grad = jnp.einsum("bf,bd->fd", sinus_rows, grad_cond, precision=HIGHEST)
     return (
         result,
         tokens_grad[None],

time: 230 us -> 198 us (0.86)
  Pallas kernels: 173 us -> 160 us
  matrix products: 31.4 us -> 21.6 us
  local copies, waits for them, and re-layouts: 17.1 us -> 8.21 us
    pallas_call x2 -> x1, Pallas kernels: 90.4 us -> 77.4 us  [enter(): pl.pallas_call(enter_kernel, out_shape=shapes, in_specs=[outside] * 8 + [...]
    slice x8 -> x0, local copies, waits for them, and re-layouts: 9.06 us -> none  [the longest x2 3.5 us: per_device(): projected[:, D:2 * D]]
    dot_general x6 -> x1, matrix products: 7.1 us -> 0.83 us  [per_device(): jnp.einsum('bf,bd->fd', sinus_rows, grad_cond, precision=HIGHEST)]
    unnamed x63 -> x57, local copies, waits for them, and re-layouts: 7.11 us -> 7.63 us
where the time goes in v3:
time: 198 us
  Pallas kernels  160 us (81%)
  matrix products  21.6 us (11%)
  local copies, waits for them, and re-layouts  8.21 us (4%)
  other arithmetic  5.6 us (3%)
  between operations  2.33 us (1%)
    pallas_call x1, Pallas kernels, leave(): pl.pallas_call(leave_kernel, out_shape=[jax.ShapeDtypeStruct((rows, colum...  82.8 us
    pallas_call x1, Pallas kernels, enter(): pl.pallas_call(enter_kernel, out_shape=shapes, in_specs=[outside] * 8 + [...  77.4 us
    unnamed x57, local copies, waits for them, and re-layouts  7.63 us
    dot_general x1, matrix products, per_device(): jnp.dot(second_in, w_expand, preferred_element_type=F32) + b_hidden  5.48 us
    dot_general x1, matrix products, per_device(): jnp.einsum('td,fd->tf', grad_two, w_contract, preferred_element_type=F32)  4.07 us

profile of v3, /device:TPU:1, one launch (start us, length us, event | category | flops | bytes accessed | tf_op | source)
XLA Modules:
  0.0 198.0 jit_solution(6425372762552584336)
XLA Ops:
  0.6 0.7 bitcast_convert_fusion
  1.3 0.1 tile.16
  2.1 0.1 sine_convert_fusion
  2.8 0.1 pad.3.clone
  2.9 0.1 pad.5.clone
  2.9 0.7 maximum_maximum_fusion.own_ids
  3.6 0.7 convert_element_type.86
  4.3 0.3 dynamic_update_slice.3.placed
  4.5 0.6 copy-done.12
  5.2 77.4 %enter.1 = (bf16[2,4,4,2,16,3072]{5,4,3,2,1,0:T(8,128)(2,1)}, bf16[2,4,4,2,16,1024]{5,4,3,2,1,0:T(8,128)(2,1)}, bf16[2,4,4,2,16,4096]{5,4,3,2,1,0:T(8,128)(2,1)}...) custom-call(bf16[16,3072]{1,0:T(8,128)(2,1)} %bitcast.108, ...), custom_call_target="tpu_custom_call" | custom-call | tf_op jit(solution)/shard_map/enter/pallas_call | solution.py:480
  82.6 1.6 fusion.41
  84.2 2.2 %fusion.40 = (f32[128]{0:T(128)S(1)}, f32[128,1024]{1,0:T(8,128)S(1)}, f32[128,1024]{1,0:T(8,128)S(1)}) fusion(f32[1024]{0:T(1024)S(1)} %bitcast.114, bf16[1,128,1024]{2,1,0:T(8,128)(2,1)} %param.13, bf16[128,1024]{1,0:T(8,128)(2,1)} %get-tuple-element.30.refs_1_, bf16[1024,1024]{1,0:T(8,128)(2,1)} %bitcast.87), kind=kOutput, calls=%fused_computation.80 | convolution fusion | flops 268959616 | bytes 3674624 | tf_op jit(solution)/shard_map/dot_general | solution.py:997
  86.4 0.2 multiply_reduce_fusion.3
  86.6 0.0 slice-start
  86.6 0.2 add_convert_fusion.1.refs_2_
  86.8 0.0 copy-start.6
  86.8 0.0 copy-done.18
  86.8 0.0 slice-start.1
  86.8 0.0 copy-start.5
  86.8 0.0 slice-start.2
  86.9 5.5 %multiply_convert_fusion = (bf16[128,4096]{1,0:T(8,128)(2,1)S(1)}, f32[128,4096]{1,0:T(8,128)S(1)}) fusion(f32[4096]{0:T(1024)S(1)} %bitcast.125, bf16[128,1024]{1,0:T(8,128)(2,1)S(1)} %add_convert_fusion.1.refs_2_, bf16[1024,4096]{1,0:T(8,128)(2,1)} %bitcast.89), kind=kOutput, calls=%fused_computation.12 | convolution fusion | flops 1078984704 | bytes 11812864 | tf_op jit(solution)/shard_map/dot_general | solution.py:1000
  92.3 0.0 copy-done.6
  92.4 0.0 copy-start.1
  92.4 0.0 slice-done
  92.4 0.2 slice-done.1
  92.6 0.0 copy-done.5
  92.6 4.1 %convert_reduce_fusion = (f32[4096]{0:T(1024)S(1)}, bf16[128,4096]{1,0:T(8,128)(2,1)S(1)}) fusion(f32[128,4096]{1,0:T(8,128)S(1)} %get-tuple-element.70, bf16[4096,1024]{1,0:T(8,128)(2,1)S(1)} %bitcast.85, bf16[1,128,1024]{2,1,0:T(8,128)(2,1)S(1)} %copy-done.5, f32[1024]{0:T(1024)S(1)} %bitcast.118), kind=kOutput, calls=%fused_computation.11 | convolution fusion | flops 1085665280 | bytes 11816960 | tf_op jit(solution)/shard_map/td,fd->tf/dot_general | solution.py:1008
  96.7 0.0 copy-start.3
  96.7 0.0 slice-done.2
  96.7 0.0 slice-done.3
  96.7 3.0 %multiply_reduce_fusion = (f32[1024]{0:T(1024)S(1)}, f32[128]{0:T(128)S(1)}, f32[1024]{0:T(1024)S(1)}, f32[128,1024]{1,0:T(8,128)S(1)}) fusion(f32[128,1024]{1,0:T(8,128)S(1)} %get-tuple-element.55, f32[128]{0:T(128)S(1)} %fusion.29, f32[128]{0:T(128)S(1)} %broadcast_multiply_fusion, f32[1024]{0:T(1024)S(1)} %bitcast.110, ...), kind=kOutput, calls=%fused_computation.24 | convolution fusion | flops 1074788224 | bytes 10499584 | tf_op jit(solution)/shard_map/tf,df->td/dot_general | solution.py:1012
  99.8 0.0 copy-done.3
  99.8 0.0 copy-done.1
  99.8 2.2 %fusion.11 = (f32[1024]{0:T(1024)S(1)}, bf16[1,128,1024]{2,1,0:T(8,128)(2,1)}, f32[128]{0:T(128)S(1)}, f32[128,1024]{1,0:T(8,128)S(1)}, bf16[128,1024]{1,0:T(8,128)(2,1)}) fusion(bf16[1,128,1024]{2,1,0:T(8,128)(2,1)S(1)} %copy-done.5, f32[128,1024]{1,0:T(8,128)S(1)} %get-tuple-element.55, f32[1024]{0:T(1024)S(1)} %bitcast.119, ...), kind=kOutput, calls=%fused_computation.22 | convolution fusion | flops 1075706752 | bytes 11810816 | tf_op jit(solution)/shard_map/dot_general | solution.py:1002
  102.0 0.2 multiply_reduce_fusion.1
  102.2 0.0 copy-start.2
  102.2 0.0 copy-start.15
  102.3 1.5 copy-done
  103.8 1.6 convolution_convert_fusion.refs_9_
  105.3 0.0 copy-done.2
  105.3 0.0 copy-done.15
  105.3 0.0 copy-done.4
  105.3 82.8 %leave.1 = (f32[16,3072]{1,0:T(8,128)}, f32[16,1024]{1,0:T(8,128)}, f32[16,4096]{1,0:T(8,128)}, f32[64,1024]{1,0:T(8,128)}, bf16[2,2,4,4,80,128]{5,4,3,2,1,0:T(8,128)(2,1)}, /*index=5*/f32[128,1024]{1,0:T(8,128)}) custom-call(bf16[128,1024]{1,0:T(8,128)(2,1)} %get-tuple-element.35.refs_0_, bf16[128,1024]{1,0:T(8,128)(2,1)} %get-tuple-element.30.refs_1_, ...), custom_call_target="tpu_custom_call" | custom-call | tf_op jit(solution)/shard_map/leave/pallas_call | solution.py:908
  188.2 0.0 copy-start.16
  188.2 0.0 copy-start.10
  188.2 1.7 copy.31
  189.9 0.0 copy-done.16
  189.9 0.0 copy-start.13
  189.9 0.0 copy-start.17
  189.9 1.0 convolution_bitcast_fusion
  190.9 0.1 slice.36
  191.0 0.0 copy-start.14
  191.0 0.6 convert_reduce_fusion.2
  191.7 0.4 fusion.27
  192.0 0.8 fusion.22
  192.9 0.1 convert_reduce_fusion.3
  193.0 0.9 fusion.20
  193.9 0.6 convert_reduce_fusion.1
  194.5 0.8 copy.45
  195.3 0.7 copy.46
  196.0 0.6 copy.47
  196.6 0.0 copy-done.9
  196.6 0.7 copy.48
  197.3 0.7 copy.49
  (35 shorter events, 0.2 us)
Async XLA Ops:
  4.5 0.6 copy-start.12
  84.2 2.6 %copy-start.18 = (f32[32,128]{1,0:T(8,128)S(1)}, f32[32,128]{1,0:T(8,128)}, u32[]{:S(2)}) copy-start(f32[32,128]{1,0:T(8,128)} %get-tuple-element.33) | copy-start | bytes 49156
  86.6 5.7 %slice-start = ((s8[8388608]{0:T(1024)(128)(4,1)}), s8[4194304]{0:T(1024)(128)(4,1)S(1)}, s32[]{:S(2)}) async-start(s8[8388608]{0:T(1024)(128)(4,1)} %bitcast.83), calls=%async_computation | async-start | bytes 8388608
  86.8 5.5 %copy-start.6 = (bf16[128,1024]{1,0:T(8,128)(2,1)}, bf16[128,1024]{1,0:T(8,128)(2,1)S(1)}, u32[]{:S(2)}) copy-start(bf16[128,1024]{1,0:T(8,128)(2,1)S(1)} %add_convert_fusion.1.refs_2_) | copy-start | bytes 786436
  86.8 5.8 %slice-start.1 = ((s8[8388608]{0:T(1024)(128)(4,1)}), s8[4194304]{0:T(1024)(128)(4,1)S(1)}, s32[]{:S(2)}) async-start(s8[8388608]{0:T(1024)(128)(4,1)} %bitcast.83), calls=%async_computation.1 | async-start | bytes 8388608
  86.8 5.8 %copy-start.5 = (bf16[1,128,1024]{2,1,0:T(8,128)(2,1)S(1)}, bf16[1,128,1024]{2,1,0:T(8,128)(2,1)}, u32[]{:S(2)}) copy-start(bf16[1,128,1024]{2,1,0:T(8,128)(2,1)} %param.16) | copy-start | bytes 786436
  86.8 9.9 %slice-start.2 = ((s8[8388608]{0:T(1024)(128)(4,1)}), s8[4194304]{0:T(1024)(128)(4,1)S(1)}, s32[]{:S(2)}) async-start(s8[8388608]{0:T(1024)(128)(4,1)} %bitcast.90), calls=%async_computation.2 | async-start | bytes 8388608
  92.4 7.4 %copy-start.1 = (bf16[128,4096]{1,0:T(8,128)(2,1)}, bf16[128,4096]{1,0:T(8,128)(2,1)S(1)}, u32[]{:S(2)}) copy-start(bf16[128,4096]{1,0:T(8,128)(2,1)S(1)} %get-tuple-element.69.refs_3_) | copy-start | bytes 3145732
  92.6 4.1 %slice-start.3 = ((s8[8388608]{0:T(1024)(128)(4,1)}), s8[4194304]{0:T(1024)(128)(4,1)S(1)}, s32[]{:S(2)}) async-start(s8[8388608]{0:T(1024)(128)(4,1)} %bitcast.90), calls=%async_computation.3 | async-start | bytes 8388608
  96.7 3.1 %copy-start.3 = (bf16[128,4096]{1,0:T(8,128)(2,1)}, bf16[128,4096]{1,0:T(8,128)(2,1)S(1)}, u32[]{:S(2)}) copy-start(bf16[128,4096]{1,0:T(8,128)(2,1)S(1)} %get-tuple-element.73.refs_5_) | copy-start | bytes 3145732
  102.0 1.8 copy-start
  102.2 3.2 %copy-start.2 = (f32[128,1024]{1,0:T(8,128)}, f32[128,1024]{1,0:T(8,128)S(1)}, u32[]{:S(2)}) copy-start(f32[128,1024]{1,0:T(8,128)S(1)} %get-tuple-element.51.refs_11_) | copy-start | bytes 1572868
  102.2 3.1 %copy-start.15 = (f32[10240]{0:T(1024)}, f32[10240]{0:T(1024)S(1)}, u32[]{:S(2)}) copy-start(f32[10240]{0:T(1024)S(1)} %constant_dynamic-update-slice_fusion) | copy-start | bytes 122884
  103.8 1.6 copy-start.4
  188.2 1.7 copy-start.16
  188.2 3.5 %copy-start.10 = (bf16[1,16,6144]{2,1,0:T(8,128)(2,1)S(1)}, bf16[1,16,6144]{2,1,0:T(8,128)(2,1)}, u32[]{:S(2)}) copy-start(bf16[1,16,6144]{2,1,0:T(8,128)(2,1)} %param.19) | copy-start | bytes 589828
  189.9 2.1 %copy-start.13 = (f32[2,64,128]{2,1,0:T(8,128)S(1)}, f32[2,64,128]{2,1,0:T(8,128)}, u32[]{:S(2)}) copy-start(f32[2,64,128]{2,1,0:T(8,128)} %get-tuple-element.42) | copy-start | bytes 196612
  189.9 3.0 %copy-start.17 = (f32[64,128]{1,0:T(8,128)S(1)}, f32[64,128]{1,0:T(8,128)}, u32[]{:S(2)}) copy-start(f32[64,128]{1,0:T(8,128)} %get-tuple-element.39) | copy-start | bytes 98308
  190.9 3.6 %copy-start.7 = (f32[128,1024]{1,0:T(8,128)S(1)}, f32[128,1024]{1,0:T(8,128)}, u32[]{:S(2)}) copy-start(f32[128,1024]{1,0:T(8,128)} %get-tuple-element.38) | copy-start | bytes 1572868
  190.9 4.3 %copy-start.11 = (f32[16,3072]{1,0:T(8,128)S(1)}, f32[16,3072]{1,0:T(8,128)}, u32[]{:S(2)}) copy-start(f32[16,3072]{1,0:T(8,128)} %get-tuple-element.43) | copy-start | bytes 589828
  191.0 5.0 %copy-start.14 = (f32[16,1024]{1,0:T(8,128)S(1)}, f32[16,1024]{1,0:T(8,128)}, u32[]{:S(2)}) copy-start(f32[16,1024]{1,0:T(8,128)} %get-tuple-element.44) | copy-start | bytes 196612
  191.0 5.6 %copy-start.9 = (f32[16,4096]{1,0:T(8,128)S(1)}, f32[16,4096]{1,0:T(8,128)}, u32[]{:S(2)}) copy-start(f32[16,4096]{1,0:T(8,128)} %get-tuple-element.45) | copy-start | bytes 786436
  191.0 6.3 %copy-start.8 = (f32[64,1024]{1,0:T(8,128)S(1)}, f32[64,1024]{1,0:T(8,128)}, u32[]{:S(2)}) copy-start(f32[64,1024]{1,0:T(8,128)} %get-tuple-element.46) | copy-start | bytes 786436

commit v4 on v3

--- a/solution.py
+++ b/solution.py
@@ -728,11 +728,11 @@
 
 
 LEAVE_STEPS = (
-    "M3", "S30", "M2", "S20", "M1", "S10", "A0", "F3", "A1", "F2",
-    "F1", "M0", "S00", "L", "N30", "S31", "N20", "S21", "F0", "G0",
-    "N10", "S11", "N31", "S32", "N21", "S22", "G1", "N00", "S01", "N11",
-    "S12", "G2", "N32", "H3", "N22", "H2", "N01", "S02", "G3", "N12",
-    "H1", "T3", "T2", "N02", "H0", "T1", "G4", "T0",
+    "M3", "S30", "M2", "S20", "A0", "F3", "A1", "F2", "M1", "S10",
+    "M0", "S00", "F1", "L", "N30", "S31", "F0", "N20", "S21", "N10",
+    "S11", "G0", "N00", "S01", "N31", "S32", "N21", "S22", "N11", "S12",
+    "G1", "N01", "S02", "N32", "H3", "N22", "H2", "G2", "N12", "H1",
+    "N02", "H0", "G3", "T3", "T2", "T1", "G4", "T0",
 )
 
 
@@ -788,22 +788,22 @@
         for scatter in scatters[3 * wave : 3 * wave + 3]:
             scatter.store()
 
-    pairs = {}
-    for i in (3, 2, 1):
-        pairs[i] = [
-            Pair(place, copies, lefts_in[i], lefts[i]),
-            Pair(place, copies, rights_in[i], rights[i], BLOCKS[i]),
-        ]
+    pairs, late, later = {}, [], []
+
+    def begin_pairs(which):
+        for i in which:
+            pairs[i] = [
+                Pair(place, copies, lefts_in[i], lefts[i]),
+                Pair(place, copies, rights_in[i], rights[i], BLOCKS[i]),
+            ]
+
+    begin_pairs((3,))
     att_copy = copies.send(own_att, both_att.at[pl.ds(HALF, HALF)], place.along("z", 2))
-    late = [Pair(place, copies, lefts_in[0], lefts[0])]
-    weight_copy = copies.move(w_attend, weight)
     both_att[:HALF] = own_att[...]
 
     def meet(pair):
         for half in pair:
             half.wait()
-
-    later = []
 
     def make(which):
         if which == 0:
@@ -811,9 +811,12 @@
             make_parts(lefts[0], rights[0], of(0))
         elif which == 3:
             meet(pairs[3])
+            begin_pairs((2, 1))
+            late.append(Pair(place, copies, lefts_in[0], lefts[0]))
             make_tall_parts(lefts[3], rights[3], of(3))
         elif which == 2:
             meet(pairs[2])
+            later.append(copies.move(w_attend, weight))
             make_parts(lefts[2], rights[2], of(2, 2))
         else:
             meet(pairs[1])
@@ -829,7 +832,7 @@
             late.append(Pair(place, copies, grad_proj, rights[0], BLOCKS[0]))
 
     def input_gradient():
-        weight_copy.wait()
+        later[0].wait()
         normal, scale = normal_parts(tokens[...].astype(F32))
         grad_first = jnp.concatenate(
             [
@@ -858,7 +861,7 @@
 
     def vectors(which):
         if which == 0:
-            later[0].wait_recv()
+            later[1].wait_recv()
             whole[place.core, place.z_lo, place.at["x"], place.at["y"]] = (
                 vector_sent[...].astype(F32) + vector_got[...].astype(F32)
             ).astype(BF16)

time: 198 us -> 196 us (0.990)
  Pallas kernels: 160 us -> 158 us
    pallas_call x1, Pallas kernels: 82.8 us -> 80.5 us  [leave(): pl.pallas_call(leave_kernel, out_shape=[jax.ShapeDtypeStruct((rows, colum...]
where the time goes in v4:
time: 196 us
  Pallas kernels  158 us (81%)
  matrix products  21.6 us (11%)
  local copies, waits for them, and re-layouts  8.21 us (4%)
  other arithmetic  5.6 us (3%)
  between operations  2.33 us (1%)
    pallas_call x1, Pallas kernels, leave(): pl.pallas_call(leave_kernel, out_shape=[jax.ShapeDtypeStruct((rows, colum...  80.5 us
    pallas_call x1, Pallas kernels, enter(): pl.pallas_call(enter_kernel, out_shape=shapes, in_specs=[outside] * 8 + [...  77.4 us
    unnamed x57, local copies, waits for them, and re-layouts  7.63 us
    dot_general x1, matrix products, per_device(): jnp.dot(second_in, w_expand, preferred_element_type=F32) + b_hidden  5.48 us
    dot_general x1, matrix products, per_device(): jnp.einsum('td,fd->tf', grad_two, w_contract, preferred_element_type=F32)  4.07 us

profile of v4, /device:TPU:1, one launch (start us, length us, event | category | flops | bytes accessed | tf_op | source)
XLA Modules:
  0.0 195.7 jit_solution(4572108795511982182)
XLA Ops:
  0.6 0.7 bitcast_convert_fusion
  1.3 0.1 tile.16
  2.1 0.1 sine_convert_fusion
  2.8 0.1 pad.3.clone
  2.9 0.1 pad.5.clone
  2.9 0.7 maximum_maximum_fusion.own_ids
  3.6 0.7 convert_element_type.86
  4.3 0.3 dynamic_update_slice.3.placed
  4.5 0.6 copy-done.12
  5.2 77.4 %enter.1 = (bf16[2,4,4,2,16,3072]{5,4,3,2,1,0:T(8,128)(2,1)}, bf16[2,4,4,2,16,1024]{5,4,3,2,1,0:T(8,128)(2,1)}, bf16[2,4,4,2,16,4096]{5,4,3,2,1,0:T(8,128)(2,1)}...) custom-call(bf16[16,3072]{1,0:T(8,128)(2,1)} %bitcast.108, ...), custom_call_target="tpu_custom_call" | custom-call | tf_op jit(solution)/shard_map/enter/pallas_call | solution.py:480
  82.6 1.6 fusion.41
  84.2 2.2 %fusion.40 = (f32[128]{0:T(128)S(1)}, f32[128,1024]{1,0:T(8,128)S(1)}, f32[128,1024]{1,0:T(8,128)S(1)}) fusion(f32[1024]{0:T(1024)S(1)} %bitcast.114, bf16[1,128,1024]{2,1,0:T(8,128)(2,1)} %param.13, bf16[128,1024]{1,0:T(8,128)(2,1)} %get-tuple-element.30.refs_1_, bf16[1024,1024]{1,0:T(8,128)(2,1)} %bitcast.87), kind=kOutput, calls=%fused_computation.80 | convolution fusion | flops 268959616 | bytes 3674624 | tf_op jit(solution)/shard_map/dot_general | solution.py:1000
  86.4 0.2 multiply_reduce_fusion.3
  86.6 0.0 slice-start
  86.6 0.2 add_convert_fusion.1.refs_2_
  86.8 0.0 copy-start.6
  86.8 0.0 copy-done.18
  86.8 0.0 slice-start.1
  86.8 0.0 copy-start.5
  86.8 0.0 slice-start.2
  86.9 5.5 %multiply_convert_fusion = (bf16[128,4096]{1,0:T(8,128)(2,1)S(1)}, f32[128,4096]{1,0:T(8,128)S(1)}) fusion(f32[4096]{0:T(1024)S(1)} %bitcast.125, bf16[128,1024]{1,0:T(8,128)(2,1)S(1)} %add_convert_fusion.1.refs_2_, bf16[1024,4096]{1,0:T(8,128)(2,1)} %bitcast.89), kind=kOutput, calls=%fused_computation.12 | convolution fusion | flops 1078984704 | bytes 11812864 | tf_op jit(solution)/shard_map/dot_general | solution.py:1003
  92.3 0.0 copy-done.6
  92.4 0.0 copy-start.1
  92.4 0.0 slice-done
  92.4 0.2 slice-done.1
  92.6 0.0 copy-done.5
  92.6 4.1 %convert_reduce_fusion = (f32[4096]{0:T(1024)S(1)}, bf16[128,4096]{1,0:T(8,128)(2,1)S(1)}) fusion(f32[128,4096]{1,0:T(8,128)S(1)} %get-tuple-element.70, bf16[4096,1024]{1,0:T(8,128)(2,1)S(1)} %bitcast.85, bf16[1,128,1024]{2,1,0:T(8,128)(2,1)S(1)} %copy-done.5, f32[1024]{0:T(1024)S(1)} %bitcast.118), kind=kOutput, calls=%fused_computation.11 | convolution fusion | flops 1085665280 | bytes 11816960 | tf_op jit(solution)/shard_map/td,fd->tf/dot_general | solution.py:1011
  96.7 0.0 copy-start.3
  96.7 0.0 slice-done.2
  96.7 0.0 slice-done.3
  96.7 3.0 %multiply_reduce_fusion = (f32[1024]{0:T(1024)S(1)}, f32[128]{0:T(128)S(1)}, f32[1024]{0:T(1024)S(1)}, f32[128,1024]{1,0:T(8,128)S(1)}) fusion(f32[128,1024]{1,0:T(8,128)S(1)} %get-tuple-element.55, f32[128]{0:T(128)S(1)} %fusion.29, f32[128]{0:T(128)S(1)} %broadcast_multiply_fusion, f32[1024]{0:T(1024)S(1)} %bitcast.110, ...), kind=kOutput, calls=%fused_computation.24 | convolution fusion | flops 1074788224 | bytes 10499584 | tf_op jit(solution)/shard_map/tf,df->td/dot_general | solution.py:1015
  99.8 0.0 copy-done.3
  99.8 0.0 copy-done.1
  99.8 2.2 %fusion.11 = (f32[1024]{0:T(1024)S(1)}, bf16[1,128,1024]{2,1,0:T(8,128)(2,1)}, f32[128]{0:T(128)S(1)}, f32[128,1024]{1,0:T(8,128)S(1)}, bf16[128,1024]{1,0:T(8,128)(2,1)}) fusion(bf16[1,128,1024]{2,1,0:T(8,128)(2,1)S(1)} %copy-done.5, f32[128,1024]{1,0:T(8,128)S(1)} %get-tuple-element.55, f32[1024]{0:T(1024)S(1)} %bitcast.119, ...), kind=kOutput, calls=%fused_computation.22 | convolution fusion | flops 1075706752 | bytes 11810816 | tf_op jit(solution)/shard_map/dot_general | solution.py:1005
  102.0 0.2 multiply_reduce_fusion.1
  102.2 0.0 copy-start.2
  102.2 0.0 copy-start.15
  102.3 1.5 copy-done
  103.8 1.6 convolution_convert_fusion.refs_9_
  105.3 0.0 copy-done.2
  105.3 0.0 copy-done.15
  105.3 0.0 copy-done.4
  105.3 80.5 %leave.1 = (f32[16,3072]{1,0:T(8,128)}, f32[16,1024]{1,0:T(8,128)}, f32[16,4096]{1,0:T(8,128)}, f32[64,1024]{1,0:T(8,128)}, bf16[2,2,4,4,80,128]{5,4,3,2,1,0:T(8,128)(2,1)}, /*index=5*/f32[128,1024]{1,0:T(8,128)}) custom-call(bf16[128,1024]{1,0:T(8,128)(2,1)} %get-tuple-element.35.refs_0_, bf16[128,1024]{1,0:T(8,128)(2,1)} %get-tuple-element.30.refs_1_, ...), custom_call_target="tpu_custom_call" | custom-call | tf_op jit(solution)/shard_map/leave/pallas_call | solution.py:911
  185.8 0.0 copy-start.16
  185.8 0.0 copy-start.10
  185.8 1.7 copy.31
  187.5 0.0 copy-done.16
  187.6 1.0 convolution_bitcast_fusion
  188.6 0.1 slice.36
  188.6 0.0 copy-start.14
  188.7 0.0 copy-start.9
  188.7 0.0 copy-start.8
  188.7 0.6 convert_reduce_fusion.2
  189.3 0.4 fusion.27
  189.7 0.8 fusion.22
  190.5 0.1 convert_reduce_fusion.3
  190.6 0.9 fusion.20
  191.5 0.6 convert_reduce_fusion.1
  192.1 0.8 copy.45
  192.9 0.7 copy.46
  193.6 0.6 copy.47
  194.2 0.0 copy-done.9
  194.2 0.7 copy.48
  195.0 0.7 copy.49
  (35 shorter events, 0.2 us)
Async XLA Ops:
  4.5 0.6 copy-start.12
  84.2 2.6 %copy-start.18 = (f32[32,128]{1,0:T(8,128)S(1)}, f32[32,128]{1,0:T(8,128)}, u32[]{:S(2)}) copy-start(f32[32,128]{1,0:T(8,128)} %get-tuple-element.33) | copy-start | bytes 49156
  86.6 5.7 %slice-start = ((s8[8388608]{0:T(1024)(128)(4,1)}), s8[4194304]{0:T(1024)(128)(4,1)S(1)}, s32[]{:S(2)}) async-start(s8[8388608]{0:T(1024)(128)(4,1)} %bitcast.83), calls=%async_computation | async-start | bytes 8388608
  86.8 5.5 %copy-start.6 = (bf16[128,1024]{1,0:T(8,128)(2,1)}, bf16[128,1024]{1,0:T(8,128)(2,1)S(1)}, u32[]{:S(2)}) copy-start(bf16[128,1024]{1,0:T(8,128)(2,1)S(1)} %add_convert_fusion.1.refs_2_) | copy-start | bytes 786436
  86.8 5.8 %slice-start.1 = ((s8[8388608]{0:T(1024)(128)(4,1)}), s8[4194304]{0:T(1024)(128)(4,1)S(1)}, s32[]{:S(2)}) async-start(s8[8388608]{0:T(1024)(128)(4,1)} %bitcast.83), calls=%async_computation.1 | async-start | bytes 8388608
  86.8 5.8 %copy-start.5 = (bf16[1,128,1024]{2,1,0:T(8,128)(2,1)S(1)}, bf16[1,128,1024]{2,1,0:T(8,128)(2,1)}, u32[]{:S(2)}) copy-start(bf16[1,128,1024]{2,1,0:T(8,128)(2,1)} %param.16) | copy-start | bytes 786436
  86.8 9.9 %slice-start.2 = ((s8[8388608]{0:T(1024)(128)(4,1)}), s8[4194304]{0:T(1024)(128)(4,1)S(1)}, s32[]{:S(2)}) async-start(s8[8388608]{0:T(1024)(128)(4,1)} %bitcast.90), calls=%async_computation.2 | async-start | bytes 8388608
  92.4 7.4 %copy-start.1 = (bf16[128,4096]{1,0:T(8,128)(2,1)}, bf16[128,4096]{1,0:T(8,128)(2,1)S(1)}, u32[]{:S(2)}) copy-start(bf16[128,4096]{1,0:T(8,128)(2,1)S(1)} %get-tuple-element.69.refs_3_) | copy-start | bytes 3145732
  92.6 4.1 %slice-start.3 = ((s8[8388608]{0:T(1024)(128)(4,1)}), s8[4194304]{0:T(1024)(128)(4,1)S(1)}, s32[]{:S(2)}) async-start(s8[8388608]{0:T(1024)(128)(4,1)} %bitcast.90), calls=%async_computation.3 | async-start | bytes 8388608
  96.7 3.1 %copy-start.3 = (bf16[128,4096]{1,0:T(8,128)(2,1)}, bf16[128,4096]{1,0:T(8,128)(2,1)S(1)}, u32[]{:S(2)}) copy-start(bf16[128,4096]{1,0:T(8,128)(2,1)S(1)} %get-tuple-element.73.refs_5_) | copy-start | bytes 3145732
  102.0 1.8 copy-start
  102.2 3.2 %copy-start.2 = (f32[128,1024]{1,0:T(8,128)}, f32[128,1024]{1,0:T(8,128)S(1)}, u32[]{:S(2)}) copy-start(f32[128,1024]{1,0:T(8,128)S(1)} %get-tuple-element.51.refs_11_) | copy-start | bytes 1572868
  102.2 3.1 %copy-start.15 = (f32[10240]{0:T(1024)}, f32[10240]{0:T(1024)S(1)}, u32[]{:S(2)}) copy-start(f32[10240]{0:T(1024)S(1)} %constant_dynamic-update-slice_fusion) | copy-start | bytes 122884
  103.8 1.6 copy-start.4
  185.8 1.7 copy-start.16
  185.8 3.5 %copy-start.10 = (bf16[1,16,6144]{2,1,0:T(8,128)(2,1)S(1)}, bf16[1,16,6144]{2,1,0:T(8,128)(2,1)}, u32[]{:S(2)}) copy-start(bf16[1,16,6144]{2,1,0:T(8,128)(2,1)} %param.19) | copy-start | bytes 589828
  187.5 2.1 %copy-start.13 = (f32[2,64,128]{2,1,0:T(8,128)S(1)}, f32[2,64,128]{2,1,0:T(8,128)}, u32[]{:S(2)}) copy-start(f32[2,64,128]{2,1,0:T(8,128)} %get-tuple-element.42) | copy-start | bytes 196612
  187.5 3.0 %copy-start.17 = (f32[64,128]{1,0:T(8,128)S(1)}, f32[64,128]{1,0:T(8,128)}, u32[]{:S(2)}) copy-start(f32[64,128]{1,0:T(8,128)} %get-tuple-element.39) | copy-start | bytes 98308
  188.6 3.6 %copy-start.7 = (f32[128,1024]{1,0:T(8,128)S(1)}, f32[128,1024]{1,0:T(8,128)}, u32[]{:S(2)}) copy-start(f32[128,1024]{1,0:T(8,128)} %get-tuple-element.38) | copy-start | bytes 1572868
  188.6 4.3 %copy-start.11 = (f32[16,3072]{1,0:T(8,128)S(1)}, f32[16,3072]{1,0:T(8,128)}, u32[]{:S(2)}) copy-start(f32[16,3072]{1,0:T(8,128)} %get-tuple-element.43) | copy-start | bytes 589828
  188.6 5.0 %copy-start.14 = (f32[16,1024]{1,0:T(8,128)S(1)}, f32[16,1024]{1,0:T(8,128)}, u32[]{:S(2)}) copy-start(f32[16,1024]{1,0:T(8,128)} %get-tuple-element.44) | copy-start | bytes 196612
  188.7 5.6 %copy-start.9 = (f32[16,4096]{1,0:T(8,128)S(1)}, f32[16,4096]{1,0:T(8,128)}, u32[]{:S(2)}) copy-start(f32[16,4096]{1,0:T(8,128)} %get-tuple-element.45) | copy-start | bytes 786436
  188.7 6.3 %copy-start.8 = (f32[64,1024]{1,0:T(8,128)S(1)}, f32[64,1024]{1,0:T(8,128)}, u32[]{:S(2)}) copy-start(f32[64,1024]{1,0:T(8,128)} %get-tuple-element.46) | copy-start | bytes 786436

commit v5 on v4

--- a/solution.py
+++ b/solution.py
@@ -680,7 +680,7 @@
         self.kept.wait()
         for slot in range(4):
             start = self.column + slot * QUARTER
-            self.out[self.row : self.row + 16, start : start + QUARTER] = self.final[slot].astype(F32)
+            self.out[self.row : self.row + 16, start : start + QUARTER] = self.final[slot]
 
 
 LEFTS = (D, D, D, FF)
@@ -910,7 +910,7 @@
     scratch += copy_scratch(12 * 15 + 4 + 9 + 10, 4 + 9 + 1 + 12)
     return pl.pallas_call(
         leave_kernel,
-        out_shape=[jax.ShapeDtypeStruct((rows, columns), F32) for rows, columns in WEIGHTS]
+        out_shape=[jax.ShapeDtypeStruct((rows, columns), BF16) for rows, columns in WEIGHTS]
         + [jax.ShapeDtypeStruct((2, 2, 4, 4) + sums.shape, BF16), jax.ShapeDtypeStruct((HALF, D), F32)],
         in_specs=[outside] * 8 + [inside] * 6,
         out_specs=[inside] * 6,
@@ -1059,11 +1059,11 @@
         time_grad,
         modulate_grad[None],
         offset_grad[None],
-        attend_grad[None],
-        output_grad[None],
-        expand_grad[None],
+        attend_grad.astype(F32)[None],
+        output_grad.astype(F32)[None],
+        expand_grad.astype(F32)[None],
         hidden_grad[None],
-        contract_grad[None],
+        contract_grad.astype(F32)[None],
     )
 
 

time: 196 us -> 196 us (level)
  other arithmetic: 5.6 us -> 8.37 us
  local copies, waits for them, and re-layouts: 8.21 us -> 5.5 us
    broadcast_in_dim x0 -> x4, other arithmetic: none -> 2.77 us  [the longest x1 0.72 us: per_device(): expand_grad.astype(F32)[None]]
    unnamed x57 -> x53, local copies, waits for them, and re-layouts: 7.63 us -> 4.91 us
where the time goes in v5:
time: 196 us
  Pallas kernels  158 us (81%)
  matrix products  21.7 us (11%)
  other arithmetic  8.37 us (4%)
  local copies, waits for them, and re-layouts  5.5 us (3%)
  between operations  2.32 us (1%)
    pallas_call x1, Pallas kernels, leave(): pl.pallas_call(leave_kernel, out_shape=[jax.ShapeDtypeStruct((rows, colum...  80.3 us
    pallas_call x1, Pallas kernels, enter(): pl.pallas_call(enter_kernel, out_shape=shapes, in_specs=[outside] * 8 + [...  77.4 us
    dot_general x1, matrix products, per_device(): jnp.dot(second_in, w_expand, preferred_element_type=F32) + b_hidden  5.48 us
    unnamed x53, local copies, waits for them, and re-layouts  4.91 us
    dot_general x1, matrix products, per_device(): jnp.einsum('td,fd->tf', grad_two, w_contract, preferred_element_type=F32)  4.07 us

profile of v5, /device:TPU:1, one launch (start us, length us, event | category | flops | bytes accessed | tf_op | source)
XLA Modules:
  0.0 195.6 jit_solution(9264154870284554420)
XLA Ops:
  0.6 0.7 bitcast_convert_fusion.4
  1.3 0.1 tile.16
  2.1 0.1 sine_convert_fusion
  2.8 0.1 pad.3.clone
  2.9 0.1 pad.5.clone
  2.9 0.7 maximum_maximum_fusion.own_ids
  3.6 0.7 convert_element_type.90
  4.3 0.3 dynamic_update_slice.3.placed
  4.5 0.6 copy-done.12
  5.2 77.4 %enter.1 = (bf16[2,4,4,2,16,3072]{5,4,3,2,1,0:T(8,128)(2,1)}, bf16[2,4,4,2,16,1024]{5,4,3,2,1,0:T(8,128)(2,1)}, bf16[2,4,4,2,16,4096]{5,4,3,2,1,0:T(8,128)(2,1)}...) custom-call(bf16[16,3072]{1,0:T(8,128)(2,1)} %bitcast.113, ...), custom_call_target="tpu_custom_call" | custom-call | tf_op jit(solution)/shard_map/enter/pallas_call | solution.py:480
  82.6 1.6 fusion.41
  84.2 2.2 %fusion.40 = (f32[128]{0:T(128)S(1)}, f32[128,1024]{1,0:T(8,128)S(1)}, f32[128,1024]{1,0:T(8,128)S(1)}) fusion(f32[1024]{0:T(1024)S(1)} %bitcast.118, bf16[1,128,1024]{2,1,0:T(8,128)(2,1)} %param.13, bf16[128,1024]{1,0:T(8,128)(2,1)} %get-tuple-element.30.refs_1_, bf16[1024,1024]{1,0:T(8,128)(2,1)} %bitcast.95), kind=kOutput, calls=%fused_computation.84 | convolution fusion | flops 268959616 | bytes 3674624 | tf_op jit(solution)/shard_map/dot_general | solution.py:1000
  86.4 0.2 multiply_reduce_fusion.3
  86.6 0.0 slice-start
  86.6 0.2 add_convert_fusion.1.refs_2_
  86.8 0.0 copy-start.6
  86.8 0.0 copy-done.18
  86.8 0.0 slice-start.1
  86.8 0.0 copy-start.5
  86.8 0.0 slice-start.2
  86.9 5.5 %multiply_convert_fusion = (bf16[128,4096]{1,0:T(8,128)(2,1)S(1)}, f32[128,4096]{1,0:T(8,128)S(1)}) fusion(f32[4096]{0:T(1024)S(1)} %bitcast.129, bf16[128,1024]{1,0:T(8,128)(2,1)S(1)} %add_convert_fusion.1.refs_2_, bf16[1024,4096]{1,0:T(8,128)(2,1)} %bitcast.97), kind=kOutput, calls=%fused_computation.12 | convolution fusion | flops 1078984704 | bytes 11812864 | tf_op jit(solution)/shard_map/dot_general | solution.py:1003
  92.3 0.0 copy-done.6
  92.4 0.0 copy-start.1
  92.4 0.0 slice-done
  92.4 0.2 slice-done.1
  92.6 0.0 copy-done.5
  92.6 4.1 %convert_reduce_fusion = (f32[4096]{0:T(1024)S(1)}, bf16[128,4096]{1,0:T(8,128)(2,1)S(1)}) fusion(f32[128,4096]{1,0:T(8,128)S(1)} %get-tuple-element.70, bf16[4096,1024]{1,0:T(8,128)(2,1)S(1)} %bitcast.93, bf16[1,128,1024]{2,1,0:T(8,128)(2,1)S(1)} %copy-done.5, f32[1024]{0:T(1024)S(1)} %bitcast.122), kind=kOutput, calls=%fused_computation.11 | convolution fusion | flops 1085665280 | bytes 11816960 | tf_op jit(solution)/shard_map/td,fd->tf/dot_general | solution.py:1011
  96.7 0.0 copy-start.3
  96.7 0.0 slice-done.2
  96.7 0.0 slice-done.3
  96.7 3.0 %multiply_reduce_fusion = (f32[1024]{0:T(1024)S(1)}, f32[128]{0:T(128)S(1)}, f32[1024]{0:T(1024)S(1)}, f32[128,1024]{1,0:T(8,128)S(1)}) fusion(f32[128,1024]{1,0:T(8,128)S(1)} %get-tuple-element.55, f32[128]{0:T(128)S(1)} %fusion.29, f32[128]{0:T(128)S(1)} %broadcast_multiply_fusion, f32[1024]{0:T(1024)S(1)} %bitcast.115, ...), kind=kOutput, calls=%fused_computation.24 | convolution fusion | flops 1074788224 | bytes 10499584 | tf_op jit(solution)/shard_map/tf,df->td/dot_general | solution.py:1015
  99.8 0.0 copy-done.3
  99.8 0.0 copy-done.1
  99.8 2.2 %fusion.11 = (f32[1024]{0:T(1024)S(1)}, bf16[1,128,1024]{2,1,0:T(8,128)(2,1)}, f32[128]{0:T(128)S(1)}, f32[128,1024]{1,0:T(8,128)S(1)}, bf16[128,1024]{1,0:T(8,128)(2,1)}) fusion(bf16[1,128,1024]{2,1,0:T(8,128)(2,1)S(1)} %copy-done.5, f32[128,1024]{1,0:T(8,128)S(1)} %get-tuple-element.55, f32[1024]{0:T(1024)S(1)} %bitcast.123, ...), kind=kOutput, calls=%fused_computation.22 | convolution fusion | flops 1075706752 | bytes 11810816 | tf_op jit(solution)/shard_map/dot_general | solution.py:1005
  102.0 0.2 multiply_reduce_fusion.1
  102.2 0.0 copy-start.2
  102.2 0.0 copy-start.14
  102.3 1.5 copy-done
  103.8 1.6 convolution_convert_fusion.refs_9_
  105.4 0.0 copy-done.2
  105.4 0.0 copy-done.14
  105.4 0.0 copy-done.4
  105.4 80.3 %leave.1 = (bf16[16,3072]{1,0:T(8,128)(2,1)}, bf16[16,1024]{1,0:T(8,128)(2,1)}, bf16[16,4096]{1,0:T(8,128)(2,1)}, bf16[64,1024]{1,0:T(8,128)(2,1)}, bf16[2,2,4,4...) custom-call(bf16[128,1024]{1,0:T(8,128)(2,1)} %get-tuple-element.35.refs_0_, ...), custom_call_target="tpu_custom_call" | custom-call | tf_op jit(solution)/shard_map/leave/pallas_call | solution.py:911
  185.7 0.0 copy-start.15
  185.7 0.0 copy-start.8
  185.7 1.7 copy.31
  187.4 0.0 copy-done.15
  187.4 0.0 copy-start.13
  187.4 0.0 copy-start.17
  187.5 1.0 convolution_bitcast_fusion
  188.5 0.0 copy-start.7
  188.5 0.1 slice.36
  188.6 0.6 convert_reduce_fusion.2
  189.2 0.0 copy-done.8
  189.2 0.4 fusion.27
  189.6 0.8 fusion.22
  190.4 0.1 convert_reduce_fusion.3
  190.5 0.9 fusion.20
  191.4 0.6 convert_reduce_fusion.1
  192.0 0.7 bitcast_convert_fusion
  192.8 0.7 bitcast_convert_fusion.1
  193.5 0.7 bitcast_convert_fusion.2
  194.2 0.6 bitcast_convert_fusion.3
  194.8 0.8 copy.41
  (35 shorter events, 0.2 us)
Async XLA Ops:
  4.5 0.6 copy-start.12
  84.2 2.6 %copy-start.18 = (f32[32,128]{1,0:T(8,128)S(1)}, f32[32,128]{1,0:T(8,128)}, u32[]{:S(2)}) copy-start(f32[32,128]{1,0:T(8,128)} %get-tuple-element.33) | copy-start | bytes 49156
  86.6 5.7 %slice-start = ((s8[8388608]{0:T(1024)(128)(4,1)}), s8[4194304]{0:T(1024)(128)(4,1)S(1)}, s32[]{:S(2)}) async-start(s8[8388608]{0:T(1024)(128)(4,1)} %bitcast.91), calls=%async_computation | async-start | bytes 8388608
  86.8 5.5 %copy-start.6 = (bf16[128,1024]{1,0:T(8,128)(2,1)}, bf16[128,1024]{1,0:T(8,128)(2,1)S(1)}, u32[]{:S(2)}) copy-start(bf16[128,1024]{1,0:T(8,128)(2,1)S(1)} %add_convert_fusion.1.refs_2_) | copy-start | bytes 786436
  86.8 5.8 %slice-start.1 = ((s8[8388608]{0:T(1024)(128)(4,1)}), s8[4194304]{0:T(1024)(128)(4,1)S(1)}, s32[]{:S(2)}) async-start(s8[8388608]{0:T(1024)(128)(4,1)} %bitcast.91), calls=%async_computation.1 | async-start | bytes 8388608
  86.8 5.8 %copy-start.5 = (bf16[1,128,1024]{2,1,0:T(8,128)(2,1)S(1)}, bf16[1,128,1024]{2,1,0:T(8,128)(2,1)}, u32[]{:S(2)}) copy-start(bf16[1,128,1024]{2,1,0:T(8,128)(2,1)} %param.16) | copy-start | bytes 786436
  86.8 9.9 %slice-start.2 = ((s8[8388608]{0:T(1024)(128)(4,1)}), s8[4194304]{0:T(1024)(128)(4,1)S(1)}, s32[]{:S(2)}) async-start(s8[8388608]{0:T(1024)(128)(4,1)} %bitcast.98), calls=%async_computation.2 | async-start | bytes 8388608
  92.4 7.4 %copy-start.1 = (bf16[128,4096]{1,0:T(8,128)(2,1)}, bf16[128,4096]{1,0:T(8,128)(2,1)S(1)}, u32[]{:S(2)}) copy-start(bf16[128,4096]{1,0:T(8,128)(2,1)S(1)} %get-tuple-element.69.refs_3_) | copy-start | bytes 3145732
  92.6 4.1 %slice-start.3 = ((s8[8388608]{0:T(1024)(128)(4,1)}), s8[4194304]{0:T(1024)(128)(4,1)S(1)}, s32[]{:S(2)}) async-start(s8[8388608]{0:T(1024)(128)(4,1)} %bitcast.98), calls=%async_computation.3 | async-start | bytes 8388608
  96.7 3.1 %copy-start.3 = (bf16[128,4096]{1,0:T(8,128)(2,1)}, bf16[128,4096]{1,0:T(8,128)(2,1)S(1)}, u32[]{:S(2)}) copy-start(bf16[128,4096]{1,0:T(8,128)(2,1)S(1)} %get-tuple-element.73.refs_5_) | copy-start | bytes 3145732
  102.0 1.8 copy-start
  102.2 3.2 %copy-start.2 = (f32[128,1024]{1,0:T(8,128)}, f32[128,1024]{1,0:T(8,128)S(1)}, u32[]{:S(2)}) copy-start(f32[128,1024]{1,0:T(8,128)S(1)} %get-tuple-element.51.refs_11_) | copy-start | bytes 1572868
  102.2 3.1 %copy-start.14 = (f32[10240]{0:T(1024)}, f32[10240]{0:T(1024)S(1)}, u32[]{:S(2)}) copy-start(f32[10240]{0:T(1024)S(1)} %constant_dynamic-update-slice_fusion) | copy-start | bytes 122884
  103.8 1.6 copy-start.4
  185.7 1.7 copy-start.15
  185.7 3.5 %copy-start.8 = (bf16[1,16,6144]{2,1,0:T(8,128)(2,1)S(1)}, bf16[1,16,6144]{2,1,0:T(8,128)(2,1)}, u32[]{:S(2)}) copy-start(bf16[1,16,6144]{2,1,0:T(8,128)(2,1)} %param.19) | copy-start | bytes 589828
  187.4 2.1 %copy-start.13 = (f32[2,64,128]{2,1,0:T(8,128)S(1)}, f32[2,64,128]{2,1,0:T(8,128)}, u32[]{:S(2)}) copy-start(f32[2,64,128]{2,1,0:T(8,128)} %get-tuple-element.42) | copy-start | bytes 196612
  187.4 3.0 %copy-start.17 = (f32[64,128]{1,0:T(8,128)S(1)}, f32[64,128]{1,0:T(8,128)}, u32[]{:S(2)}) copy-start(f32[64,128]{1,0:T(8,128)} %get-tuple-element.39) | copy-start | bytes 98308
  188.5 3.5 %copy-start.10 = (bf16[64,1024]{1,0:T(8,128)(2,1)S(1)}, bf16[64,1024]{1,0:T(8,128)(2,1)}, u32[]{:S(2)}) copy-start(bf16[64,1024]{1,0:T(8,128)(2,1)} %get-tuple-element.46) | copy-start | bytes 393220
  188.5 4.3 %copy-start.9 = (bf16[16,4096]{1,0:T(8,128)(2,1)S(1)}, bf16[16,4096]{1,0:T(8,128)(2,1)}, u32[]{:S(2)}) copy-start(bf16[16,4096]{1,0:T(8,128)(2,1)} %get-tuple-element.45) | copy-start | bytes 393220
  188.5 5.0 %copy-start.11 = (bf16[16,3072]{1,0:T(8,128)(2,1)S(1)}, bf16[16,3072]{1,0:T(8,128)(2,1)}, u32[]{:S(2)}) copy-start(bf16[16,3072]{1,0:T(8,128)(2,1)} %get-tuple-element.43) | copy-start | bytes 294916
  188.5 5.7 %copy-start.16 = (bf16[16,1024]{1,0:T(8,128)(2,1)S(1)}, bf16[16,1024]{1,0:T(8,128)(2,1)}, u32[]{:S(2)}) copy-start(bf16[16,1024]{1,0:T(8,128)(2,1)} %get-tuple-element.44) | copy-start | bytes 98308
  188.5 6.3 %copy-start.7 = (f32[128,1024]{1,0:T(8,128)S(1)}, f32[128,1024]{1,0:T(8,128)}, u32[]{:S(2)}) copy-start(f32[128,1024]{1,0:T(8,128)} %get-tuple-element.38) | copy-start | bytes 1572868
